TPU v7x, 32 devices: a whole 2x2x4 slice. The times are simulated.
32 devices in a mesh: ckpt: 4 (over z), tok: 4 (over x, core), vocab: 2 (over y).
Axes of the slice: x: 2, y: 2, z: 4, core: 2. Of those that a mesh axis runs over, the one named last changes fastest.
Arguments:
- heads: bfloat16 [4, 2560, 10240], P('ckpt', 'tok', 'vocab'), may hold values from -5 to 5
- hidden: bfloat16 [4, 512, 2560], P('ckpt', 'tok'), may hold values from -4 to 4
- targets: int32 [512], P('tok'), may hold values from 0 to 10239
Outputs:
- merged: bfloat16 [2560, 10240], P(('ckpt', 'tok'), 'vocab')
All inputs are finite; a program needn't handle non-finite values.
Results may differ from a plain program's by a relative error of at most 0.0044.
Values may be sent and summed in bfloat16 or wider, within the bound.
No kernel may reach another device: no remote copies, remote signals or barrier semaphores. Data moves between devices by JAX's collectives and lax.ppermute only.
A program may use at most 128 MiB of HBM per device.

v0:
```python
import jax
import jax.numpy as jnp
from jax import lax
from jax.sharding import PartitionSpec as P

D = 2560


prior_weight = 0.05


def shards(heads, hidden, targets):
    columns = lax.all_to_all(heads[0], "tok", split_axis=1, concat_axis=0, tiled=True)
    states, labels = (
        lax.all_gather(hidden[0], "tok", axis=0, tiled=True),
        lax.all_gather(targets, "tok", axis=0, tiled=True),
    )
    width = columns.shape[1]
    ntok = lax.axis_size("tok")
    nvocab = lax.axis_size("vocab")
    offset = (lax.axis_index("vocab") * ntok + lax.axis_index("tok")) * width
    logits = jnp.dot(states, columns, preferred_element_type=jnp.float32)
    peak = lax.pmax(jnp.max(logits, axis=1), ("tok", "vocab"))
    shifted = jnp.exp(logits - peak[:, None])
    total = lax.psum(jnp.sum(shifted, axis=1), ("tok", "vocab"))
    column_ids = offset + jnp.arange(width, dtype=jnp.int32)
    onehot = (labels[:, None] == column_ids[None, :]).astype(jnp.float32)
    resid_sq = jnp.square(shifted / total[:, None] - onehot).astype(jnp.bfloat16)
    hidden_sq = jnp.square(states.astype(jnp.float32)).astype(jnp.bfloat16)
    tokens = states.shape[0]
    partial_value = jnp.sum(
        jnp.sum(hidden_sq.astype(jnp.float32), axis=1)
        * jnp.sum(resid_sq.astype(jnp.float32), axis=1)
    )
    vocab_total = width * ntok * nvocab
    count = float(tokens * D * vocab_total)
    level = lax.psum(partial_value, ("tok", "vocab")) / jnp.float32(count)
    fisher = lax.dot_general(
        hidden_sq, resid_sq, (((0,), (0,)), ((), ())), preferred_element_type=jnp.float32
    ) / jnp.float32(tokens)
    weight = (jnp.float32(vocab_total) * fisher / level + prior_weight).astype(jnp.bfloat16)
    weight_wide = weight.astype(jnp.float32)
    numer = weight_wide * columns.astype(jnp.float32)
    numer_sum, weight_sum = (
        lax.psum_scatter(numer, "ckpt", scatter_dimension=0, tiled=True),
        lax.psum_scatter(weight_wide, "ckpt", scatter_dimension=0, tiled=True),
    )
    blended = (numer_sum / weight_sum).astype(jnp.bfloat16)
    return lax.all_to_all(blended, "tok", split_axis=0, concat_axis=1, tiled=True)


def solution(mesh):
    placed = (P("ckpt", "tok", "vocab"), P("ckpt", "tok", None), P("tok"))
    return jax.shard_map(
        shards, mesh=mesh, in_specs=placed, out_specs=P(("ckpt", "tok"), "vocab"), check_vma=False
    )
```

profile of v0, /device:TPU:9, one launch (start us, length us, event | category | flops | bytes accessed | tf_op | source)
XLA Modules:
  0.0 668.7 jit_solution(18382875787577479818)
XLA Ops:
  6.5 12.5 %all_to_all.28 = bf16[640,4,1280]{2,1,0:T(4,128)(2,1)} reshape(bf16[1,640,5120]{2,1,0:T(8,128)(2,1)} %param.3) | data formatting | bytes 13107200 | tf_op jit(solution)/shard_map/all_to_all | solution.py:13
  19.0 6.4 copy.6
  25.5 0.0 copy-start
  25.5 6.1 all-to-all-start
  31.5 0.0 all-gather.4.cloned.1.call-start
  31.5 0.7 all-gather.4.cloned.1.call-update
  32.2 0.0 reduce-scatter.3.cloned.1.call-start
  32.3 0.0 copy-done
  32.3 87.4 %all-gather.1 = s32[4,1,128]{2,1,0:T(1,128)S(1)} all-gather(s32[1,1,128]{2,1,0:T(1,128)S(1)} %bitcast.26), channel_id=1, replica_groups=mesh['ckpt'=4,'tok'=4,'vocab'=2] {'tok'}, dimensions={0}, use_global_device_ids=true | all-gather | bytes 2560 | tf_op jit(solution)/shard_map/all_gather | solution.py:16
  119.7 0.0 all-gather.4.cloned.1.call-done
  119.8 2.3 convert_reduce_fusion
  122.1 0.0 all-to-all-done
  122.1 7.3 %fusion.4 = (f32[512]{0:T(512)S(1)}, f32[512,1280]{1,0:T(8,128)S(1)}) fusion(bf16[2560,1280]{1,0:T(8,128)(2,1)} %bitcast.2, bf16[1,512,2560]{2,1,0:T(8,128)(2,1)} %all-gather.4.cloned.1.call-done), kind=kOutput, calls=%fused_computation.15 | convolution fusion | flops 3356098048 | bytes 11798528 | tf_op jit(solution)/shard_map/dot_general | solution.py:22
  129.4 13.2 %pmax.7 = f32[512]{0:T(512)S(1)} all-reduce(f32[512]{0:T(512)S(1)} %get-tuple-element.7), channel_id=1, replica_groups=mesh['ckpt'=4,'tok'=4,'vocab'=2] {'tok','vocab'}, use_global_device_ids=true, to_apply=%region_1.0 | all-reduce | flops 512 | bytes 4096 | tf_op jit(solution)/shard_map/pmax | solution.py:23
  142.6 0.5 fusion.3
  143.1 12.7 %psum.14 = f32[512]{0:T(512)S(1)} all-reduce(f32[512]{0:T(512)S(1)} %fusion.3), channel_id=1, replica_groups=mesh['ckpt'=4,'tok'=4,'vocab'=2] {'tok','vocab'}, use_global_device_ids=true, to_apply=%region_3.0 | all-reduce | flops 512 | bytes 4096 | tf_op jit(solution)/shard_map/psum | solution.py:25
  155.8 2.0 convert_reduce_fusion.1
  157.7 0.7 multiply_reduce_fusion
  158.4 14.1 %psum.15 = f32[]{:T(128)} all-reduce(f32[]{:T(128)} %multiply_reduce_fusion), channel_id=1, replica_groups=mesh['ckpt'=4,'tok'=4,'vocab'=2] {'tok','vocab'}, use_global_device_ids=true, to_apply=%region_7.0 | all-reduce | flops 1 | bytes 8 | tf_op jit(solution)/shard_map/psum | solution.py:37
  173.2 17.0 %convert_multiply_fusion = (f32[2560,1280]{1,0:T(8,128)}, f32[2560,1280]{1,0:T(8,128)}) fusion(bf16[640,4,1280]{2,0,1:T(8,128)(2,1)} %all-to-all-done, f32[]{:T(128)S(6)} %div.24, bf16[512,1280]{1,0:T(8,128)(2,1)} %get-tuple-element.6, bf16[1,512,2560]{2,1,0:T(8,128)(2,1)} %all-gather.4.cloned.1.call-done), kind=kOutput, calls=%fused_computation.1 | convolution fusion | flops 3382312960 | bytes 36700164 | tf_op jit(solution)/shard_map/dot_general | solution.py:38
  190.2 0.0 reduce-scatter.3.cloned.1.call-update
  190.2 0.0 reduce-scatter.5.cloned.1.call-start
  190.3 0.7 reduce-scatter.5.cloned.1.call-update
  191.0 219.6 %reduce-scatter.3.cloned.1.call-done = f32[640,1280]{1,0:T(8,128)} async-done(((f32[2560,1280]{1,0:T(8,128)}), f32[640,1280]{1,0:T(8,128)}) %reduce-scatter.3.cloned.1.call-update) | async-done | bytes 3276816 | tf_op jit(solution)/shard_map/reduce_scatter | solution.py:45
  410.5 223.8 %reduce-scatter.5.cloned.1.call-done = f32[640,1280]{1,0:T(8,128)} async-done(((f32[2560,1280]{1,0:T(8,128)}), f32[640,1280]{1,0:T(8,128)}) %reduce-scatter.5.cloned.1.call-update) | async-done | bytes 3276816 | tf_op jit(solution)/shard_map/reduce_scatter | solution.py:46
  634.3 3.4 divide_convert_fusion
  637.7 23.2 %all_to_all.38 = bf16[4,160,1280]{2,1,0:T(8,128)(2,1)S(1)} all-to-all(bf16[4,160,1280]{2,1,0:T(8,128)(2,1)S(1)} %bitcast.24), channel_id=1, replica_groups=mesh['ckpt'=4,'tok'=4,'vocab'=2] {'tok'}, dimensions={0} | all-to-all | bytes 3276800 | tf_op jit(solution)/shard_map/all_to_all | solution.py:49
  660.9 1.4 copy.8
  (1 shorter events, 0.0 us)
Async XLA Ops:
  25.5 6.8 %copy-start = (s32[128]{0:T(128)S(1)}, s32[128]{0:T(128)}, u32[]{:S(2)}) copy-start(s32[128]{0:T(128)} %param.5) | copy-start | bytes 1540
  25.5 96.6 %all-to-all-start = ((bf16[640,4,1280]{2,0,1:T(8,128)(2,1)}), bf16[640,4,1280]{2,0,1:T(8,128)(2,1)}, u32[]{:S(2)}, u32[]{:S(2)}) async-start(bf16[640,4,1280]{2,0,1:T(8,128)(2,1)} %copy.6), calls=%async_computation | async-start | bytes 13107200 | tf_op jit(solution)/shard_map/all_to_all | solution.py:13
  31.5 88.2 %all-gather.4.cloned.1.call-start = ((), (), s32[]{:S(2)}) async-start(), calls=%async_computation.6 | async-start | bytes 3276800 | tf_op jit(solution)/shard_map/all_gather | solution.py:15
  32.2 378.3 %reduce-scatter.3.cloned.1.call-start = ((), (), s32[]{:S(2)}) async-start(), calls=%async_computation.4 | async-start | bytes 16384000 | tf_op jit(solution)/shard_map/reduce_scatter | solution.py:45
  190.2 444.1 %reduce-scatter.5.cloned.1.call-start = ((), (), s32[]{:S(2)}) async-start(), calls=%async_computation.5 | async-start | bytes 16384000 | tf_op jit(solution)/shard_map/reduce_scatter | solution.py:46
Sparse Core Ops, SparseCore 0:
  33.9 41.1 all-gather.3
  190.3 220.1 reduce-scatter.2
  412.9 221.3 reduce-scatter.4
where the time goes:
time: 671 us; the launch traced here: 669 us
  waiting for transfers between devices  445 us (66%)
  blocking collectives  151 us (23%)
  matrix products  24.3 us (4%)
  local copies, waits for them, and re-layouts  20.3 us (3%)
  between operations  13.8 us (2%)
  other arithmetic  8.86 us (1%)
    reduce_scatter x1, waiting for transfers between devices, shards(): lax.psum_scatter(weight_wide, 'ckpt', scatter_dimension=0, tiled=True)  224 us
    reduce_scatter x1, waiting for transfers between devices, shards(): lax.psum_scatter(numer, 'ckpt', scatter_dimension=0, tiled=True)  220 us
    all_gather x1, blocking collectives, shards(): lax.all_gather(targets, 'tok', axis=0, tiled=True)  87.4 us
    all_to_all x1, blocking collectives, shards(): lax.all_to_all(blended, 'tok', split_axis=0, concat_axis=1, tiled=True)  23.2 us
    all_to_all x2, local copies, waits for them, and re-layouts, shards(): lax.all_to_all(heads[0], 'tok', split_axis=1, concat_axis=0, tiled=True)  18.9 us
    dot_general x1, matrix products, shards(): lax.dot_general(hidden_sq, resid_sq, (((0,), (0,)), ((), ())), preferred_...  17 us
    psum x1, blocking collectives, shards(): level = lax.psum(partial_value, ('tok', 'vocab')) / jnp.float32(count)  14.1 us
  transfers between devices with their start and end apart: 4, of which 2 were waited for; matrix products, arithmetic and copies ran while one was open for 0% of the time, Pallas kernels for 0%

commit v1 on v0

v1 whole, which is shorter than its diff:
```python
import functools

import jax
import jax.numpy as jnp
from jax import lax
from jax.experimental import pallas as pl
from jax.experimental.pallas import tpu as pltpu
from jax.sharding import PartitionSpec as P

prior_weight = 0.05
VMEM = 56 * 1024 * 1024


def score_kernel(turn_ref, *refs):
    states, blocks, out_ref = refs[0:4], refs[4:8], refs[8]
    total = None
    for far in range(4):
        dot = jnp.dot(states[far][...], blocks[far][...], preferred_element_type=jnp.float32)
        total = dot if total is None else total + dot
    out_ref[...] = total


def score(turns, states, blocks):
    tokens = states.shape[0]
    depth, width = blocks[0].shape
    tile = 256 if width % 256 == 0 else 128

    def part(far):
        return pl.BlockSpec((tokens, depth), lambda i, s: (0, s[far]))

    return pl.pallas_call(
        score_kernel,
        out_shape=jax.ShapeDtypeStruct((tokens, width), jnp.float32),
        grid_spec=pltpu.PrefetchScalarGridSpec(
            num_scalar_prefetch=1,
            grid=(width // tile,),
            in_specs=[part(far) for far in range(4)]
            + [pl.BlockSpec((depth, tile), lambda i, s: (0, i))] * 4,
            out_specs=pl.BlockSpec((tokens, tile), lambda i, s: (0, i)),
        ),
        compiler_params=pltpu.CompilerParams(vmem_limit_bytes=VMEM),
        cost_estimate=pl.CostEstimate(flops=0, bytes_accessed=0, transcendentals=0),
        name="score",
    )(turns, *([states] * 4), *blocks)


def merge_kernel(scale_ref, *refs):
    heads, resids, hiddens, out_ref = refs[0:4], refs[4:8], refs[8:12], refs[12]
    numer = denom = None
    for slot in range(4):
        product = lax.dot_general(
            hiddens[slot][...], resids[slot][...], (((1,), (0,)), ((), ())),
            preferred_element_type=jnp.float32,
        )
        scaled = (product * scale_ref[4]) * scale_ref[slot]
        weight = (scaled + prior_weight).astype(jnp.bfloat16).astype(jnp.float32)
        term = weight * heads[slot][...].astype(jnp.float32)
        numer = term if numer is None else numer + term
        denom = weight if denom is None else denom + weight
    out_ref[...] = (numer / denom).astype(out_ref.dtype)


def merge(scales, heads, resids, hiddens, start):
    rows, width = heads[0].shape
    tokens = resids[0].shape[0]
    tile = rows // 2
    tall = pl.BlockSpec((tile, width), lambda i: (i, 0))
    resid = pl.BlockSpec((tokens, width), lambda i: (0, 0))
    hidden = pl.BlockSpec((tile, tokens), lambda i: (i, 0))
    return pl.pallas_call(
        merge_kernel,
        out_shape=jax.ShapeDtypeStruct((rows, width), jnp.bfloat16),
        grid=(rows // tile,),
        in_specs=[pl.BlockSpec(memory_space=pltpu.SMEM)] + [tall] * 4 + [resid] * 4 + [hidden] * 4,
        out_specs=tall,
        compiler_params=pltpu.CompilerParams(vmem_limit_bytes=VMEM),
        cost_estimate=pl.CostEstimate(flops=0, bytes_accessed=0, transcendentals=0),
        name="merge",
    )(scales, *heads, *[x[:, start : start + width] for x in resids], *hiddens)


def after(value, *earlier):
    return lax.optimization_barrier((value, *earlier))[0] if earlier else value


def shards(heads, hidden, targets):
    ntok = lax.axis_size("tok")
    nckpt = lax.axis_size("ckpt")
    nvocab = lax.axis_size("vocab")
    assert ntok == nckpt == 4
    tok = lax.axis_index("tok")
    ckpt = lax.axis_index("ckpt")
    rows = heads[0]
    depth = rows.shape[0]
    width = rows.shape[1] // ntok
    per_device, features_all = hidden.shape[1:]
    tokens = per_device * ntok
    part = width // 5

    def swap(x, far):
        return lax.ppermute(x, "tok", [(t, t ^ far) for t in range(ntok)])

    def from_plane(x, far):
        return lax.ppermute(x, "ckpt", [(c, (c - far) % nckpt) for c in range(nckpt)])

    def shift(x, step, first):
        pairs = [(c, c + step) for c in range(nckpt) if 0 <= c + step < nckpt]
        return lax.ppermute(x, "ckpt", pairs[first:] if step > 0 else pairs[: len(pairs) - first])

    def columns_of(far, lo, w):
        return lax.dynamic_slice(rows, (0, (tok ^ far) * width + lo), (depth, w))

    own, beside = columns_of(0, 0, width), swap(columns_of(1, 0, width), 1)

    def cross(lo, w, deps, extra=None):
        two, three = columns_of(2, lo, w), columns_of(3, lo, w)
        if extra is not None:
            two = jnp.concatenate([two, extra], axis=1)
        return swap(after(two, *deps), 2), swap(after(three, *deps), 3)

    def spread(two, three, lo, skip, w, deps, extra=None):
        def pick(plane):
            return lax.select_n(
                tok ^ plane, own[:, lo : lo + w], beside[:, lo : lo + w],
                two[:, skip : skip + w], three[:, skip : skip + w],
            )

        out = [pick(ckpt)]
        for far in (1, 2, 3):
            plane = (ckpt - far) % nckpt
            piece = pick(plane)
            if extra is not None:
                piece = jnp.concatenate([piece, extra(plane).reshape(-1, w)])
            out.append(from_plane(after(piece, *deps), far))
        return out

    def by_tok(x):
        return jnp.stack([lax.dynamic_index_in_dim(x, tok ^ t, 0, keepdims=False) for t in range(4)])

    two_a, three_a = cross(0, part, ())
    first = (two_a, three_a, beside)

    def features_for(plane):
        return lax.dynamic_slice_in_dim(hidden[0], plane * depth, depth, 1)

    heads_a = spread(two_a, three_a, 0, 0, part, first, features_for)
    two_b, three_b = cross(part, 2 * part, first, hidden[0].reshape(depth, -1))
    second = (two_b, three_b, *heads_a[1:])

    heads_b = spread(two_b, three_b, part, 0, part, second)
    two_c, three_c = cross(3 * part, 2 * part, second)
    near = jnp.stack([hidden[0], two_b[:, 2 * part :].reshape(per_device, -1)])
    pairs = [[t, t + 1] for t in range(0, ntok, 2)]
    states = lax.all_gather(after(near, *second), "tok", axis=0, axis_index_groups=pairs)
    core = tok % 2
    states = jnp.stack(
        [lax.dynamic_index_in_dim(states[:, chip], core ^ c, 0, keepdims=False) for chip in (0, 1) for c in (0, 1)]
    )
    states = by_tok(states).reshape(tokens, features_all)
    third = (two_c, three_c, *heads_b[1:])

    heads_c = spread(two_b, three_b, 2 * part, part, part, third)
    fourth = tuple(heads_c[1:])
    packed = jnp.stack(
        [features_for(ckpt)] + [x[depth:].reshape(per_device, depth) for x in heads_a[1:]]
    )
    features = lax.all_gather(after(packed, *third), "tok", axis=1, tiled=True)
    heads_a = heads_a[:1] + [x[:depth] for x in heads_a[1:]]

    turns = jnp.stack([tok ^ far for far in range(4)]).astype(jnp.int32)
    pieces = [
        score(turns, states, [own[:, lo : lo + w], beside[:, lo : lo + w], two[:, :w], three[:, :w]])
        for lo, w, two, three in (
            (0, part, two_a, three_a), (part, 2 * part, two_b, three_b), (3 * part, 2 * part, two_c, three_c)
        )
    ]
    peak = functools.reduce(jnp.maximum, [jnp.max(x, axis=1) for x in pieces])
    mass = sum(jnp.sum(jnp.exp(x - peak[:, None]), axis=1) for x in pieces)
    local = jnp.concatenate([peak, mass, targets.astype(jnp.float32)])
    every = lax.all_gather(after(local, *third), ("tok", "vocab"), axis=0)
    both = every[:, : 2 * tokens].reshape(-1, 2, tokens)
    top = jnp.max(both[:, 0], axis=0)
    total = jnp.sum(both[:, 1] * jnp.exp(both[:, 0] - top[None]), axis=0)
    labels = every[:, 2 * tokens :].reshape(ntok, nvocab, -1)[:, 0].reshape(-1).astype(jnp.int32)

    offset = (lax.axis_index("vocab") * ntok + tok) * width
    resids = []
    for x, lo in zip(pieces, (0, part, 3 * part)):
        ids = offset + lo + jnp.arange(x.shape[1], dtype=jnp.int32)
        onehot = (labels[:, None] == ids[None, :]).astype(jnp.float32)
        shifted = jnp.exp(x - top[:, None]) / total[:, None]
        resids.append(jnp.square(shifted - onehot).astype(jnp.bfloat16))
    resid_sq = jnp.concatenate(resids, axis=1)

    up = [resid_sq, shift(after(resid_sq, *fourth), 1, 0)]
    down = [resid_sq, shift(after(resid_sq, *fourth), -1, 0)]
    fifth = (up[1], down[1])
    up.append(shift(after(up[1], *fifth), 1, 1))
    down.append(shift(after(down[1], *fifth), -1, 1))
    up.append(lax.ppermute(after(up[1], *fifth), "ckpt", [(1, 3)]))
    down.append(lax.ppermute(after(down[1], *fifth), "ckpt", [(2, 0)]))
    sixth = (up[2], down[2], up[3], down[3])
    heads_d = spread(two_c, three_c, 3 * part, 0, 2 * part, sixth)

    vocab_total = width * ntok * nvocab
    hidden_rows = jnp.sum(
        jnp.square(states.astype(jnp.float32)).astype(jnp.bfloat16).astype(jnp.float32), axis=1
    )
    share = jnp.sum(hidden_rows * jnp.sum(resid_sq.astype(jnp.float32), axis=1))
    count = float(tokens * features_all * vocab_total)
    level = lax.psum(share, ("tok", "vocab")) / jnp.float32(count)
    inverse = jnp.full((8, 128), 1.0 / level, jnp.float32)
    inverses = [inverse] + [from_plane(after(inverse, *fifth), far) for far in (1, 2, 3)]
    scales = jnp.stack(
        [x[0, 0] for x in inverses] + [jnp.float32(vocab_total / tokens)]
    )

    resid_of = [resid_sq]
    for far in range(1, nckpt):
        resid_of.append(jnp.where(ckpt + far < nckpt, down[far], up[nckpt - far]))

    features_sq = [
        jnp.square(features[far].astype(jnp.float32)).astype(jnp.bfloat16).T
        for far in range(nckpt)
    ]

    own_rows = depth // ntok
    result = jnp.zeros((own_rows, width * ntok), jnp.bfloat16)
    for block, lo in ((heads_a, 0), (heads_b, part), (heads_c, 2 * part), (heads_d, 3 * part)):
        blended = merge(scales, block, resid_of, features_sq, lo)
        for far in (2, 3, 1, 0):
            piece = lax.dynamic_slice_in_dim(blended, (tok ^ far) * own_rows, own_rows, 0)
            if far:
                piece = swap(piece, far)
            result = lax.dynamic_update_slice(result, piece, (0, (tok ^ far) * width + lo))
    return result


def solution(mesh):
    placed = (P("ckpt", "tok", "vocab"), P("ckpt", "tok", None), P("tok"))
    return jax.shard_map(
        shards, mesh=mesh, in_specs=placed, out_specs=P(("ckpt", "tok"), "vocab"), check_vma=False
    )
```

time: 671 us -> 407 us (0.61)
  waiting for transfers between devices: 445 us -> 162 us
  blocking collectives: 151 us -> 30.3 us
  starting transfers between devices: 6.14 us -> 57.4 us
  local copies, waits for them, and re-layouts: 20.3 us -> 67.2 us
  Pallas kernels: 0 us -> 34.1 us
  other arithmetic: 8.86 us -> 39.9 us
  matrix products: 24.3 us -> 0 us
    reduce_scatter x2 -> x0, waiting for transfers between devices: 443 us -> none  [the longest x1 224 us: shards(): lax.psum_scatter(weight_wide, 'ckpt', scatter_dimension=0, tiled=True)]
    ppermute x0 -> x40, waiting for transfers between devices: none -> 162 us  [the longest x15 61.3 us: from_plane(): lax.ppermute(x, 'ckpt', [(c, (c - far) % nckpt) for c in range(nckpt)])]
    all_gather x1, blocking collectives: 87.4 us -> 15.9 us  [shards(): every = lax.all_gather(after(local, *third), ('tok', 'vocab'), axis=0)]
    ppermute x0 -> x40, starting transfers between devices: none -> 57.3 us  [the longest x19 19.5 us: swap(): return lax.ppermute(x, 'tok', [(t, t ^ far) for t in range(ntok)])]
    pallas_call x0 -> x7, Pallas kernels: none -> 34.1 us  [the longest x4 18.1 us: merge(): pl.pallas_call(merge_kernel, out_shape=jax.ShapeDtypeStruct((rows, width)...]
    dot_general x2 -> x0, matrix products: 24.3 us -> none  [the longest x1 17 us: shards(): lax.dot_general(hidden_sq, resid_sq, (((0,), (0,)), ((), ())), preferred_...]
    all_to_all x1 -> x0, blocking collectives: 23.2 us -> none  [shards(): lax.all_to_all(blended, 'tok', split_axis=0, concat_axis=1, tiled=True)]
    slice x0 -> x20, local copies, waits for them, and re-layouts: none -> 22 us  [the longest x7 6.15 us: merge(): x[:, start:start + width]]
  transfers between devices with their start and end apart: 4 -> 42, of which waited for: 2 -> 20; matrix products, arithmetic and copies ran while one was open for 0% -> 24% of each run, Pallas kernels for 0% -> 8%
where the time goes in v1:
time: 407 us; the launch traced here: 405 us
  waiting for transfers between devices  162 us (40%)
  local copies, waits for them, and re-layouts  67.2 us (17%)
  starting transfers between devices  57.4 us (14%)
  other arithmetic  39.9 us (10%)
  Pallas kernels  34.1 us (8%)
  blocking collectives  30.3 us (7%)
  between operations  14.7 us (4%)
    ppermute x15, waiting for transfers between devices, from_plane(): lax.ppermute(x, 'ckpt', [(c, (c - far) % nckpt) for c in range(nckpt)])  61.3 us
    ppermute x19, waiting for transfers between devices, swap(): return lax.ppermute(x, 'tok', [(t, t ^ far) for t in range(ntok)])  56.7 us
    ppermute x4, waiting for transfers between devices, shift(): lax.ppermute(x, 'ckpt', pairs[first:] if step > 0 else pairs[:len(pairs)...  29.5 us
    ppermute x19, starting transfers between devices, swap(): return lax.ppermute(x, 'tok', [(t, t ^ far) for t in range(ntok)])  19.5 us
    pallas_call x4, Pallas kernels, merge(): pl.pallas_call(merge_kernel, out_shape=jax.ShapeDtypeStruct((rows, width)...  18.1 us
    pallas_call x3, Pallas kernels, score(): pl.pallas_call(score_kernel, out_shape=jax.ShapeDtypeStruct((tokens, widt...  16 us
    all_gather x1, blocking collectives, shards(): every = lax.all_gather(after(local, *third), ('tok', 'vocab'), axis=0)  15.9 us
    ppermute x4, starting transfers between devices, shift(): lax.ppermute(x, 'ckpt', pairs[first:] if step > 0 else pairs[:len(pairs)...  15.4 us
  transfers between devices with their start and end apart: 42, of which 20 were waited for; matrix products, arithmetic and copies ran while one was open for 24% of the time, Pallas kernels for 8%

profile of v1, /device:TPU:9, one launch (start us, length us, event | category | flops | bytes accessed | tf_op | source)
XLA Modules:
  0.0 405.1 jit_solution(4484671867391353414)
XLA Ops:
  6.5 3.3 dynamic-slice_bitcast_fusion
  14.1 2.3 reshape_squeeze.4
  16.4 3.1 dynamic-slice_bitcast_fusion.2
  22.1 7.1 %collective-permute-done.1.refs_7_ = bf16[640,256]{1,0:T(8,128)(2,1)} collective-permute-done((bf16[640,256]{1,0:T(8,128)(2,1)}, bf16[640,256]{1,0:T(8,128)(2,1)}, u32[]{:S(2)}, u32[]{:S(2)}) %collective-permute-start.1) | collective-permute-done | bytes 327712 | tf_op jit(solution)/shard_map/ppermute | solution.py:101
  43.6 30.5 %collective-permute-done.4.refs_7_ = bf16[640,512]{1,0:T(8,128)(2,1)} collective-permute-done((bf16[640,512]{1,0:T(8,128)(2,1)}, bf16[640,512]{1,0:T(8,128)(2,1)}, u32[]{:S(2)}, u32[]{:S(2)}) %collective-permute-start.4) | collective-permute-done | bytes 655392 | tf_op jit(solution)/shard_map/ppermute | solution.py:101
  74.1 2.4 select_select_fusion.9
  77.7 2.4 fusion.12
  80.1 2.3 stack_reshape.12
  82.4 2.5 pad_maximum_fusion.3
  84.9 5.7 %collective-permute-done.5 = bf16[960,256]{1,0:T(8,128)(2,1)} collective-permute-done((bf16[960,256]{1,0:T(8,128)(2,1)}, bf16[960,256]{1,0:T(8,128)(2,1)}, u32[]{:S(2)}, u32[]{:S(2)}) %collective-permute-start.5) | collective-permute-done | bytes 491552 | tf_op jit(solution)/shard_map/ppermute | solution.py:104
  93.6 2.5 select_select_fusion.5
  96.1 2.5 select_select_fusion.4
  100.0 3.0 collective-permute-start.11
  120.2 2.0 pad_maximum_fusion.5
  122.2 6.1 %collective-permute-done.11.refs_2_ = bf16[640,256]{1,0:T(8,128)(2,1)} collective-permute-done((bf16[640,256]{1,0:T(8,128)(2,1)}, bf16[640,256]{1,0:T(8,128)(2,1)}, u32[]{:S(2)}, u32[]{:S(2)}) %collective-permute-start.11) | collective-permute-done | bytes 327712 | tf_op jit(solution)/shard_map/ppermute | solution.py:104
  128.4 4.3 %collective-permute-done.10.refs_1_ = bf16[640,256]{1,0:T(8,128)(2,1)} collective-permute-done((bf16[640,256]{1,0:T(8,128)(2,1)}, bf16[640,256]{1,0:T(8,128)(2,1)}, u32[]{:S(2)}, u32[]{:S(2)}) %collective-permute-start.10) | collective-permute-done | bytes 327712 | tf_op jit(solution)/shard_map/ppermute | solution.py:104
  134.1 2.5 select_select_fusion.3
  136.7 3.2 select_select_fusion
  144.3 4.6 %score.3 = f32[512,256]{1,0:T(8,128)} custom-call(s32[4]{0:T(128)} %pad_add_fusion.turn_ref, bf16[512,2560]{1,0:T(8,128)(2,1)} %bitcast.72, bf16[512,2560]{1,0:T(8,128)(2,1)} %bitcast.73, bf16[512,2560]{1,0:T(8,128)(2,1)} %bitcast.74, bf16[512,2560]{1,0:T(8,128)(2,1)} %bitcast.75, bf16[640,256]{1,0:T(8,128)(2,1)} %get-tuple-element.95.refs_4_, ...), custom_call_target="tpu_custom_call" | custom-call | tf_op jit(solution)/shard_map/score/pallas_call | solution.py:31
  150.1 5.7 %score.5 = f32[512,512]{1,0:T(8,128)} custom-call(s32[4]{0:T(128)} %pad_add_fusion.turn_ref, bf16[512,2560]{1,0:T(8,128)(2,1)} %bitcast.76, bf16[512,2560]{1,0:T(8,128)(2,1)} %bitcast.77, bf16[512,2560]{1,0:T(8,128)(2,1)} %bitcast.78, bf16[512,2560]{1,0:T(8,128)(2,1)} %bitcast.79, bf16[640,512]{1,0:T(8,128)(2,1)} %get-tuple-element.90.refs_4_, ...), custom_call_target="tpu_custom_call" | custom-call | tf_op jit(solution)/shard_map/score/pallas_call | solution.py:31
  157.2 5.7 %score.4 = f32[512,512]{1,0:T(8,128)} custom-call(s32[4]{0:T(128)} %pad_add_fusion.turn_ref, bf16[512,2560]{1,0:T(8,128)(2,1)} %bitcast.80, bf16[512,2560]{1,0:T(8,128)(2,1)} %bitcast.81, bf16[512,2560]{1,0:T(8,128)(2,1)} %bitcast.82, bf16[512,2560]{1,0:T(8,128)(2,1)} %bitcast.83, bf16[640,512]{1,0:T(8,128)(2,1)} %get-tuple-element.91.refs_4_, ...), custom_call_target="tpu_custom_call" | custom-call | tf_op jit(solution)/shard_map/score/pallas_call | solution.py:31
  166.4 15.9 %all-gather.2 = f32[8,1,1152]{2,1,0:T(1,128)S(1)} all-gather(f32[1,1,1152]{2,1,0:T(1,128)S(1)} %reshape.93), channel_id=3, replica_groups=mesh['ckpt'=4,'tok'=4,'vocab'=2] {'tok','vocab'}, dimensions={0}, use_global_device_ids=true | all-gather | bytes 41472 | tf_op jit(solution)/shard_map/all_gather | solution.py:180
  184.0 3.1 collective-permute-start.16
  187.1 3.5 collective-permute-start.17
  190.6 26.2 %collective-permute-done.16 = bf16[512,1280]{1,0:T(8,128)(2,1)} collective-permute-done((bf16[512,1280]{1,0:T(8,128)(2,1)S(1)}, bf16[512,1280]{1,0:T(8,128)(2,1)}, u32[]{:S(2)}, u32[]{:S(2)}) %collective-permute-start.16) | collective-permute-done | bytes 1310752 | tf_op jit(solution)/shard_map/ppermute | solution.py:108
  216.8 3.3 collective-permute-done.17
  221.9 2.4 collective-permute-start.22
  224.4 6.4 %collective-permute-start.23 = (bf16[512,1280]{1,0:T(8,128)(2,1)}, bf16[512,1280]{1,0:T(8,128)(2,1)}, u32[]{:S(2)}, u32[]{:S(2)}) collective-permute-start(bf16[512,1280]{1,0:T(8,128)(2,1)} %collective-permute-done.16), channel_id=1, source_target_pairs={{8,16},{16,24},{9,17},{17,25},{10,18},{18,26},{11,19},{19,27},{12,... | collective-permute-start | bytes 3932168 | tf_op jit(solution)/shard_map/ppermute | solution.py:108
  231.4 14.4 %psum.7 = f32[]{:T(128)} all-reduce(f32[]{:T(128)} %fusion.7), channel_id=1, replica_groups=mesh['ckpt'=4,'tok'=4,'vocab'=2] {'tok','vocab'}, use_global_device_ids=true, to_apply=%region_11.12 | all-reduce | flops 1 | bytes 8 | tf_op jit(solution)/shard_map/psum | solution.py:211
  251.8 29.1 %collective-permute-done.18 = f32[8,128]{1,0:T(8,128)S(1)} collective-permute-done((f32[8,128]{1,0:T(8,128)S(1)}, f32[8,128]{1,0:T(8,128)S(1)}, u32[]{:S(2)}, u32[]{:S(2)}) %collective-permute-start.18) | collective-permute-done | bytes 4128 | tf_op jit(solution)/shard_map/ppermute | solution.py:104
  282.3 6.1 %collective-permute-start.21 = (bf16[512,1280]{1,0:T(8,128)(2,1)}, bf16[512,1280]{1,0:T(8,128)(2,1)S(1)}, u32[]{:S(2)}, u32[]{:S(2)}) collective-permute-start(bf16[512,1280]{1,0:T(8,128)(2,1)} %collective-permute-done.16), channel_id=1, source_target_pairs={{8,24},{9,25},{10,26},{11,27},{12,28},{13,29},{14,30},{15,31}} | collective-permute-start | bytes 3932168 | tf_op jit(solution)/shard_map/ppermute | solution.py:200
  289.5 2.5 stack.47.scale_ref
  292.0 3.5 fusion.3
  302.0 14.0 %collective-permute-done.21 = bf16[512,1280]{1,0:T(8,128)(2,1)S(1)} collective-permute-done((bf16[512,1280]{1,0:T(8,128)(2,1)}, bf16[512,1280]{1,0:T(8,128)(2,1)S(1)}, u32[]{:S(2)}, u32[]{:S(2)}) %collective-permute-start.21) | collective-permute-done | bytes 1310752 | tf_op jit(solution)/shard_map/ppermute | solution.py:200
  318.0 3.1 collective-permute-start.35
  322.4 4.1 %merge.6 = bf16[640,256]{1,0:T(8,128)(2,1)} custom-call(f32[5]{0:T(128)} %stack.47.scale_ref, bf16[640,256]{1,0:T(8,128)(2,1)} %get-tuple-element.65.refs_0_, bf16[640,256]{1,0:T(8,128)(2,1)} %collective-permute-done.13.refs_1_, bf16[640,256]{1,0:T(8,128)(2,1)} %collective-permute-done.14.refs_2_, bf16[640,256]{1,0:T(8,128)(2,1)} %collective-permute-done.15.refs_3_, ...), custom_call_target="tpu_custom_call" | custom-call | tf_op jit(solution)/shard_map/merge/pallas_call | solution.py:70
  328.0 4.1 %merge.4 = bf16[640,256]{1,0:T(8,128)(2,1)} custom-call(f32[5]{0:T(128)} %stack.47.scale_ref, bf16[640,256]{1,0:T(8,128)(2,1)} %get-tuple-element.76.refs_0_, bf16[640,256]{1,0:T(8,128)(2,1)} %slice.267.refs_1_, bf16[640,256]{1,0:T(8,128)(2,1)} %slice.268.refs_2_, bf16[640,256]{1,0:T(8,128)(2,1)} %slice.269.refs_3_, bf16[512,256]{1,0:T(8,128)(2,1)} %copy-done.5, ...), custom_call_target="tpu_custom_call" | custom-call | tf_op jit(solution)/shard_map/merge/pallas_call | solution.py:70
  334.3 4.1 %merge.5 = bf16[640,256]{1,0:T(8,128)(2,1)} custom-call(f32[5]{0:T(128)} %stack.47.scale_ref, bf16[640,256]{1,0:T(8,128)(2,1)} %get-tuple-element.68.refs_0_, bf16[640,256]{1,0:T(8,128)(2,1)} %collective-permute-done.10.refs_1_, bf16[640,256]{1,0:T(8,128)(2,1)} %collective-permute-done.11.refs_2_, bf16[640,256]{1,0:T(8,128)(2,1)} %collective-permute-done.12.refs_3_, ...), custom_call_target="tpu_custom_call" | custom-call | tf_op jit(solution)/shard_map/merge/pallas_call | solution.py:70
  339.4 3.4 collective-permute-start.26
  342.9 2.4 collective-permute-done.26
  351.1 2.1 collective-permute-start.29
  353.2 3.2 collective-permute-done.29
  359.8 2.3 collective-permute-done.32
  362.2 10.6 %collective-permute-done.35.refs_2_ = bf16[640,512]{1,0:T(8,128)(2,1)S(1)} collective-permute-done((bf16[640,512]{1,0:T(8,128)(2,1)S(1)}, bf16[640,512]{1,0:T(8,128)(2,1)S(1)}, u32[]{:S(2)}, u32[]{:S(2)}) %collective-permute-start.35) | collective-permute-done | bytes 655392 | tf_op jit(solution)/shard_map/ppermute | solution.py:104
  372.8 5.5 %collective-permute-done.34.refs_1_ = bf16[640,512]{1,0:T(8,128)(2,1)S(1)} collective-permute-done((bf16[640,512]{1,0:T(8,128)(2,1)S(1)}, bf16[640,512]{1,0:T(8,128)(2,1)S(1)}, u32[]{:S(2)}, u32[]{:S(2)}) %collective-permute-start.34) | collective-permute-done | bytes 655392 | tf_op jit(solution)/shard_map/ppermute | solution.py:104
  379.2 5.7 %merge.7 = bf16[640,512]{1,0:T(8,128)(2,1)} custom-call(f32[5]{0:T(128)} %stack.47.scale_ref, bf16[640,512]{1,0:T(8,128)(2,1)} %get-tuple-element.92.refs_0_, bf16[640,512]{1,0:T(8,128)(2,1)} %copy-done.9, bf16[640,512]{1,0:T(8,128)(2,1)} %copy-done.8, bf16[640,512]{1,0:T(8,128)(2,1)} %copy-done.7, bf16[512,512]{1,0:T(8,128)(2,1)} %copy-done.3, ...), custom_call_target="tpu_custom_call" | custom-call | tf_op jit(solution)/shard_map/merge/pallas_call | solution.py:70
  389.1 2.2 collective-permute-done.37
  391.3 4.1 %collective-permute-done.38 = bf16[160,512]{1,0:T(8,128)(2,1)S(1)} collective-permute-done((bf16[160,512]{1,0:T(8,128)(2,1)S(1)}, bf16[160,512]{1,0:T(8,128)(2,1)S(1)}, u32[]{:S(2)}, u32[]{:S(2)}) %collective-permute-start.38) | collective-permute-done | bytes 163872 | tf_op jit(solution)/shard_map/ppermute | solution.py:101
  (183 shorter events, 99.3 us)
Async XLA Ops:
  6.5 133.3 %all-gather.8.cloned.1.call-start = ((), (), s32[]{:S(2)}) async-start(), calls=%async_computation.1 | async-start | bytes 3932160 | tf_op jit(solution)/shard_map/all_gather | solution.py:154
  9.8 19.4 %collective-permute-start.2 = (bf16[640,1280]{1,0:T(8,128)(2,1)}, bf16[640,1280]{1,0:T(8,128)(2,1)S(1)}, u32[]{:S(2)}, u32[]{:S(2)}) collective-permute-start(bf16[640,1280]{1,0:T(8,128)(2,1)} %get-tuple-element.62), channel_id=1, source_target_pairs={{0,2},{2,0},{4,6},{6,4},{1,3},{3,1},{5,7},{7,5},{8,10},{10,8},{12,... | collective-permute-start | bytes 4915208 | tf_op jit(solution)/shard_map/ppermute | solution.py:101
  12.5 9.7 %collective-permute-start = (bf16[640,256]{1,0:T(8,128)(2,1)}, bf16[640,256]{1,0:T(8,128)(2,1)}, u32[]{:S(2)}, u32[]{:S(2)}) collective-permute-start(bf16[640,256]{1,0:T(8,128)(2,1)} %get-tuple-element.64), channel_id=1, source_target_pairs={{0,4},{2,6},{4,0},{6,2},{1,5},{3,7},{5,1},{7,3},{8,12},{10,14},{12... | collective-permute-start | bytes 983048 | tf_op jit(solution)/shard_map/ppermute | solution.py:101
  13.7 15.6 %collective-permute-start.1 = (bf16[640,256]{1,0:T(8,128)(2,1)}, bf16[640,256]{1,0:T(8,128)(2,1)}, u32[]{:S(2)}, u32[]{:S(2)}) collective-permute-start(bf16[640,256]{1,0:T(8,128)(2,1)} %get-tuple-element.63), channel_id=1, source_target_pairs={{0,6},{2,4},{4,2},{6,0},{1,7},{3,5},{5,3},{7,1},{8,14},{10,12},{12... | collective-permute-start | bytes 983048 | tf_op jit(solution)/shard_map/ppermute | solution.py:101
  29.3 44.9 %collective-permute-start.3 = (bf16[640,1024]{1,0:T(8,128)(2,1)}, bf16[640,1024]{1,0:T(8,128)(2,1)}, u32[]{:S(2)}, u32[]{:S(2)}) collective-permute-start(bf16[640,1024]{1,0:T(8,128)(2,1)} %pad_maximum_fusion.2), channel_id=1, source_target_pairs={{0,4},{2,6},{4,0},{6,2},{1,5},{3,7},{5,1},{7,3},{8,12},{10,14},{12... | collective-permute-start | bytes 3932168 | tf_op jit(solution)/shard_map/ppermute | solution.py:101
  30.5 43.7 %collective-permute-start.4 = (bf16[640,512]{1,0:T(8,128)(2,1)}, bf16[640,512]{1,0:T(8,128)(2,1)}, u32[]{:S(2)}, u32[]{:S(2)}) collective-permute-start(bf16[640,512]{1,0:T(8,128)(2,1)} %get-tuple-element.29), channel_id=1, source_target_pairs={{0,6},{2,4},{4,2},{6,0},{1,7},{3,5},{5,3},{7,1},{8,14},{10,12},{12... | collective-permute-start | bytes 1966088 | tf_op jit(solution)/shard_map/ppermute | solution.py:101
  41.3 43.6 %collective-permute-start.7 = (bf16[960,256]{1,0:T(8,128)(2,1)}, bf16[960,256]{1,0:T(8,128)(2,1)}, u32[]{:S(2)}, u32[]{:S(2)}) collective-permute-start(bf16[960,256]{1,0:T(8,128)(2,1)} %get-tuple-element.32), channel_id=1, source_target_pairs={{0,8},{8,16},{16,24},{24,0},{1,9},{9,17},{17,25},{25,1},{2,10},{10... | collective-permute-start | bytes 1474568 | tf_op jit(solution)/shard_map/ppermute | solution.py:104
  42.6 33.9 %copy-start.14 = (bf16[320,256]{1,0:T(8,128)(2,1)S(1)}, bf16[320,256]{1,0:T(8,128)(2,1)}, u32[]{:S(2)}) copy-start(bf16[320,256]{1,0:T(8,128)(2,1)} %reshape.85) | copy-start | bytes 491524
  42.6 42.3 %collective-permute-start.6 = (bf16[960,256]{1,0:T(8,128)(2,1)}, bf16[960,256]{1,0:T(8,128)(2,1)}, u32[]{:S(2)}, u32[]{:S(2)}) collective-permute-start(bf16[960,256]{1,0:T(8,128)(2,1)} %get-tuple-element.31), channel_id=1, source_target_pairs={{0,16},{8,24},{16,0},{24,8},{1,17},{9,25},{17,1},{25,9},{2,18},{10... | collective-permute-start | bytes 1474568 | tf_op jit(solution)/shard_map/ppermute | solution.py:104
  77.3 13.2 %collective-permute-start.5 = (bf16[960,256]{1,0:T(8,128)(2,1)}, bf16[960,256]{1,0:T(8,128)(2,1)}, u32[]{:S(2)}, u32[]{:S(2)}) collective-permute-start(bf16[960,256]{1,0:T(8,128)(2,1)} %pad_maximum_fusion.6), channel_id=1, source_target_pairs={{0,24},{8,0},{16,8},{24,16},{1,25},{9,1},{17,9},{25,17},{2,26},{10... | collective-permute-start | bytes 1474568 | tf_op jit(solution)/shard_map/ppermute | solution.py:104
  82.4 8.3 %copy-start.17 = (s32[128]{0:T(128)S(1)}, s32[128]{0:T(128)}, u32[]{:S(2)}) copy-start(s32[128]{0:T(128)} %param.5) | copy-start | bytes 1540
  90.6 201.4 %all-gather.6.cloned.1.call-start = ((), (), s32[]{:S(2)}) async-start(), calls=%async_computation | async-start | bytes 3276800 | tf_op jit(solution)/shard_map/all_gather | solution.py:167
  91.5 41.1 %collective-permute-start.9 = (bf16[640,512]{1,0:T(8,128)(2,1)}, bf16[640,512]{1,0:T(8,128)(2,1)}, u32[]{:S(2)}, u32[]{:S(2)}) collective-permute-start(bf16[640,512]{1,0:T(8,128)(2,1)} %get-tuple-element.35), channel_id=1, source_target_pairs={{0,6},{2,4},{4,2},{6,0},{1,7},{3,5},{5,3},{7,1},{8,14},{10,12},{12... | collective-permute-start | bytes 1966088 | tf_op jit(solution)/shard_map/ppermute | solution.py:101
  93.4 39.3 %collective-permute-start.8 = (bf16[640,512]{1,0:T(8,128)(2,1)}, bf16[640,512]{1,0:T(8,128)(2,1)}, u32[]{:S(2)}, u32[]{:S(2)}) collective-permute-start(bf16[640,512]{1,0:T(8,128)(2,1)} %get-tuple-element.34), channel_id=1, source_target_pairs={{0,4},{2,6},{4,0},{6,2},{1,5},{3,7},{5,1},{7,3},{8,12},{10,14},{12... | collective-permute-start | bytes 1966088 | tf_op jit(solution)/shard_map/ppermute | solution.py:101
  98.6 21.6 %copy-start.13 = (bf16[1,128,640]{1,2,0:T(8,128)(2,1)S(1)}, bf16[1,128,640]{1,2,0:T(8,128)(2,1)}, u32[]{:S(2)}) copy-start(bf16[1,128,640]{1,2,0:T(8,128)(2,1)} %copy.14) | copy-start | bytes 491524
  98.6 23.6 %collective-permute-start.12 = (bf16[640,256]{1,0:T(8,128)(2,1)}, bf16[640,256]{1,0:T(8,128)(2,1)}, u32[]{:S(2)}, u32[]{:S(2)}) collective-permute-start(bf16[640,256]{1,0:T(8,128)(2,1)} %get-tuple-element.38), channel_id=1, source_target_pairs={{0,8},{8,16},{16,24},{24,0},{1,9},{9,17},{17,25},{25,1},{2,10},{10... | collective-permute-start | bytes 983048 | tf_op jit(solution)/shard_map/ppermute | solution.py:104
  100.0 28.3 %collective-permute-start.11 = (bf16[640,256]{1,0:T(8,128)(2,1)}, bf16[640,256]{1,0:T(8,128)(2,1)}, u32[]{:S(2)}, u32[]{:S(2)}) collective-permute-start(bf16[640,256]{1,0:T(8,128)(2,1)} %get-tuple-element.37), channel_id=1, source_target_pairs={{0,16},{8,24},{16,0},{24,8},{1,17},{9,25},{17,1},{25,9},{2,18},{10... | collective-permute-start | bytes 983048 | tf_op jit(solution)/shard_map/ppermute | solution.py:104
  103.1 29.6 %collective-permute-start.10 = (bf16[640,256]{1,0:T(8,128)(2,1)}, bf16[640,256]{1,0:T(8,128)(2,1)}, u32[]{:S(2)}, u32[]{:S(2)}) collective-permute-start(bf16[640,256]{1,0:T(8,128)(2,1)} %get-tuple-element.36), channel_id=1, source_target_pairs={{0,24},{8,0},{16,8},{24,16},{1,25},{9,1},{17,9},{25,17},{2,26},{10... | collective-permute-start | bytes 983048 | tf_op jit(solution)/shard_map/ppermute | solution.py:104
  132.6 51.3 %collective-permute-start.15 = (bf16[640,256]{1,0:T(8,128)(2,1)}, bf16[640,256]{1,0:T(8,128)(2,1)}, u32[]{:S(2)}, u32[]{:S(2)}) collective-permute-start(bf16[640,256]{1,0:T(8,128)(2,1)} %get-tuple-element.42), channel_id=1, source_target_pairs={{0,8},{8,16},{16,24},{24,0},{1,9},{9,17},{17,25},{25,1},{2,10},{10... | collective-permute-start | bytes 983048 | tf_op jit(solution)/shard_map/ppermute | solution.py:104
  132.6 51.3 %collective-permute-start.14 = (bf16[640,256]{1,0:T(8,128)(2,1)}, bf16[640,256]{1,0:T(8,128)(2,1)}, u32[]{:S(2)}, u32[]{:S(2)}) collective-permute-start(bf16[640,256]{1,0:T(8,128)(2,1)} %get-tuple-element.41), channel_id=1, source_target_pairs={{0,16},{8,24},{16,0},{24,8},{1,17},{9,25},{17,1},{25,9},{2,18},{10... | collective-permute-start | bytes 983048 | tf_op jit(solution)/shard_map/ppermute | solution.py:104
  132.7 51.2 %collective-permute-start.13 = (bf16[640,256]{1,0:T(8,128)(2,1)}, bf16[640,256]{1,0:T(8,128)(2,1)}, u32[]{:S(2)}, u32[]{:S(2)}) collective-permute-start(bf16[640,256]{1,0:T(8,128)(2,1)} %get-tuple-element.40), channel_id=1, source_target_pairs={{0,24},{8,0},{16,8},{24,16},{1,25},{9,1},{17,9},{25,17},{2,26},{10... | collective-permute-start | bytes 983048 | tf_op jit(solution)/shard_map/ppermute | solution.py:104
  164.4 18.1 %copy-start.1 = (f32[512,512]{1,0:T(8,128)S(1)}, f32[512,512]{1,0:T(8,128)}, u32[]{:S(2)}) copy-start(f32[512,512]{1,0:T(8,128)} %score.4) | copy-start | bytes 3145732
  183.4 64.9 %copy-start.5 = (bf16[512,256]{1,0:T(8,128)(2,1)}, bf16[512,256]{1,0:T(8,128)(2,1)S(1)}, u32[]{:S(2)}) copy-start(bf16[512,256]{1,0:T(8,128)(2,1)S(1)} %multiply_convert_fusion.7.refs_4_) | copy-start | bytes 786436
  184.0 32.8 %collective-permute-start.16 = (bf16[512,1280]{1,0:T(8,128)(2,1)S(1)}, bf16[512,1280]{1,0:T(8,128)(2,1)}, u32[]{:S(2)}, u32[]{:S(2)}) collective-permute-start(bf16[512,1280]{1,0:T(8,128)(2,1)S(1)} %get-tuple-element.43), channel_id=1, source_target_pairs={{0,8},{8,16},{16,24},{1,9},{9,17},{17,25},{2,10},{10,18},{18,26},{... | collective-permute-start | bytes 3932168 | tf_op jit(solution)/shard_map/ppermute | solution.py:108
  187.1 33.0 %collective-permute-start.17 = (bf16[512,1280]{1,0:T(8,128)(2,1)S(1)}, bf16[512,1280]{1,0:T(8,128)(2,1)S(1)}, u32[]{:S(2)}, u32[]{:S(2)}) collective-permute-start(bf16[512,1280]{1,0:T(8,128)(2,1)S(1)} %get-tuple-element.43), channel_id=1, source_target_pairs={{8,0},{16,8},{24,16},{9,1},{17,9},{25,17},{10,2},{18,10},{26,18},{... | collective-permute-start | bytes 3932168 | tf_op jit(solution)/shard_map/ppermute | solution.py:108
  220.1 75.4 %collective-permute-start.24 = (bf16[512,1280]{1,0:T(8,128)(2,1)S(1)}, bf16[512,1280]{1,0:T(8,128)(2,1)}, u32[]{:S(2)}, u32[]{:S(2)}) collective-permute-start(bf16[512,1280]{1,0:T(8,128)(2,1)S(1)} %collective-permute-done.17), channel_id=1, source_target_pairs={{16,0},{17,1},{18,2},{19,3},{20,4},{21,5},{22,6},{23,7}} | collective-permute-start | bytes 3932168 | tf_op jit(solution)/shard_map/ppermute | solution.py:201
  221.9 75.9 %collective-permute-start.22 = (bf16[512,1280]{1,0:T(8,128)(2,1)S(1)}, bf16[512,1280]{1,0:T(8,128)(2,1)}, u32[]{:S(2)}, u32[]{:S(2)}) collective-permute-start(bf16[512,1280]{1,0:T(8,128)(2,1)S(1)} %collective-permute-done.17), channel_id=1, source_target_pairs={{8,0},{16,8},{9,1},{17,9},{10,2},{18,10},{11,3},{19,11},{12,4},{20... | collective-permute-start | bytes 3932168 | tf_op jit(solution)/shard_map/ppermute | solution.py:108
  224.4 73.4 %collective-permute-start.23 = (bf16[512,1280]{1,0:T(8,128)(2,1)}, bf16[512,1280]{1,0:T(8,128)(2,1)}, u32[]{:S(2)}, u32[]{:S(2)}) collective-permute-start(bf16[512,1280]{1,0:T(8,128)(2,1)} %collective-permute-done.16), channel_id=1, source_target_pairs={{8,16},{16,24},{9,17},{17,25},{10,18},{18,26},{11,19},{19,27},{12,... | collective-permute-start | bytes 3932168 | tf_op jit(solution)/shard_map/ppermute | solution.py:108
  246.5 34.5 %collective-permute-start.18 = (f32[8,128]{1,0:T(8,128)S(1)}, f32[8,128]{1,0:T(8,128)S(1)}, u32[]{:S(2)}, u32[]{:S(2)}) collective-permute-start(f32[8,128]{1,0:T(8,128)S(1)} %broadcast_in_dim.5), channel_id=1, source_target_pairs={{0,24},{8,0},{16,8},{24,16},{1,25},{9,1},{17,9},{25,17},{2,26},{10... | collective-permute-start | bytes 12296 | tf_op jit(solution)/shard_map/ppermute | solution.py:104
  251.8 30.5 %collective-permute-start.19 = (f32[8,128]{1,0:T(8,128)S(1)}, f32[8,128]{1,0:T(8,128)S(1)}, u32[]{:S(2)}, u32[]{:S(2)}) collective-permute-start(f32[8,128]{1,0:T(8,128)S(1)} %broadcast_in_dim.5), channel_id=1, source_target_pairs={{0,16},{8,24},{16,0},{24,8},{1,17},{9,25},{17,1},{25,9},{2,18},{10... | collective-permute-start | bytes 12296 | tf_op jit(solution)/shard_map/ppermute | solution.py:104
  281.0 8.0 %collective-permute-start.20 = (f32[8,128]{1,0:T(8,128)S(1)}, f32[8,128]{1,0:T(8,128)S(1)}, u32[]{:S(2)}, u32[]{:S(2)}) collective-permute-start(f32[8,128]{1,0:T(8,128)S(1)} %broadcast_in_dim.5), channel_id=1, source_target_pairs={{0,8},{8,16},{16,24},{24,0},{1,9},{9,17},{17,25},{25,1},{2,10},{10... | collective-permute-start | bytes 12296 | tf_op jit(solution)/shard_map/ppermute | solution.py:104
  282.3 33.7 %collective-permute-start.21 = (bf16[512,1280]{1,0:T(8,128)(2,1)}, bf16[512,1280]{1,0:T(8,128)(2,1)S(1)}, u32[]{:S(2)}, u32[]{:S(2)}) collective-permute-start(bf16[512,1280]{1,0:T(8,128)(2,1)} %collective-permute-done.16), channel_id=1, source_target_pairs={{8,24},{9,25},{10,26},{11,27},{12,28},{13,29},{14,30},{15,31}} | collective-permute-start | bytes 3932168 | tf_op jit(solution)/shard_map/ppermute | solution.py:200
  317.9 44.3 %collective-permute-start.36 = (bf16[640,512]{1,0:T(8,128)(2,1)S(1)}, bf16[640,512]{1,0:T(8,128)(2,1)S(1)}, u32[]{:S(2)}, u32[]{:S(2)}) collective-permute-start(bf16[640,512]{1,0:T(8,128)(2,1)S(1)} %copy-done.12), channel_id=1, source_target_pairs={{0,8},{8,16},{16,24},{24,0},{1,9},{9,17},{17,25},{25,1},{2,10},{10... | collective-permute-start | bytes 1966088 | tf_op jit(solution)/shard_map/ppermute | solution.py:104
  318.0 54.8 %collective-permute-start.35 = (bf16[640,512]{1,0:T(8,128)(2,1)S(1)}, bf16[640,512]{1,0:T(8,128)(2,1)S(1)}, u32[]{:S(2)}, u32[]{:S(2)}) collective-permute-start(bf16[640,512]{1,0:T(8,128)(2,1)S(1)} %copy-done.11), channel_id=1, source_target_pairs={{0,16},{8,24},{16,0},{24,8},{1,17},{9,25},{17,1},{25,9},{2,18},{10... | collective-permute-start | bytes 1966088 | tf_op jit(solution)/shard_map/ppermute | solution.py:104
  321.0 57.3 %collective-permute-start.34 = (bf16[640,512]{1,0:T(8,128)(2,1)S(1)}, bf16[640,512]{1,0:T(8,128)(2,1)S(1)}, u32[]{:S(2)}, u32[]{:S(2)}) collective-permute-start(bf16[640,512]{1,0:T(8,128)(2,1)S(1)} %copy-done.10), channel_id=1, source_target_pairs={{0,24},{8,0},{16,8},{24,16},{1,25},{9,1},{17,9},{25,17},{2,26},{10... | collective-permute-start | bytes 1966088 | tf_op jit(solution)/shard_map/ppermute | solution.py:104
  327.5 32.1 %collective-permute-start.31 = (bf16[160,256]{1,0:T(8,128)(2,1)S(1)}, bf16[160,256]{1,0:T(8,128)(2,1)S(1)}, u32[]{:S(2)}, u32[]{:S(2)}) collective-permute-start(bf16[160,256]{1,0:T(8,128)(2,1)S(1)} %get-tuple-element.123), channel_id=1, source_target_pairs={{0,4},{2,6},{4,0},{6,2},{1,5},{3,7},{5,1},{7,3},{8,12},{10,14},{12... | collective-permute-start | bytes 245768 | tf_op jit(solution)/shard_map/ppermute | solution.py:101
  333.1 6.2 %collective-permute-start.25 = (bf16[160,256]{1,0:T(8,128)(2,1)S(1)}, bf16[160,256]{1,0:T(8,128)(2,1)S(1)}, u32[]{:S(2)}, u32[]{:S(2)}) collective-permute-start(bf16[160,256]{1,0:T(8,128)(2,1)S(1)} %get-tuple-element.129), channel_id=1, source_target_pairs={{0,4},{2,6},{4,0},{6,2},{1,5},{3,7},{5,1},{7,3},{8,12},{10,14},{12... | collective-permute-start | bytes 245768 | tf_op jit(solution)/shard_map/ppermute | solution.py:101
  339.4 6.0 %collective-permute-start.26 = (bf16[160,256]{1,0:T(8,128)(2,1)S(1)}, bf16[160,256]{1,0:T(8,128)(2,1)S(1)}, u32[]{:S(2)}, u32[]{:S(2)}) collective-permute-start(bf16[160,256]{1,0:T(8,128)(2,1)S(1)} %get-tuple-element.128), channel_id=1, source_target_pairs={{0,6},{2,4},{4,2},{6,0},{1,7},{3,5},{5,3},{7,1},{8,14},{10,12},{12... | collective-permute-start | bytes 245768 | tf_op jit(solution)/shard_map/ppermute | solution.py:101
  345.4 2.0 collective-permute-start.27
  347.4 3.7 collective-permute-start.28
  351.1 5.3 %collective-permute-start.29 = (bf16[160,256]{1,0:T(8,128)(2,1)S(1)}, bf16[160,256]{1,0:T(8,128)(2,1)S(1)}, u32[]{:S(2)}, u32[]{:S(2)}) collective-permute-start(bf16[160,256]{1,0:T(8,128)(2,1)S(1)} %get-tuple-element.125), channel_id=1, source_target_pairs={{0,6},{2,4},{4,2},{6,0},{1,7},{3,5},{5,3},{7,1},{8,14},{10,12},{12... | collective-permute-start | bytes 245768 | tf_op jit(solution)/shard_map/ppermute | solution.py:101
  356.3 1.4 collective-permute-start.30
  357.8 4.4 %collective-permute-start.32 = (bf16[160,256]{1,0:T(8,128)(2,1)S(1)}, bf16[160,256]{1,0:T(8,128)(2,1)S(1)}, u32[]{:S(2)}, u32[]{:S(2)}) collective-permute-start(bf16[160,256]{1,0:T(8,128)(2,1)S(1)} %get-tuple-element.122), channel_id=1, source_target_pairs={{0,6},{2,4},{4,2},{6,0},{1,7},{3,5},{5,3},{7,1},{8,14},{10,12},{12... | collective-permute-start | bytes 245768 | tf_op jit(solution)/shard_map/ppermute | solution.py:101
  359.6 26.8 %collective-permute-start.33 = (bf16[160,256]{1,0:T(8,128)(2,1)S(1)}, bf16[160,256]{1,0:T(8,128)(2,1)S(1)}, u32[]{:S(2)}, u32[]{:S(2)}) collective-permute-start(bf16[160,256]{1,0:T(8,128)(2,1)S(1)} %get-tuple-element.121), channel_id=1, source_target_pairs={{0,2},{2,0},{4,6},{6,4},{1,3},{3,1},{5,7},{7,5},{8,10},{10,8},{12,... | collective-permute-start | bytes 245768 | tf_op jit(solution)/shard_map/ppermute | solution.py:101
  362.2 16.1 %copy-start.7 = (bf16[640,512]{1,0:T(8,128)(2,1)}, bf16[640,512]{1,0:T(8,128)(2,1)S(1)}, u32[]{:S(2)}) copy-start(bf16[640,512]{1,0:T(8,128)(2,1)S(1)} %collective-permute-done.36.refs_3_) | copy-start | bytes 1966084
  386.0 5.3 %collective-permute-start.37 = (bf16[160,512]{1,0:T(8,128)(2,1)S(1)}, bf16[160,512]{1,0:T(8,128)(2,1)S(1)}, u32[]{:S(2)}, u32[]{:S(2)}) collective-permute-start(bf16[160,512]{1,0:T(8,128)(2,1)S(1)} %get-tuple-element.114), channel_id=1, source_target_pairs={{0,4},{2,6},{4,0},{6,2},{1,5},{3,7},{5,1},{7,3},{8,12},{10,14},{12... | collective-permute-start | bytes 491528 | tf_op jit(solution)/shard_map/ppermute | solution.py:101
  386.5 9.0 %collective-permute-start.38 = (bf16[160,512]{1,0:T(8,128)(2,1)S(1)}, bf16[160,512]{1,0:T(8,128)(2,1)S(1)}, u32[]{:S(2)}, u32[]{:S(2)}) collective-permute-start(bf16[160,512]{1,0:T(8,128)(2,1)S(1)} %get-tuple-element.113), channel_id=1, source_target_pairs={{0,6},{2,4},{4,2},{6,0},{1,7},{3,5},{5,3},{7,1},{8,14},{10,12},{12... | collective-permute-start | bytes 491528 | tf_op jit(solution)/shard_map/ppermute | solution.py:101
  389.1 6.4 %collective-permute-start.39 = (bf16[160,512]{1,0:T(8,128)(2,1)S(1)}, bf16[160,512]{1,0:T(8,128)(2,1)S(1)}, u32[]{:S(2)}, u32[]{:S(2)}) collective-permute-start(bf16[160,512]{1,0:T(8,128)(2,1)S(1)} %get-tuple-element.112), channel_id=1, source_target_pairs={{0,2},{2,0},{4,6},{6,4},{1,3},{3,1},{5,7},{7,5},{8,10},{10,8},{12,... | collective-permute-start | bytes 491528 | tf_op jit(solution)/shard_map/ppermute | solution.py:101
  (12 other events, 28.7 us)
Sparse Core Ops, SparseCore 0:
  90.7 15.3 all-gather.7
  134.3 28.1 all-gather.5

commit v2 on v0

v2 whole, which is shorter than its diff:
```python
import jax
import jax.numpy as jnp
from jax import lax
from jax.experimental import pallas as pl
from jax.experimental.pallas import tpu as pltpu
from jax.sharding import PartitionSpec as P

prior_weight = 0.05
VMEM = 56 * 1024 * 1024
BOTH = ("ckpt", "tok")


def call(kernel, name, **options):
    return pl.pallas_call(
        kernel, name=name, compiler_params=pltpu.CompilerParams(vmem_limit_bytes=VMEM), **options
    )


def pack_kernel(*refs):
    parts, (wide_ref, narrow_ref) = refs[:-2], refs[-2:]
    peers, _, _, wide = wide_ref.shape
    narrow = narrow_ref.shape[2] // len(parts)
    split = peers * wide
    for g in range(peers):
        for q, part in enumerate(parts):
            wide_ref[g, q] = part[:, g * wide : (g + 1) * wide]
        lo = split + g * narrow
        narrow_ref[g] = jnp.concatenate([part[:, lo : lo + narrow] for part in parts], axis=1)


def pack(rows, peers, wide, narrow, fold):
    depth, columns = rows.shape
    height = depth // fold
    tall = 32
    steps = height // tall

    def part(q):
        return pl.BlockSpec((tall, columns), lambda i: (q * steps + i, 0))

    wide_out, narrow_out = call(
        pack_kernel, "pack",
        out_shape=(
            jax.ShapeDtypeStruct((peers, fold, height, wide), rows.dtype),
            jax.ShapeDtypeStruct((peers, height, fold * narrow), rows.dtype),
        ),
        grid=(steps,),
        in_specs=[part(q) for q in range(fold)],
        out_specs=(
            pl.BlockSpec((peers, fold, tall, wide), lambda i: (0, 0, i, 0)),
            pl.BlockSpec((peers, tall, fold * narrow), lambda i: (0, i, 0)),
        ),
    )(*([rows] * fold))
    return wide_out.reshape(peers, depth, wide), narrow_out


def copy_kernel(in_ref, out_ref):
    out_ref[...] = in_ref[...]


def staged(x):
    block = pl.BlockSpec((1, *x.shape[1:]), lambda i: (i, 0, 0))
    return call(
        copy_kernel, "staged",
        out_shape=jax.ShapeDtypeStruct(x.shape, x.dtype),
        grid=(x.shape[0],),
        in_specs=[block],
        out_specs=block,
        cost_estimate=pl.CostEstimate(flops=5 * 10**10, bytes_accessed=2 * x.size * 2, transcendentals=0),
    )(x)


def square_kernel(states_ref, *refs):
    out_ref, sum_ref = refs[-2:]
    x = states_ref[...].reshape(-1, states_ref.shape[3]).astype(jnp.float32)
    turned = jnp.square(x).astype(jnp.bfloat16).T
    out_ref[0] = turned
    sum_ref[0] = jnp.sum(turned.astype(jnp.float32), axis=0, keepdims=True)


def squares(states, so_far, step, steps):
    groups, ckpts, size, features = states.shape
    tokens = groups * size
    tile = features // steps
    return call(
        square_kernel, "squares",
        out_shape=(
            jax.ShapeDtypeStruct((ckpts, features, tokens), jnp.bfloat16),
            jax.ShapeDtypeStruct((ckpts, 1, tokens), jnp.float32),
        ),
        grid=(ckpts,),
        in_specs=[pl.BlockSpec((groups, 1, size, tile), lambda c: (0, c, 0, step))]
        + [pl.BlockSpec(memory_space=pl.ANY)] * len(so_far),
        out_specs=(
            pl.BlockSpec((1, tile, tokens), lambda c: (c, step, 0)),
            pl.BlockSpec((1, 1, tokens), lambda c: (c, 0, 0)),
        ),
        input_output_aliases={1: 0} if so_far else {},
    )(states, *so_far)


def unfolded(block, fold):
    w = block.shape[1] // fold
    return jnp.concatenate([block[:, q * w : (q + 1) * w] for q in range(fold)], axis=0)


def score_kernel(states_ref, wide_ref, narrow_ref, labels_ref, ids_ref, wide_out, narrow_out, stats_ref):
    states = states_ref[...].reshape(-1, states_ref.shape[3])
    blocks, height, folded = narrow_ref.shape[1:]
    narrow = narrow_out.shape[2]
    heads = jnp.concatenate([unfolded(narrow_ref[0, b], folded // narrow) for b in range(blocks)], axis=0)
    parts = (
        jnp.dot(states, wide_ref[0], preferred_element_type=jnp.float32),
        jnp.dot(states, heads, preferred_element_type=jnp.float32),
    )
    wide_out[0], narrow_out[0] = parts
    wide = wide_out.shape[2]
    top = jnp.maximum(*[jnp.max(x, axis=1, keepdims=True) for x in parts])
    mass = square = hit = 0.0
    for x, columns in zip(parts, (ids_ref[:, :wide], ids_ref[:, wide:])):
        grown = jnp.exp(x - top)
        target = labels_ref[...] == columns
        mass += jnp.sum(grown, axis=1, keepdims=True)
        hit += jnp.sum(jnp.where(target, grown, 0.0), axis=1, keepdims=True)
        square += jnp.sum(jnp.where(target, 0.0, grown * grown), axis=1, keepdims=True)
    lane = lax.broadcasted_iota(jnp.int32, (top.shape[0], 128), 1)
    table = jnp.where(lane == 0, top, jnp.where(lane == 1, mass, jnp.where(lane == 2, square, hit)))
    stats_ref[0] = table.T[:8]


def score(states, wide, narrow, narrow_width, labels, ids):
    groups, ckpts, size, features = states.shape
    tokens = groups * size
    return call(
        score_kernel, "score",
        out_shape=(
            jax.ShapeDtypeStruct((ckpts, tokens, wide.shape[2]), jnp.float32),
            jax.ShapeDtypeStruct((ckpts, tokens, narrow_width), jnp.float32),
            jax.ShapeDtypeStruct((ckpts, 8, tokens), jnp.float32),
        ),
        grid=(ckpts,),
        in_specs=[
            pl.BlockSpec((groups, 1, size, features), lambda c: (0, c, 0, 0)),
            pl.BlockSpec((1, *wide.shape[1:]), lambda c: (c, 0, 0)),
            pl.BlockSpec((1, *narrow.shape[1:]), lambda c: (c, 0, 0, 0)),
            pl.BlockSpec(labels.shape, lambda c: (0, 0)),
            pl.BlockSpec(ids.shape, lambda c: (0, 0)),
        ],
        out_specs=(
            pl.BlockSpec((1, tokens, wide.shape[2]), lambda c: (c, 0, 0)),
            pl.BlockSpec((1, tokens, narrow_width), lambda c: (c, 0, 0)),
            pl.BlockSpec((1, 8, tokens), lambda c: (c, 0, 0)),
        ),
    )(states, wide, narrow, labels, ids)


def merge_kernel(
    scale_ref, wide_logits, narrow_logits, table_ref, labels_ref, ids_ref, hidden_ref, wide_ref, narrow_ref,
    out_ref, wide_resid, narrow_resid,
):
    ckpts, _, wide = wide_logits.shape
    narrow = narrow_logits.shape[2]
    fold = narrow_ref.shape[3] // narrow

    @pl.when(pl.program_id(0) == 0)
    def _():
        target = jnp.where(labels_ref[...] == ids_ref[...], 1.0, 0.0)
        for c in range(ckpts):
            top, total = table_ref[:, c : c + 1], table_ref[:, ckpts + c : ckpts + c + 1]
            for logits, resid, hot in (
                (wide_logits, wide_resid, target[:, :wide]), (narrow_logits, narrow_resid, target[:, wide:])
            ):
                share = jnp.exp(logits[c] - top) / total
                resid[c] = jnp.square(share - hot).astype(jnp.bfloat16)

    def blend(resid, heads_of):
        numer = denom = None
        for c in range(ckpts):
            product = jnp.dot(hidden_ref[c], resid[c], preferred_element_type=jnp.float32)
            scaled = (product * scale_ref[ckpts]) * scale_ref[c]
            weight = (scaled + prior_weight).astype(jnp.bfloat16).astype(jnp.float32)
            term = weight * heads_of(c).astype(jnp.float32)
            numer = term if numer is None else numer + term
            denom = weight if denom is None else denom + weight
        return numer / denom

    peers, own = out_ref.shape[0], wide_ref.shape[2] // out_ref.shape[0]
    merged = blend(wide_resid, lambda c: wide_ref[c, 0])
    out_ref[:, :own] = merged.astype(out_ref.dtype).reshape(peers, own, wide)
    merged = blend(narrow_resid, lambda c: unfolded(narrow_ref[c, 0], fold))
    height = own // fold
    for peer in range(peers):
        pieces = [merged[peer * own + q * height : peer * own + (q + 1) * height] for q in range(fold)]
        block = jnp.concatenate(pieces, axis=1)
        rest = jnp.zeros((out_ref.shape[1] - own - height, block.shape[1]), jnp.float32)
        out_ref[peer, own:] = jnp.concatenate([block, rest], axis=0).astype(out_ref.dtype)


def merge(scales, wide_logits, narrow_logits, table, labels, ids, hidden_sq, wide, narrow, ntok):
    ckpts, blocks, depth, width = wide.shape
    tokens, slim = narrow_logits.shape[1:]
    own = depth // ntok
    tall = own + -(-own * slim // width // 16) * 16

    def whole(x):
        return pl.BlockSpec(x.shape, lambda i: (0,) * x.ndim)

    return call(
        merge_kernel, "merge",
        out_shape=jax.ShapeDtypeStruct((blocks * ntok, tall, width), jnp.bfloat16),
        grid=(blocks,),
        in_specs=[pl.BlockSpec(memory_space=pltpu.SMEM)]
        + [whole(x) for x in (wide_logits, narrow_logits, table, labels, ids)]
        + [
            pl.BlockSpec((ckpts, depth, tokens), lambda i: (0, i, 0)),
            pl.BlockSpec((ckpts, 1, depth, width), lambda i: (0, i, 0, 0)),
            pl.BlockSpec((ckpts, 1, *narrow.shape[2:]), lambda i: (0, i, 0, 0)),
        ],
        out_specs=pl.BlockSpec((ntok, tall, width), lambda i: (i, 0, 0)),
        scratch_shapes=[
            pltpu.VMEM((ckpts, tokens, width), jnp.bfloat16), pltpu.VMEM((ckpts, tokens, slim), jnp.bfloat16)
        ],
    )(scales, wide_logits, narrow_logits, table, labels, ids, hidden_sq, wide, narrow)


def after(value, *earlier):
    return lax.optimization_barrier((value, *earlier))[0] if earlier else value


def exchange(x):
    return lax.all_to_all(x, BOTH, 0, 0, tiled=True)


def combined(x, y):
    top = jnp.maximum(x[0], y[0])
    fx, fy = jnp.exp(x[0] - top), jnp.exp(y[0] - top)
    return jnp.stack(
        [top, x[1] * fx + y[1] * fy, x[2] * (fx * fx) + y[2] * (fy * fy), x[3] * fx + y[3] * fy]
    )


def everywhere(stats, beside):
    for axis in ("tok", "vocab", "ckpt"):
        size, far = lax.axis_size(axis), 1
        while far < size:
            other = lax.ppermute(stats, axis, [(i, i ^ far) for i in range(size)])
            stats, far = combined(stats, other), far * 2
            if beside:
                stats = after(stats, beside.pop(0))
    return stats


def shards(heads, hidden, targets):
    ntok, nckpt, nvocab = (lax.axis_size(a) for a in ("tok", "ckpt", "vocab"))
    peers = nckpt * ntok
    mine = lax.axis_index("ckpt") * ntok + lax.axis_index("tok")
    rows = heads[0]
    depth, columns = rows.shape
    share = columns // peers
    wide = share // 128 * 128
    narrow = share - wide
    split = peers * wide
    per_device, features = hidden.shape[1:]
    tokens = per_device * ntok
    ckpts = nckpt
    fold = 4

    size = per_device // nvocab
    own = lax.dynamic_slice_in_dim(hidden[0], lax.axis_index("vocab") * size, size, 0)
    along = lax.all_gather(own, "ckpt", axis=0)

    wide_block, narrow_block = pack(rows, peers, wide, narrow, fold)
    narrow_in = exchange(narrow_block)
    states = lax.all_gather(after(staged(along), narrow_in), ("tok", "vocab"), axis=0)
    if size % 16:
        states = states.transpose(1, 0, 2, 3).reshape(1, ckpts, tokens, features)
    wide_in = exchange(after(wide_block, narrow_in))
    labels = lax.all_gather(after(targets, narrow_in), "tok", axis=0, tiled=True)[:, None]
    narrow_in = narrow_in.reshape(ckpts, ntok, depth // fold, fold * narrow)

    base = lax.axis_index("vocab") * columns
    ids = jnp.concatenate(
        [base + mine * wide + jnp.arange(wide), base + split + mine * narrow + jnp.arange(narrow)]
    ).astype(jnp.int32)[None]
    wide_logits, narrow_logits, stats = score(
        states, wide_in.reshape(ckpts, ntok * depth, wide), narrow_in, narrow, labels, ids
    )
    hidden_sq, hidden_rows, pieces = (), [], []
    for step in range(4):
        whole, part = squares(after(states, stats), hidden_sq, step, 4)
        hidden_sq = (whole,)
        hidden_rows.append(part)
        pieces.append(part)
    hidden_sq, hidden_rows = hidden_sq[0], sum(hidden_rows)
    top, total, squared, hit = everywhere(stats[:, :4].transpose(1, 0, 2), pieces)
    resid_rows = squared / (total * total) + jnp.square(hit / total - 1.0)
    vocab_total = columns * nvocab
    count = float(tokens * features * vocab_total)
    level = jnp.sum(hidden_rows[:, 0] * resid_rows, axis=1) / jnp.float32(count)
    scales = jnp.concatenate([1.0 / level, jnp.full((1,), vocab_total / tokens, jnp.float32)])
    table = jnp.concatenate([top, total]).T

    out = exchange(
        merge(
            scales, wide_logits, narrow_logits, table, labels, ids, hidden_sq,
            wide_in.reshape(ckpts, ntok, depth, wide), narrow_in, ntok,
        )
    )
    own_rows = depth // ntok
    height = own_rows // fold
    narrow_out = out[:, own_rows : own_rows + height].reshape(peers, height, fold, narrow).transpose(2, 1, 0, 3)
    return jnp.concatenate(
        [out[:, :own_rows].transpose(1, 0, 2).reshape(own_rows, -1), narrow_out.reshape(own_rows, -1)], axis=1
    )


def solution(mesh):
    placed = (P("ckpt", "tok", "vocab"), P("ckpt", "tok", None), P("tok"))
    return jax.shard_map(
        shards, mesh=mesh, in_specs=placed, out_specs=P(("ckpt", "tok"), "vocab"), check_vma=False
    )
```

time: 671 us -> 302 us (0.45)
  waiting for transfers between devices: 445 us -> 117 us
  blocking collectives: 151 us -> 86 us
  Pallas kernels: 0 us -> 53.4 us
  matrix products: 24.3 us -> 0 us
  local copies, waits for them, and re-layouts: 20.3 us -> 7.32 us
  starting transfers between devices: 6.14 us -> 18.9 us
    reduce_scatter x2 -> x0, waiting for transfers between devices: 443 us -> none  [the longest x1 224 us: shards(): lax.psum_scatter(weight_wide, 'ckpt', scatter_dimension=0, tiled=True)]
    all_to_all x1 -> x2, waiting for transfers between devices: 0.01 us -> 76.2 us  [exchange(): return lax.all_to_all(x, BOTH, 0, 0, tiled=True)]
    pallas_call x0 -> x8, Pallas kernels: none -> 53.4 us  [the longest x4 17.7 us: squares(): call(square_kernel, 'squares', out_shape=(jax.ShapeDtypeStruct((ckpts, fe...]
    all_gather x1, blocking collectives: 87.4 us -> 39 us  [shards(): lax.all_gather(after(targets, narrow_in), 'tok', axis=0, tiled=True)]
    all_gather x1 -> x2, waiting for transfers between devices: 0.01 us -> 39.3 us  [the longest x1 39.3 us: shards(): along = lax.all_gather(own, 'ckpt', axis=0)]
    psum x2 -> x0, blocking collectives: 26.7 us -> none  [the longest x1 14.1 us: shards(): level = lax.psum(partial_value, ('tok', 'vocab')) / jnp.float32(count)]
    dot_general x2 -> x0, matrix products: 24.3 us -> none  [the longest x1 17 us: shards(): lax.dot_general(hidden_sq, resid_sq, (((0,), (0,)), ((), ())), preferred_...]
    all_to_all x1, blocking collectives: 23.2 us -> 47.1 us  [exchange(): return lax.all_to_all(x, BOTH, 0, 0, tiled=True)]
  transfers between devices with their start and end apart: 4 -> 9, of which waited for: 2 -> 4; matrix products, arithmetic and copies ran while one was open for 0% -> 1% of each run, Pallas kernels for 0% -> 10%
where the time goes in v2:
time: 302 us; the launch traced here: 299 us
  waiting for transfers between devices  117 us (39%)
  blocking collectives  86 us (28%)
  Pallas kernels  53.4 us (18%)
  starting transfers between devices  18.9 us (6%)
  between operations  13.6 us (5%)
  local copies, waits for them, and re-layouts  7.32 us (2%)
    all_to_all x2, waiting for transfers between devices, exchange(): return lax.all_to_all(x, BOTH, 0, 0, tiled=True)  76.2 us
    all_to_all x1, blocking collectives, exchange(): return lax.all_to_all(x, BOTH, 0, 0, tiled=True)  47.1 us
    all_gather x1, waiting for transfers between devices, shards(): along = lax.all_gather(own, 'ckpt', axis=0)  39.3 us
    all_gather x1, blocking collectives, shards(): lax.all_gather(after(targets, narrow_in), 'tok', axis=0, tiled=True)  39 us
    pallas_call x4, Pallas kernels, squares(): call(square_kernel, 'squares', out_shape=(jax.ShapeDtypeStruct((ckpts, fe...  17.7 us
    pallas_call x1, Pallas kernels, merge(): call(merge_kernel, 'merge', out_shape=jax.ShapeDtypeStruct((blocks * ntok...  13.2 us
    all_to_all x2, starting transfers between devices, exchange(): return lax.all_to_all(x, BOTH, 0, 0, tiled=True)  12 us
    pallas_call x1, Pallas kernels, score(): call(score_kernel, 'score', out_shape=(jax.ShapeDtypeStruct((ckpts, token...  11.4 us
  transfers between devices with their start and end apart: 9, of which 4 were waited for; matrix products, arithmetic and copies ran while one was open for 1% of the time, Pallas kernels for 10%

profile of v2, /device:TPU:9, one launch (start us, length us, event | category | flops | bytes accessed | tf_op | source)
XLA Modules:
  0.0 299.2 jit_solution(9548799147688199132)
XLA Ops:
  6.5 0.0 copy-start
  6.5 1.1 copy-done
  7.6 0.7 constant_dynamic-slice_fusion
  8.4 0.0 all-gather.5.cloned.1.call-update
  8.4 7.6 %pack.1 = (bf16[16,4,160,256]{3,2,1,0:T(8,128)(2,1)}, bf16[16,160,256]{2,1,0:T(8,128)(2,1)}) custom-call(bf16[640,5120]{1,0:T(8,128)(2,1)} %bitcast.94, bf16[640,5120]{1,0:T(8,128)(2,1)} %bitcast.95, bf16[640,5120]{1,0:T(8,128)(2,1)} %bitcast.96, bf16[640,5120]{1,0:T(8,128)(2,1)} %bitcast.97), custom_call_target="tpu_custom_call" | custom-call | tf_op jit(solution)/shard_map/pack/pallas_call | solution.py:40
  16.0 6.6 %all-to-all-start = ((bf16[16,160,256]{2,1,0:T(8,128)(2,1)}), bf16[16,160,256]{2,1,0:T(8,128)(2,1)S(1)}, u32[]{:S(2)}, u32[]{:S(2)}) async-start(bf16[16,160,256]{2,1,0:T(8,128)(2,1)} %get-tuple-element.26), calls=%async_computation | async-start | bytes 2621440 | tf_op jit(solution)/shard_map/all_to_all | solution.py:230
  22.5 0.0 all-gather.7.cloned.1.call-start
  22.6 39.3 %all-gather.5.cloned.1.call-done.in_ref = bf16[4,64,2560]{2,1,0:T(8,128)(2,1)} async-done(((bf16[1,64,2560]{2,1,0:T(8,128)(2,1)}), bf16[4,64,2560]{2,1,0:T(8,128)(2,1)}) %all-gather.5.cloned.1.call-update) | async-done | bytes 1310736 | tf_op jit(solution)/shard_map/all_gather | solution.py:269
  61.9 3.5 %staged.1 = bf16[4,64,2560]{2,1,0:T(8,128)(2,1)} custom-call(bf16[4,64,2560]{2,1,0:T(8,128)(2,1)} %all-gather.5.cloned.1.call-done.in_ref), custom_call_target="tpu_custom_call" | custom-call | flops 49999998976 | bytes 2621440 | tf_op jit(solution)/shard_map/staged/pallas_call | solution.py:62
  65.3 3.8 %all-to-all-done = bf16[16,160,256]{2,1,0:T(8,128)(2,1)S(1)} async-done(((bf16[16,160,256]{2,1,0:T(8,128)(2,1)}), bf16[16,160,256]{2,1,0:T(8,128)(2,1)S(1)}, u32[]{:S(2)}, u32[]{:S(2)}) %all-to-all-start) | async-done | bytes 1310752 | tf_op jit(solution)/shard_map/all_to_all | solution.py:230
  69.1 0.0 all-gather.7.cloned.1.call-update
  69.1 0.0 copy-start.5
  69.2 1.1 copy-done.1
  70.2 5.4 %all-to-all-start.1 = ((bf16[16,640,256]{2,1,0:T(8,128)(2,1)}), bf16[16,640,256]{2,1,0:T(8,128)(2,1)}, u32[]{:S(2)}, u32[]{:S(2)}) async-start(bf16[16,640,256]{2,1,0:T(8,128)(2,1)} %bitcast.101), calls=%async_computation.1 | async-start | bytes 10485760 | tf_op jit(solution)/shard_map/all_to_all | solution.py:230
  75.7 0.6 broadcast_in_dim.7.ids_ref
  76.2 0.0 copy-done.5
  76.3 39.0 %all-gather.1 = s32[4,1,128]{2,1,0:T(1,128)S(1)} all-gather(s32[1,1,128]{2,1,0:T(1,128)S(1)} %bitcast.105), channel_id=1, replica_groups=mesh['ckpt'=4,'tok'=4,'vocab'=2] {'tok'}, dimensions={0}, use_global_device_ids=true | all-gather | bytes 2560 | tf_op jit(solution)/shard_map/all_gather | solution.py:277
  115.2 0.9 copy.36.labels_ref
  116.1 72.5 %all-to-all-done.1 = bf16[16,640,256]{2,1,0:T(8,128)(2,1)} async-done(((bf16[16,640,256]{2,1,0:T(8,128)(2,1)}), bf16[16,640,256]{2,1,0:T(8,128)(2,1)}, u32[]{:S(2)}, u32[]{:S(2)}) %all-to-all-start.1) | async-done | bytes 5242912 | tf_op jit(solution)/shard_map/all_to_all | solution.py:230
  188.5 11.4 %score.1 = (f32[4,512,256]{2,1,0:T(8,128)}, f32[4,512,64]{2,1,0:T(8,128)}, f32[4,8,512]{2,1,0:T(8,128)}) custom-call(bf16[8,4,64,2560]{3,2,1,0:T(8,128)(2,1)} %bitcast.89, bf16[4,2560,256]{2,1,0:T(8,128)(2,1)} %bitcast.3.wide_ref, bf16[4,4,160,256]{3,2,1,0:T(8,128)(2,1)} %bitcast.98, s32[512,1]{1,0:T(8,128)} %copy.36.labels_ref, ...), custom_call_target="tpu_custom_call" | custom-call | tf_op jit(solution)/shard_map/score/pallas_call | solution.py:133
  199.9 0.8 slice_bitcast_fusion.1
  200.8 1.0 collective-permute-start
  201.7 4.4 %squares.4 = (bf16[4,2560,512]{2,1,0:T(8,128)(2,1)}, f32[4,1,512]{2,1,0:T(1,128)}) custom-call(bf16[8,4,64,2560]{3,2,1,0:T(8,128)(2,1)} %bitcast.90), custom_call_target="tpu_custom_call" | custom-call | tf_op jit(solution)/shard_map/squares/pallas_call | solution.py:84
  206.2 0.0 collective-permute-done
  206.2 0.1 slice_maximum_fusion.3
  206.3 2.7 collective-permute-start.1
  209.0 4.4 %squares.5 = (bf16[4,2560,512]{2,1,0:T(8,128)(2,1)}, f32[4,1,512]{2,1,0:T(1,128)}) custom-call(bf16[8,4,64,2560]{3,2,1,0:T(8,128)(2,1)} %bitcast.91, bf16[4,2560,512]{2,1,0:T(8,128)(2,1)} %get-tuple-element.34.refs_0_), custom_call_target="tpu_custom_call", output_to_operand_aliasing={{0}: (1, {})} | custom-call | tf_op jit(solution)/shard_map/squares/pallas_call | solution.py:84
  213.4 0.0 collective-permute-done.1
  213.5 1.5 collective-permute-start.2
  215.0 4.4 %squares.6 = (bf16[4,2560,512]{2,1,0:T(8,128)(2,1)}, f32[4,1,512]{2,1,0:T(1,128)}) custom-call(bf16[8,4,64,2560]{3,2,1,0:T(8,128)(2,1)} %bitcast.92, bf16[4,2560,512]{2,1,0:T(8,128)(2,1)} %get-tuple-element.36.refs_0_), custom_call_target="tpu_custom_call", output_to_operand_aliasing={{0}: (1, {})} | custom-call | tf_op jit(solution)/shard_map/squares/pallas_call | solution.py:84
  219.4 0.0 collective-permute-done.2
  219.5 0.1 collective-permute-start.3
  219.6 4.5 %squares.7 = (bf16[4,2560,512]{2,1,0:T(8,128)(2,1)}, f32[4,1,512]{2,1,0:T(1,128)}) custom-call(bf16[8,4,64,2560]{3,2,1,0:T(8,128)(2,1)} %bitcast.93, bf16[4,2560,512]{2,1,0:T(8,128)(2,1)} %get-tuple-element.38.refs_0_), custom_call_target="tpu_custom_call", output_to_operand_aliasing={{0}: (1, {})} | custom-call | tf_op jit(solution)/shard_map/squares/pallas_call | solution.py:84
  224.1 0.0 collective-permute-done.3
  224.1 1.6 collective-permute-start.4
  225.7 0.7 add_add_fusion
  226.4 1.4 collective-permute-done.4
  227.9 0.1 fusion.20
  228.0 0.8 copy.46
  228.9 0.6 pad_maximum_fusion.6.scale_ref
  229.5 13.2 %merge.1 = bf16[16,208,256]{2,1,0:T(8,128)(2,1)} custom-call(f32[5]{0:T(128)} %pad_maximum_fusion.6.scale_ref, f32[4,512,256]{2,1,0:T(8,128)} %get-tuple-element.44.wide_logits, f32[4,512,64]{2,1,0:T(8,128)} %get-tuple-element.45.narrow_logits, f32[512,8]{1,0:T(8,128)} %bitcast.103, s32[512,1]{1,0:T(8,128)} %copy.36.labels_ref, ...), custom_call_target="tpu_custom_call" | custom-call | tf_op jit(solution)/shard_map/merge/pallas_call | solution.py:207
  242.7 47.1 %all_to_all.15 = bf16[16,208,256]{2,1,0:T(8,128)(2,1)S(1)} all-to-all(bf16[16,208,256]{2,1,0:T(8,128)(2,1)} %merge.1), channel_id=1, replica_groups=mesh['ckpt'=4,'tok'=4,'vocab'=2] {'ckpt','tok'}, dimensions={0} | all-to-all | bytes 3407872 | tf_op jit(solution)/shard_map/all_to_all | solution.py:230
  289.7 0.1 slice_bitcast_fusion
  289.9 0.1 copy.55
  290.0 0.3 reshape.28
  290.3 0.3 copy.49
  290.6 0.4 reshape.29
  291.0 1.3 pad_maximum_fusion
  (31 shorter events, 0.2 us)
Async XLA Ops:
  6.5 1.1 copy-start
  6.5 55.3 %all-gather.5.cloned.1.call-start = ((), (), s32[]{:S(2)}) async-start(), calls=%async_computation.3 | async-start | bytes 1638400 | tf_op jit(solution)/shard_map/all_gather | solution.py:269
  16.0 53.1 %all-to-all-start = ((bf16[16,160,256]{2,1,0:T(8,128)(2,1)}), bf16[16,160,256]{2,1,0:T(8,128)(2,1)S(1)}, u32[]{:S(2)}, u32[]{:S(2)}) async-start(bf16[16,160,256]{2,1,0:T(8,128)(2,1)} %get-tuple-element.26), calls=%async_computation | async-start | bytes 2621440 | tf_op jit(solution)/shard_map/all_to_all | solution.py:230
  22.5 166.0 %all-gather.7.cloned.1.call-start = ((), (), s32[]{:S(2)}) async-start(), calls=%async_computation.4 | async-start | bytes 11796480 | tf_op jit(solution)/shard_map/all_gather | solution.py:273
  69.1 1.1 copy-start.1
  69.1 7.1 %copy-start.5 = (s32[128]{0:T(128)S(1)}, s32[128]{0:T(128)}, u32[]{:S(2)}) copy-start(s32[128]{0:T(128)} %param.5) | copy-start | bytes 1540
  70.2 118.3 %all-to-all-start.1 = ((bf16[16,640,256]{2,1,0:T(8,128)(2,1)}), bf16[16,640,256]{2,1,0:T(8,128)(2,1)}, u32[]{:S(2)}, u32[]{:S(2)}) async-start(bf16[16,640,256]{2,1,0:T(8,128)(2,1)} %bitcast.101), calls=%async_computation.1 | async-start | bytes 10485760 | tf_op jit(solution)/shard_map/all_to_all | solution.py:230
  200.8 5.4 %collective-permute-start = (f32[4,4,512]{2,1,0:T(4,128)S(1)}, f32[4,4,512]{2,1,0:T(4,128)S(1)}, u32[]{:S(2)}, u32[]{:S(2)}) collective-permute-start(f32[4,4,512]{2,1,0:T(4,128)S(1)} %copy.37), channel_id=1, source_target_pairs={{0,2},{2,0},{4,6},{6,4},{1,3},{3,1},{5,7},{7,5},{8,10},{10,8},{12,... | collective-permute-start | bytes 98312 | tf_op jit(solution)/shard_map/ppermute | solution.py:245
  206.3 7.1 %collective-permute-start.1 = (f32[4,4,512]{2,1,0:T(4,128)S(1)}, f32[4,4,512]{2,1,0:T(4,128)S(1)}, u32[]{:S(2)}, u32[]{:S(2)}) collective-permute-start(f32[4,4,512]{2,1,0:T(4,128)S(1)} %pad_maximum_fusion.1), channel_id=1, source_target_pairs={{0,4},{2,6},{4,0},{6,2},{1,5},{3,7},{5,1},{7,3},{8,12},{10,14},{12... | collective-permute-start | bytes 98312 | tf_op jit(solution)/shard_map/ppermute | solution.py:245
  213.5 5.9 %collective-permute-start.2 = (f32[4,4,512]{2,1,0:T(4,128)S(1)}, f32[4,4,512]{2,1,0:T(4,128)S(1)}, u32[]{:S(2)}, u32[]{:S(2)}) collective-permute-start(f32[4,4,512]{2,1,0:T(4,128)S(1)} %pad_maximum_fusion.2), channel_id=1, source_target_pairs={{0,1},{1,0},{2,3},{3,2},{4,5},{5,4},{6,7},{7,6},{8,9},{9,8},{10,11... | collective-permute-start | bytes 98312 | tf_op jit(solution)/shard_map/ppermute | solution.py:245
  219.5 4.6 %collective-permute-start.3 = (f32[4,4,512]{2,1,0:T(4,128)S(1)}, f32[4,4,512]{2,1,0:T(4,128)S(1)}, u32[]{:S(2)}, u32[]{:S(2)}) collective-permute-start(f32[4,4,512]{2,1,0:T(4,128)S(1)} %pad_maximum_fusion.3), channel_id=1, source_target_pairs={{0,8},{8,0},{16,24},{24,16},{1,9},{9,1},{17,25},{25,17},{2,10},{10... | collective-permute-start | bytes 98312 | tf_op jit(solution)/shard_map/ppermute | solution.py:245
  219.6 6.2 %copy-start.2 = (f32[4,1,512]{2,1,0:T(1,128)S(1)}, f32[4,1,512]{2,1,0:T(1,128)}, u32[]{:S(2)}) copy-start(f32[4,1,512]{2,1,0:T(1,128)} %get-tuple-element.33) | copy-start | bytes 24580
  219.6 6.2 %copy-start.3 = (f32[4,1,512]{2,1,0:T(1,128)S(1)}, f32[4,1,512]{2,1,0:T(1,128)}, u32[]{:S(2)}) copy-start(f32[4,1,512]{2,1,0:T(1,128)} %get-tuple-element.35) | copy-start | bytes 24580
  219.6 6.1 %copy-start.4 = (f32[4,1,512]{2,1,0:T(1,128)S(1)}, f32[4,1,512]{2,1,0:T(1,128)}, u32[]{:S(2)}) copy-start(f32[4,1,512]{2,1,0:T(1,128)} %get-tuple-element.37) | copy-start | bytes 24580
  224.1 3.7 %collective-permute-start.4 = (f32[4,4,512]{2,1,0:T(4,128)S(1)}, f32[4,4,512]{2,1,0:T(4,128)S(1)}, u32[]{:S(2)}, u32[]{:S(2)}) collective-permute-start(f32[4,4,512]{2,1,0:T(4,128)S(1)} %pad_maximum_fusion.4), channel_id=1, source_target_pairs={{0,16},{8,24},{16,0},{24,8},{1,17},{9,25},{17,1},{25,9},{2,18},{10... | collective-permute-start | bytes 98312 | tf_op jit(solution)/shard_map/ppermute | solution.py:245
Sparse Core Ops, SparseCore 0:
  8.9 52.8 all-gather.4
  69.3 110.5 all-gather.6

commit v3 on v2

v3 whole, which is shorter than its diff:
```python
import functools
import math

import jax
import jax.numpy as jnp
from jax import lax
from jax.experimental import pallas as pl
from jax.experimental.pallas import tpu as pltpu
from jax.sharding import PartitionSpec as P

prior_weight = 0.05
VMEM = 56 * 1024 * 1024
BOTH = ("ckpt", "tok")


def call(kernel, name, **options):
    return pl.pallas_call(
        kernel, name=name, compiler_params=pltpu.CompilerParams(vmem_limit_bytes=VMEM), **options
    )


def pack_kernel(*refs):
    parts, out_ref = refs[:-1], refs[-1]
    peers, blocks, _, wide = out_ref.shape
    fold = len(parts)
    narrow = wide // fold
    split = peers * wide
    for g in range(peers):
        for q, part in enumerate(parts):
            out_ref[g, q] = part[:, g * wide : (g + 1) * wide]
        lo = split + g * narrow
        out_ref[g, fold] = jnp.concatenate([part[:, lo : lo + narrow] for part in parts], axis=1)


def pack(rows, peers, wide, fold):
    depth, columns = rows.shape
    height = depth // fold
    tall = 32
    steps = height // tall

    def part(q):
        return pl.BlockSpec((tall, columns), lambda i: (q * steps + i, 0))

    out = call(
        pack_kernel, "pack",
        out_shape=jax.ShapeDtypeStruct((peers, fold + 1, height, wide), rows.dtype),
        grid=(steps,),
        in_specs=[part(q) for q in range(fold)],
        out_specs=pl.BlockSpec((peers, fold + 1, tall, wide), lambda i: (0, 0, i, 0)),
    )(*([rows] * fold))
    return out.reshape(peers, depth + height, wide)


def squared(x):
    return jnp.square(x.astype(jnp.float32)).astype(jnp.bfloat16)


def rows_kernel(states_ref, out_ref):
    x = squared(states_ref[...].reshape(-1, states_ref.shape[3]))
    ones = jnp.ones((8, x.shape[1]), jnp.bfloat16)
    out_ref[0] = lax.dot_general(ones, x, (((1,), (1,)), ((), ())), preferred_element_type=jnp.float32)


def row_sums(states, features):
    groups, ckpts, size, _ = states.shape
    return call(
        rows_kernel, "rows",
        out_shape=jax.ShapeDtypeStruct((ckpts, 8, groups * size), jnp.float32),
        grid=(ckpts,),
        in_specs=[pl.BlockSpec((groups, 1, size, features), lambda c: (0, c, 0, 0))],
        out_specs=pl.BlockSpec((1, 8, groups * size), lambda c: (c, 0, 0)),
    )(states)


def unfolded(block, fold):
    w = block.shape[1] // fold
    return jnp.concatenate([block[:, q * w : (q + 1) * w] for q in range(fold)], axis=0)


def padded(blocks, lanes):
    x = jnp.concatenate(blocks, axis=0)
    return jnp.concatenate([x, jnp.zeros((x.shape[0], lanes - x.shape[1]), x.dtype)], axis=1)


def score_kernel(states_ref, heads_ref, labels_ref, ids_ref, logits_ref, stats_ref):
    states = states_ref[...].reshape(-1, states_ref.shape[3])
    blocks, _, wide = heads_ref.shape[1:]
    depth = states.shape[1] // blocks
    slim = logits_ref.shape[2] - wide
    fold = wide // (slim // 2)
    narrow = padded([unfolded(heads_ref[0, b, depth:], fold) for b in range(blocks)], slim)
    heads = jnp.concatenate([heads_ref[0, b, :depth] for b in range(blocks)], axis=0)
    x = jnp.concatenate(
        [jnp.dot(states, y, preferred_element_type=jnp.float32) for y in (heads, narrow)], axis=1
    )
    x = jnp.where(ids_ref[...] >= 0, x, -3e38)
    logits_ref[0] = x
    top = jnp.max(x, axis=1, keepdims=True)
    grown = jnp.exp(x - top)
    target = labels_ref[...] == ids_ref[...]
    mass = jnp.sum(grown, axis=1, keepdims=True)
    hit = jnp.sum(jnp.where(target, grown, 0.0), axis=1, keepdims=True)
    square = jnp.sum(jnp.where(target, 0.0, grown * grown), axis=1, keepdims=True)
    lane = lax.broadcasted_iota(jnp.int32, (top.shape[0], 128), 1)
    table = jnp.where(lane == 0, top, jnp.where(lane == 1, mass, jnp.where(lane == 2, square, hit)))
    stats_ref[0] = table.T[:8]


def score(states, features, heads, labels, ids):
    groups, ckpts, size, _ = states.shape
    tokens, lanes = groups * size, ids.shape[1]
    return call(
        score_kernel, "score",
        out_shape=(
            jax.ShapeDtypeStruct((ckpts, tokens, lanes), jnp.float32),
            jax.ShapeDtypeStruct((ckpts, 8, tokens), jnp.float32),
        ),
        grid=(ckpts,),
        in_specs=[
            pl.BlockSpec((groups, 1, size, features), lambda c: (0, c, 0, 0)),
            pl.BlockSpec((1, *heads.shape[1:]), lambda c: (c, 0, 0, 0)),
            pl.BlockSpec(labels.shape, lambda c: (0, 0)),
            pl.BlockSpec(ids.shape, lambda c: (0, 0)),
        ],
        out_specs=(
            pl.BlockSpec((1, tokens, lanes), lambda c: (c, 0, 0)),
            pl.BlockSpec((1, 8, tokens), lambda c: (c, 0, 0)),
        ),
    )(states, heads, labels, ids)


def merge_kernel(
    scale_ref, logits_ref, table_ref, labels_ref, ids_ref, hidden_ref, heads_ref, out_ref, resid_ref,
    *, prior
):
    ckpts = logits_ref.shape[0]
    wide, depth = heads_ref.shape[3], hidden_ref.shape[3]
    slim = logits_ref.shape[2] - wide
    fold = wide // (slim // 2)

    @pl.when(pl.program_id(0) == 0)
    def _():
        target = jnp.where(labels_ref[...] == ids_ref[...], 1.0, 0.0)
        for c in range(ckpts):
            top, total = table_ref[:, c : c + 1], table_ref[:, ckpts + c : ckpts + c + 1]
            share = jnp.exp(logits_ref[c] - top) * (1.0 / total)
            resid_ref[c] = jnp.square(share - target).astype(jnp.bfloat16)

    hidden = [squared(hidden_ref[:, c].reshape(-1, hidden_ref.shape[3])) for c in range(ckpts)]

    def blend(lo, hi, heads_of):
        numer = denom = None
        for c in range(ckpts):
            product = lax.dot_general(
                hidden[c], resid_ref[c, :, lo:hi], (((0,), (0,)), ((), ())), preferred_element_type=jnp.float32
            )
            weight = (product * scale_ref[c] + prior).astype(jnp.bfloat16).astype(jnp.float32)
            term = weight * heads_of(c).astype(jnp.float32)
            numer = term if numer is None else numer + term
            denom = weight if denom is None else denom + weight
        return numer / denom

    peers, own = out_ref.shape[0], depth // out_ref.shape[0]
    merged = blend(0, wide, lambda c: heads_ref[c, 0, :depth])
    out_ref[:, :own] = merged.astype(out_ref.dtype).reshape(peers, own, wide)
    merged = blend(wide, wide + slim, lambda c: padded([unfolded(heads_ref[c, 0, depth:], fold)], slim))
    height = own // fold
    for peer in range(peers):
        pieces = [
            merged[peer * own + q * height : peer * own + (q + 1) * height, : slim // 2] for q in range(fold)
        ]
        block = jnp.concatenate(pieces, axis=1)
        rest = jnp.zeros((out_ref.shape[1] - own - height, block.shape[1]), jnp.float32)
        out_ref[peer, own:] = jnp.concatenate([block, rest], axis=0).astype(out_ref.dtype)


def merge(scales, prior, logits, table, labels, ids, states, heads, depth, ntok):
    ckpts, blocks, _, width = heads.shape
    tokens, lanes = logits.shape[1:]
    slim = (lanes - width) // 2
    own = depth // ntok
    tall = own + -(-own * slim // width // 16) * 16

    def whole(x):
        return pl.BlockSpec(x.shape, lambda i: (0,) * x.ndim)

    return call(
        functools.partial(merge_kernel, prior=prior), "merge",
        out_shape=jax.ShapeDtypeStruct((blocks * ntok, tall, width), jnp.bfloat16),
        grid=(blocks,),
        in_specs=[pl.BlockSpec(memory_space=pltpu.SMEM)]
        + [whole(x) for x in (logits, table, labels, ids)]
        + [
            pl.BlockSpec((*states.shape[:3], depth), lambda i: (0, 0, 0, i)),
            pl.BlockSpec((ckpts, 1, *heads.shape[2:]), lambda i: (0, i, 0, 0)),
        ],
        out_specs=pl.BlockSpec((ntok, tall, width), lambda i: (i, 0, 0)),
        scratch_shapes=[pltpu.VMEM((ckpts, tokens, lanes), jnp.bfloat16)],
    )(scales, logits, table, labels, ids, states, heads)


def after(value, *earlier):
    return lax.optimization_barrier((value, *earlier))[0] if earlier else value


def exchange(x):
    return lax.all_to_all(x, BOTH, 0, 0, tiled=True)


def combined(x, y):
    top = jnp.maximum(x[0], y[0])
    fx, fy = jnp.exp(x[0] - top), jnp.exp(y[0] - top)
    return jnp.stack(
        [top, x[1] * fx + y[1] * fy, x[2] * (fx * fx) + y[2] * (fy * fy), x[3] * fx + y[3] * fy]
    )


def everywhere(stats):
    for axis in ("tok", "vocab", "ckpt"):
        size, far = lax.axis_size(axis), 1
        while far < size:
            other = lax.ppermute(stats, axis, [(i, i ^ far) for i in range(size)])
            stats, far = combined(stats, other), far * 2
    return stats


def shards(heads, hidden, targets):
    ntok, nckpt, nvocab = (lax.axis_size(a) for a in ("tok", "ckpt", "vocab"))
    peers = nckpt * ntok
    mine = lax.axis_index("ckpt") * ntok + lax.axis_index("tok")
    rows = heads[0]
    depth, columns = rows.shape
    share = columns // peers
    wide = share // 128 * 128
    narrow = share - wide
    split = peers * wide
    per_device, features = hidden.shape[1:]
    tokens = per_device * ntok
    ckpts = nckpt
    fold = 4

    size = per_device // nvocab
    own = lax.dynamic_slice_in_dim(hidden[0], lax.axis_index("vocab") * size, size, 0)
    label = lax.dynamic_slice_in_dim(targets, lax.axis_index("vocab") * size, size, 0)[:, None]
    digits = jnp.concatenate([label % 256, label // 256 % 256, label // 65536], axis=1)
    digits = jnp.pad(digits.astype(hidden.dtype), ((0, 0), (0, 125)))
    own = jnp.concatenate([own, digits], axis=1)[None]

    def other(x, axis, far):
        return lax.ppermute(x, axis, [(i, i ^ far) for i in range(lax.axis_size(axis))])

    def paired(x, y, axis, far):
        upper = lax.axis_index(axis) // far % 2 == 1
        return jnp.concatenate([jnp.where(upper, y, x), jnp.where(upper, x, y)])

    planes = [own] + [other(own, "ckpt", far) for far in (2, 3, 1)]
    packed = pack(rows, peers, wide, fold)
    columns_in = exchange(packed).reshape(ckpts, ntok, depth + depth // fold, wide)
    states = paired(
        paired(planes[0], planes[3], "ckpt", 1), paired(planes[1], planes[2], "ckpt", 1), "ckpt", 2
    )[None]
    states = after(states, packed)
    chains = [states, other(states, "tok", 2)]
    for i in (0, 1):
        far = 1
        while far < nvocab:
            chains[i] = paired(chains[i], other(chains[i], "vocab", far), "vocab", far)
            far *= 2
    states = paired(*chains, "tok", 2)
    states = paired(states, other(states, "tok", 1), "tok", 1)
    labels = states[:, 0, :, features : features + 3].reshape(tokens, 3).astype(jnp.int32)
    labels = labels[:, :1] + 256 * labels[:, 1:2] + 65536 * labels[:, 2:]
    if size % 16:
        states = states.transpose(1, 0, 2, 3).reshape(1, ckpts, tokens, features + 128)

    base = lax.axis_index("vocab") * columns
    pad = jnp.full((narrow,), -1)
    ids = jnp.concatenate(
        [base + mine * wide + jnp.arange(wide), base + split + mine * narrow + jnp.arange(narrow), pad]
    ).astype(jnp.int32)[None]
    hidden_rows = row_sums(states, features)
    logits, stats = score(after(states, hidden_rows), features, columns_in, labels, ids)
    top, total, off, hit = everywhere(stats[:, :4].transpose(1, 0, 2))
    resid_rows = off / (total * total) + jnp.square(hit / total - 1.0)
    vocab_total = columns * nvocab
    count = float(tokens * features * vocab_total)
    level = jnp.sum(hidden_rows[:, 0] * resid_rows, axis=1) / jnp.float32(count)
    ratio = vocab_total / tokens
    shrink = 2.0 ** -math.ceil(math.log2(max(ratio, 1.0)))
    scales = jnp.float32(ratio * shrink) / level
    table = jnp.concatenate([top, total]).T

    out = exchange(
        merge(
            scales, prior_weight * shrink, logits, table, labels, ids, states,
            columns_in, depth, ntok,
        )
    )
    own_rows = depth // ntok
    height = own_rows // fold
    narrow_out = out[:, own_rows : own_rows + height].reshape(peers, height, fold, narrow).transpose(2, 1, 0, 3)
    return jnp.concatenate(
        [out[:, :own_rows].transpose(1, 0, 2).reshape(own_rows, -1), narrow_out.reshape(own_rows, -1)], axis=1
    )


def solution(mesh):
    placed = (P("ckpt", "tok", "vocab"), P("ckpt", "tok", None), P("tok"))
    return jax.shard_map(
        shards, mesh=mesh, in_specs=placed, out_specs=P(("ckpt", "tok"), "vocab"), check_vma=False
    )
```

time: 302 us -> 280 us (0.927)
  blocking collectives: 86 us -> 49.7 us
  other arithmetic: 2.99 us -> 23.7 us
  waiting for transfers between devices: 117 us -> 133 us
  Pallas kernels: 53.4 us -> 38.9 us
  between operations: 13.6 us -> 0.27 us
  starting transfers between devices: 18.9 us -> 25.3 us
    ppermute x0 -> x7, waiting for transfers between devices: none -> 91.8 us  [other(): lax.ppermute(x, axis, [(i, i ^ far) for i in range(lax.axis_size(axis))])]
    all_to_all x2 -> x1, waiting for transfers between devices: 76.2 us -> 32.2 us  [exchange(): return lax.all_to_all(x, BOTH, 0, 0, tiled=True)]
    all_gather x2 -> x0, waiting for transfers between devices: 39.3 us -> none  [the longest x1 39.3 us: shards(): along = lax.all_gather(own, 'ckpt', axis=0)]
    all_gather x1 -> x0, blocking collectives: 39 us -> none  [shards(): lax.all_gather(after(targets, narrow_in), 'tok', axis=0, tiled=True)]
    pallas_call x7 -> x3, Pallas kernels: 42 us -> 27.9 us  [the longest x1 13.6 us: merge(): call(functools.partial(merge_kernel, prior=prior), 'merge', out_shape=jax...]
    ppermute x0 -> x7, starting transfers between devices: none -> 12.5 us  [other(): lax.ppermute(x, axis, [(i, i ^ far) for i in range(lax.axis_size(axis))])]
    select_n x0 -> x9, other arithmetic: none -> 10.8 us  [the longest x7 9.27 us: paired(): return jnp.concatenate([jnp.where(upper, y, x), jnp.where(upper, x, y)])]
    concatenate x1 -> x4, other arithmetic: 0.61 us -> 9.5 us  [the longest x3 9.49 us: paired(): return jnp.concatenate([jnp.where(upper, y, x), jnp.where(upper, x, y)])]
  transfers between devices with their start and end apart: 9 -> 13, of which waited for: 4 -> 12; matrix products, arithmetic and copies ran while one was open for 1% -> 7% of each run, Pallas kernels for 10% -> 5%
where the time goes in v3:
time: 280 us; the launch traced here: 277 us
  waiting for transfers between devices  133 us (48%)
  blocking collectives  49.7 us (18%)
  Pallas kernels  38.9 us (14%)
  starting transfers between devices  25.3 us (9%)
  other arithmetic  23.7 us (8%)
  local copies, waits for them, and re-layouts  7.06 us (3%)
    ppermute x7, waiting for transfers between devices, other(): lax.ppermute(x, axis, [(i, i ^ far) for i in range(lax.axis_size(axis))])  91.8 us
    all_to_all x1, blocking collectives, exchange(): return lax.all_to_all(x, BOTH, 0, 0, tiled=True)  49.7 us
    all_to_all x1, waiting for transfers between devices, exchange(): return lax.all_to_all(x, BOTH, 0, 0, tiled=True)  32.2 us
    pallas_call x1, Pallas kernels, merge(): call(functools.partial(merge_kernel, prior=prior), 'merge', out_shape=jax...  13.6 us
    ppermute x7, starting transfers between devices, other(): lax.ppermute(x, axis, [(i, i ^ far) for i in range(lax.axis_size(axis))])  12.5 us
    pallas_call x1, Pallas kernels, score(): call(score_kernel, 'score', out_shape=(jax.ShapeDtypeStruct((ckpts, token...  11 us
    concatenate x3, other arithmetic, paired(): return jnp.concatenate([jnp.where(upper, y, x), jnp.where(upper, x, y)])  9.49 us
    select_n x7, other arithmetic, paired(): return jnp.concatenate([jnp.where(upper, y, x), jnp.where(upper, x, y)])  9.27 us
  transfers between devices with their start and end apart: 13, of which 12 were waited for; matrix products, arithmetic and copies ran while one was open for 7% of the time, Pallas kernels for 5%

profile of v3, /device:TPU:9, one launch (start us, length us, event | category | flops | bytes accessed | tf_op | source)
XLA Modules:
  0.0 277.4 jit_solution(5988201585314158098)
XLA Ops:
  0.0 0.8 fusion.47
  0.8 0.7 fusion.49
  1.8 2.5 collective-permute-start.1
  4.5 7.6 %pack.1 = bf16[16,5,160,256]{3,2,1,0:T(8,128)(2,1)} custom-call(bf16[640,5120]{1,0:T(8,128)(2,1)} %bitcast.285, bf16[640,5120]{1,0:T(8,128)(2,1)} %bitcast.286, bf16[640,5120]{1,0:T(8,128)(2,1)} %bitcast.287, bf16[640,5120]{1,0:T(8,128)(2,1)} %bitcast.288), custom_call_target="tpu_custom_call" | custom-call | tf_op jit(solution)/shard_map/pack/pallas_call | solution.py:44
  12.0 3.4 %collective-permute-done.2 = bf16[1,64,2688]{2,1,0:T(8,128)(2,1)S(1)} collective-permute-done((bf16[1,64,2688]{2,1,0:T(8,128)(2,1)S(1)}, bf16[1,64,2688]{2,1,0:T(8,128)(2,1)S(1)}, u32[]{:S(2)}, u32[]{:S(2)}) %collective-permute-start.2) | collective-permute-done | bytes 344096 | tf_op jit(solution)/shard_map/ppermute | solution.py:250
  15.6 3.6 %collective-permute-done.1 = bf16[1,64,2688]{2,1,0:T(8,128)(2,1)S(1)} collective-permute-done((bf16[1,64,2688]{2,1,0:T(8,128)(2,1)S(1)}, bf16[1,64,2688]{2,1,0:T(8,128)(2,1)S(1)}, u32[]{:S(2)}, u32[]{:S(2)}) %collective-permute-start.1) | collective-permute-done | bytes 344096 | tf_op jit(solution)/shard_map/ppermute | solution.py:250
  19.2 14.6 %collective-permute-done = bf16[1,64,2688]{2,1,0:T(8,128)(2,1)S(1)} collective-permute-done((bf16[1,64,2688]{2,1,0:T(8,128)(2,1)S(1)}, bf16[1,64,2688]{2,1,0:T(8,128)(2,1)S(1)}, u32[]{:S(2)}, u32[]{:S(2)}) %collective-permute-start) | collective-permute-done | bytes 344096 | tf_op jit(solution)/shard_map/ppermute | solution.py:250
  33.9 0.2 broadcast_select_fusion.9
  34.2 1.3 collective-permute-start.3
  35.5 6.1 %all-to-all-start = ((bf16[16,800,256]{2,1,0:T(8,128)(2,1)}), bf16[16,800,256]{2,1,0:T(8,128)(2,1)}, u32[]{:S(2)}, u32[]{:S(2)}) async-start(bf16[16,800,256]{2,1,0:T(8,128)(2,1)} %bitcast.289), calls=%async_computation | async-start | bytes 13107200 | tf_op jit(solution)/shard_map/all_to_all | solution.py:207
  41.6 1.2 collective-permute-start.5
  42.8 37.9 %collective-permute-done.3 = bf16[1,4,64,2688]{3,2,1,0:T(8,128)(2,1)S(1)} collective-permute-done((bf16[1,4,64,2688]{3,2,1,0:T(8,128)(2,1)S(1)}, bf16[1,4,64,2688]{3,2,1,0:T(8,128)(2,1)S(1)}, u32[]{:S(2)}, u32[]{:S(2)}) %collective-permute-start.3) | collective-permute-done | bytes 1376288 | tf_op jit(solution)/shard_map/ppermute | solution.py:250
  80.7 1.2 collective-permute-start.4
  82.0 1.6 broadcast_select_fusion.5
  83.6 23.9 %collective-permute-done.4 = bf16[1,4,64,2688]{3,2,1,0:T(8,128)(2,1)} collective-permute-done((bf16[1,4,64,2688]{3,2,1,0:T(8,128)(2,1)S(1)}, bf16[1,4,64,2688]{3,2,1,0:T(8,128)(2,1)}, u32[]{:S(2)}, u32[]{:S(2)}) %collective-permute-start.4) | collective-permute-done | bytes 1376288 | tf_op jit(solution)/shard_map/ppermute | solution.py:250
  107.4 1.6 broadcast_select_fusion.7
  109.0 0.7 broadcast_select_fusion.3
  109.8 3.3 %pad_maximum_fusion.1 = bf16[4,4,64,2688]{3,2,1,0:T(8,128)(2,1)} fusion(bf16[2,4,64,2688]{3,2,1,0:T(8,128)(2,1)S(1)} %get-tuple-element.27, bf16[2,4,64,2688]{3,2,1,0:T(8,128)(2,1)S(1)} %get-tuple-element.26), kind=kLoop, calls=%fused_computation.3 | loop fusion | flops 2752512 | bytes 11010048 | tf_op jit(solution)/shard_map/concatenate | solution.py:254
  113.1 0.9 copy-done.4
  114.0 6.0 %collective-permute-start.6 = (bf16[4,4,64,2688]{3,2,1,0:T(8,128)(2,1)}, bf16[4,4,64,2688]{3,2,1,0:T(8,128)(2,1)}, u32[]{:S(2)}, u32[]{:S(2)}) collective-permute-start(bf16[4,4,64,2688]{3,2,1,0:T(8,128)(2,1)} %pad_maximum_fusion.1), channel_id=1, source_target_pairs={{0,2},{2,0},{4,6},{6,4},{1,3},{3,1},{5,7},{7,5},{8,10},{10,8},{12,... | collective-permute-start | bytes 16515080 | tf_op jit(solution)/shard_map/ppermute | solution.py:250
  120.1 0.6 broadcast_in_dim.13.ids_ref
  120.7 8.3 %collective-permute-done.6 = bf16[4,4,64,2688]{3,2,1,0:T(8,128)(2,1)} collective-permute-done((bf16[4,4,64,2688]{3,2,1,0:T(8,128)(2,1)}, bf16[4,4,64,2688]{3,2,1,0:T(8,128)(2,1)}, u32[]{:S(2)}, u32[]{:S(2)}) %collective-permute-start.6) | collective-permute-done | bytes 5505056 | tf_op jit(solution)/shard_map/ppermute | solution.py:250
  129.0 5.0 %broadcast_select_fusion.1 = (bf16[4,4,64,2688]{3,2,1,0:T(8,128)(2,1)S(1)}, bf16[4,4,64,2688]{3,2,1,0:T(8,128)(2,1)S(1)}) fusion(bf16[4,4,64,2688]{3,2,1,0:T(8,128)(2,1)} %collective-permute-done.6, pred[]{:T(512)S(6)} %eq.28, bf16[2,4,64,2688]{3,2,1,0:T(8,128)(2,1)} %copy-done.4, bf16[2,4,64,2688]{3,2,1,0:T(8,128)(2,1)} %copy-done.3), kind=kLoop, calls=%fused_computation.5 | loop fusion | flops 8257536 | bytes 22020096 | tf_op jit(solution)/shard_map/jit(_where)/select_n | solution.py:254
  134.1 2.4 copy-done.2
  136.5 5.3 %pad_maximum_fusion.states_ref.hidden_ref = bf16[8,4,64,2688]{3,2,1,0:T(8,128)(2,1)} fusion(bf16[4,4,64,2688]{3,2,1,0:T(8,128)(2,1)S(1)} %get-tuple-element.25, bf16[4,4,64,2688]{3,2,1,0:T(8,128)(2,1)S(1)} %get-tuple-element.24), kind=kLoop, calls=%fused_computation.1 | loop fusion | flops 5505024 | bytes 22020096 | tf_op jit(solution)/shard_map/concatenate | solution.py:254
  141.8 6.7 %rows.1 = f32[4,8,512]{2,1,0:T(8,128)} custom-call(bf16[8,4,64,2688]{3,2,1,0:T(8,128)(2,1)} %pad_maximum_fusion.states_ref.hidden_ref), custom_call_target="tpu_custom_call" | custom-call | tf_op jit(solution)/shard_map/rows/pallas_call | solution.py:66
  148.5 0.9 fusion.5
  149.4 0.9 fusion.3.labels_ref
  150.3 32.2 %all-to-all-done = bf16[16,800,256]{2,1,0:T(8,128)(2,1)} async-done(((bf16[16,800,256]{2,1,0:T(8,128)(2,1)}), bf16[16,800,256]{2,1,0:T(8,128)(2,1)}, u32[]{:S(2)}, u32[]{:S(2)}) %all-to-all-start) | async-done | bytes 6553632 | tf_op jit(solution)/shard_map/all_to_all | solution.py:207
  182.4 11.0 %score.1 = (f32[4,512,384]{2,1,0:T(8,128)}, f32[4,8,512]{2,1,0:T(8,128)}) custom-call(bf16[8,4,64,2688]{3,2,1,0:T(8,128)(2,1)} %pad_maximum_fusion.states_ref.hidden_ref, bf16[4,4,800,256]{3,2,1,0:T(8,128)(2,1)} %bitcast.9.heads_ref, s32[512,1]{1,0:T(8,128)} %fusion.3.labels_ref, s32[1,384]{1,0:T(1,128)} %broadcast_in_dim.13.ids_ref), custom_call_target="tpu_custom_call" | custom-call | tf_op jit(solution)/shard_map/score/pallas_call | solution.py:112
  193.4 0.8 slice_bitcast_fusion.1
  194.3 1.0 collective-permute-start.7
  195.3 0.8 collective-permute-done.7
  196.2 2.8 %collective-permute-start.8 = (f32[4,4,512]{2,1,0:T(4,128)S(1)}, f32[4,4,512]{2,1,0:T(4,128)S(1)}, u32[]{:S(2)}, u32[]{:S(2)}) collective-permute-start(f32[4,4,512]{2,1,0:T(4,128)S(1)} %pad_maximum_fusion.7), channel_id=1, source_target_pairs={{0,4},{2,6},{4,0},{6,2},{1,5},{3,7},{5,1},{7,3},{8,12},{10,14},{12... | collective-permute-start | bytes 98312 | tf_op jit(solution)/shard_map/ppermute | solution.py:222
  199.1 1.3 collective-permute-done.8
  200.4 1.3 collective-permute-start.9
  201.8 1.5 collective-permute-done.9
  203.4 2.8 collective-permute-done.10
  206.2 1.5 collective-permute-start.11
  207.8 2.2 collective-permute-done.11
  210.1 0.6 multiply_divide_fusion.scale_ref
  210.7 0.8 copy.24
  211.5 13.6 %merge.1 = bf16[16,208,256]{2,1,0:T(8,128)(2,1)} custom-call(f32[4]{0:T(128)} %multiply_divide_fusion.scale_ref, f32[4,512,384]{2,1,0:T(8,128)} %get-tuple-element.12.logits_ref, f32[512,8]{1,0:T(8,128)} %bitcast.292, s32[512,1]{1,0:T(8,128)} %fusion.3.labels_ref, s32[1,384]{1,0:T(1,128)} %broadcast_in_dim.13.ids_ref, ...), custom_call_target="tpu_custom_call" | custom-call | tf_op jit(solution)/shard_map/merge/pallas_call | solution.py:187
  225.2 49.7 %all_to_all.10 = bf16[16,208,256]{2,1,0:T(8,128)(2,1)S(1)} all-to-all(bf16[16,208,256]{2,1,0:T(8,128)(2,1)} %merge.1), channel_id=1, replica_groups=mesh['ckpt'=4,'tok'=4,'vocab'=2] {'ckpt','tok'}, dimensions={0} | all-to-all | bytes 3407872 | tf_op jit(solution)/shard_map/all_to_all | solution.py:207
  275.1 0.3 reshape.71
  275.4 0.3 copy.26
  275.7 0.4 reshape.72
  276.1 1.3 pad_maximum_fusion.4
  (44 shorter events, 1.6 us)
Async XLA Ops:
  0.0 1.7 copy-start
  1.8 13.7 %collective-permute-start.2 = (bf16[1,64,2688]{2,1,0:T(8,128)(2,1)S(1)}, bf16[1,64,2688]{2,1,0:T(8,128)(2,1)S(1)}, u32[]{:S(2)}, u32[]{:S(2)}) collective-permute-start(bf16[1,64,2688]{2,1,0:T(8,128)(2,1)S(1)} %fusion.2), channel_id=1, source_target_pairs={{0,8},{8,0},{16,24},{24,16},{1,9},{9,1},{17,25},{25,17},{2,10},{10... | collective-permute-start | bytes 1032200 | tf_op jit(solution)/shard_map/ppermute | solution.py:250
  1.8 17.4 %collective-permute-start.1 = (bf16[1,64,2688]{2,1,0:T(8,128)(2,1)S(1)}, bf16[1,64,2688]{2,1,0:T(8,128)(2,1)S(1)}, u32[]{:S(2)}, u32[]{:S(2)}) collective-permute-start(bf16[1,64,2688]{2,1,0:T(8,128)(2,1)S(1)} %fusion.2), channel_id=1, source_target_pairs={{0,16},{8,24},{16,0},{24,8},{1,17},{9,25},{17,1},{25,9},{2,18},{10... | collective-permute-start | bytes 1032200 | tf_op jit(solution)/shard_map/ppermute | solution.py:250
  4.3 29.5 %collective-permute-start = (bf16[1,64,2688]{2,1,0:T(8,128)(2,1)S(1)}, bf16[1,64,2688]{2,1,0:T(8,128)(2,1)S(1)}, u32[]{:S(2)}, u32[]{:S(2)}) collective-permute-start(bf16[1,64,2688]{2,1,0:T(8,128)(2,1)S(1)} %fusion.2), channel_id=1, source_target_pairs={{0,24},{8,16},{16,8},{24,0},{1,25},{9,17},{17,9},{25,1},{2,26},{10... | collective-permute-start | bytes 1032200 | tf_op jit(solution)/shard_map/ppermute | solution.py:250
  34.2 46.5 %collective-permute-start.3 = (bf16[1,4,64,2688]{3,2,1,0:T(8,128)(2,1)S(1)}, bf16[1,4,64,2688]{3,2,1,0:T(8,128)(2,1)S(1)}, u32[]{:S(2)}, u32[]{:S(2)}) collective-permute-start(bf16[1,4,64,2688]{3,2,1,0:T(8,128)(2,1)S(1)} %maximum_bitcast_fusion), channel_id=1, source_target_pairs={{0,4},{2,6},{4,0},{6,2},{1,5},{3,7},{5,1},{7,3},{8,12},{10,14},{12... | collective-permute-start | bytes 4128776 | tf_op jit(solution)/shard_map/ppermute | solution.py:250
  35.5 146.9 %all-to-all-start = ((bf16[16,800,256]{2,1,0:T(8,128)(2,1)}), bf16[16,800,256]{2,1,0:T(8,128)(2,1)}, u32[]{:S(2)}, u32[]{:S(2)}) async-start(bf16[16,800,256]{2,1,0:T(8,128)(2,1)} %bitcast.289), calls=%async_computation | async-start | bytes 13107200 | tf_op jit(solution)/shard_map/all_to_all | solution.py:207
  41.6 40.4 %collective-permute-start.5 = (bf16[1,4,64,2688]{3,2,1,0:T(8,128)(2,1)S(1)}, bf16[1,4,64,2688]{3,2,1,0:T(8,128)(2,1)}, u32[]{:S(2)}, u32[]{:S(2)}) collective-permute-start(bf16[1,4,64,2688]{3,2,1,0:T(8,128)(2,1)S(1)} %maximum_bitcast_fusion), channel_id=1, source_target_pairs={{0,1},{1,0},{2,3},{3,2},{4,5},{5,4},{6,7},{7,6},{8,9},{9,8},{10,11... | collective-permute-start | bytes 4128776 | tf_op jit(solution)/shard_map/ppermute | solution.py:250
  80.7 26.7 %collective-permute-start.4 = (bf16[1,4,64,2688]{3,2,1,0:T(8,128)(2,1)S(1)}, bf16[1,4,64,2688]{3,2,1,0:T(8,128)(2,1)}, u32[]{:S(2)}, u32[]{:S(2)}) collective-permute-start(bf16[1,4,64,2688]{3,2,1,0:T(8,128)(2,1)S(1)} %collective-permute-done.3), channel_id=1, source_target_pairs={{0,1},{1,0},{2,3},{3,2},{4,5},{5,4},{6,7},{7,6},{8,9},{9,8},{10,11... | collective-permute-start | bytes 4128776 | tf_op jit(solution)/shard_map/ppermute | solution.py:250
  109.7 3.4 %copy-start.3 = (bf16[2,4,64,2688]{3,2,1,0:T(8,128)(2,1)}, bf16[2,4,64,2688]{3,2,1,0:T(8,128)(2,1)S(1)}, u32[]{:S(2)}) copy-start(bf16[2,4,64,2688]{3,2,1,0:T(8,128)(2,1)S(1)} %get-tuple-element.26) | copy-start | bytes 8257540
  109.7 4.3 %copy-start.4 = (bf16[2,4,64,2688]{3,2,1,0:T(8,128)(2,1)}, bf16[2,4,64,2688]{3,2,1,0:T(8,128)(2,1)S(1)}, u32[]{:S(2)}) copy-start(bf16[2,4,64,2688]{3,2,1,0:T(8,128)(2,1)S(1)} %get-tuple-element.27) | copy-start | bytes 8257540
  114.0 15.0 %collective-permute-start.6 = (bf16[4,4,64,2688]{3,2,1,0:T(8,128)(2,1)}, bf16[4,4,64,2688]{3,2,1,0:T(8,128)(2,1)}, u32[]{:S(2)}, u32[]{:S(2)}) collective-permute-start(bf16[4,4,64,2688]{3,2,1,0:T(8,128)(2,1)} %pad_maximum_fusion.1), channel_id=1, source_target_pairs={{0,2},{2,0},{4,6},{6,4},{1,3},{3,1},{5,7},{7,5},{8,10},{10,8},{12,... | collective-permute-start | bytes 16515080 | tf_op jit(solution)/shard_map/ppermute | solution.py:250
  134.0 2.4 copy-start.2
  182.4 27.5 %slice-start = ((f32[4,8,512]{2,1,0:T(8,128)}), f32[4,1,512]{2,1,0:T(1,128)S(1)}, s32[]{:S(2)}) async-start(f32[4,8,512]{2,1,0:T(8,128)} %rows.1), calls=%async_computation.2 | async-start | bytes 16384 | tf_op jit(solution)/shard_map/slice | solution.py:287
  194.3 1.9 collective-permute-start.7
  196.2 4.1 %collective-permute-start.8 = (f32[4,4,512]{2,1,0:T(4,128)S(1)}, f32[4,4,512]{2,1,0:T(4,128)S(1)}, u32[]{:S(2)}, u32[]{:S(2)}) collective-permute-start(f32[4,4,512]{2,1,0:T(4,128)S(1)} %pad_maximum_fusion.7), channel_id=1, source_target_pairs={{0,4},{2,6},{4,0},{6,2},{1,5},{3,7},{5,1},{7,3},{8,12},{10,14},{12... | collective-permute-start | bytes 98312 | tf_op jit(solution)/shard_map/ppermute | solution.py:222
  200.4 2.8 %collective-permute-start.9 = (f32[4,4,512]{2,1,0:T(4,128)S(1)}, f32[4,4,512]{2,1,0:T(4,128)S(1)}, u32[]{:S(2)}, u32[]{:S(2)}) collective-permute-start(f32[4,4,512]{2,1,0:T(4,128)S(1)} %pad_maximum_fusion.8), channel_id=1, source_target_pairs={{0,1},{1,0},{2,3},{3,2},{4,5},{5,4},{6,7},{7,6},{8,9},{9,8},{10,11... | collective-permute-start | bytes 98312 | tf_op jit(solution)/shard_map/ppermute | solution.py:222
  203.3 2.8 %collective-permute-start.10 = (f32[4,4,512]{2,1,0:T(4,128)S(1)}, f32[4,4,512]{2,1,0:T(4,128)S(1)}, u32[]{:S(2)}, u32[]{:S(2)}) collective-permute-start(f32[4,4,512]{2,1,0:T(4,128)S(1)} %pad_maximum_fusion.9), channel_id=1, source_target_pairs={{0,8},{8,0},{16,24},{24,16},{1,9},{9,1},{17,25},{25,17},{2,10},{10... | collective-permute-start | bytes 98312 | tf_op jit(solution)/shard_map/ppermute | solution.py:222
  206.2 3.7 %collective-permute-start.11 = (f32[4,4,512]{2,1,0:T(4,128)S(1)}, f32[4,4,512]{2,1,0:T(4,128)S(1)}, u32[]{:S(2)}, u32[]{:S(2)}) collective-permute-start(f32[4,4,512]{2,1,0:T(4,128)S(1)} %pad_maximum_fusion.10), channel_id=1, source_target_pairs={{0,16},{8,24},{16,0},{24,8},{1,17},{9,25},{17,1},{25,9},{2,18},{10... | collective-permute-start | bytes 98312 | tf_op jit(solution)/shard_map/ppermute | solution.py:222
  275.4 2.0 copy-start.1

commit v4 on v3

--- a/solution.py
+++ b/solution.py
@@ -13,9 +13,9 @@
 BOTH = ("ckpt", "tok")
 
 
-def call(kernel, name, **options):
+def call(kernel, name, vmem=VMEM, **options):
     return pl.pallas_call(
-        kernel, name=name, compiler_params=pltpu.CompilerParams(vmem_limit_bytes=VMEM), **options
+        kernel, name=name, compiler_params=pltpu.CompilerParams(vmem_limit_bytes=vmem), **options
     )
 
 
@@ -55,20 +55,35 @@
     return jnp.square(x.astype(jnp.float32)).astype(jnp.bfloat16)
 
 
-def rows_kernel(states_ref, out_ref):
-    x = squared(states_ref[...].reshape(-1, states_ref.shape[3]))
-    ones = jnp.ones((8, x.shape[1]), jnp.bfloat16)
-    out_ref[0] = lax.dot_general(ones, x, (((1,), (1,)), ((), ())), preferred_element_type=jnp.float32)
-
-
-def row_sums(states, features):
+def square_kernel(states_ref, out_ref, sum_ref):
+    turned = squared(states_ref[...].reshape(-1, states_ref.shape[3])).T
+    out_ref[0] = turned
+    part = jnp.sum(turned.astype(jnp.float32), axis=0, keepdims=True)
+
+    @pl.when(pl.program_id(1) == 0)
+    def _():
+        sum_ref[0] = part
+
+    @pl.when(pl.program_id(1) > 0)
+    def _():
+        sum_ref[0] += part
+
+
+def squares(states, features, blocks):
     groups, ckpts, size, _ = states.shape
+    tokens, tile = groups * size, features // blocks
     return call(
-        rows_kernel, "rows",
-        out_shape=jax.ShapeDtypeStruct((ckpts, 8, groups * size), jnp.float32),
-        grid=(ckpts,),
-        in_specs=[pl.BlockSpec((groups, 1, size, features), lambda c: (0, c, 0, 0))],
-        out_specs=pl.BlockSpec((1, 8, groups * size), lambda c: (c, 0, 0)),
+        square_kernel, "squares",
+        out_shape=(
+            jax.ShapeDtypeStruct((ckpts, features, tokens), jnp.bfloat16),
+            jax.ShapeDtypeStruct((ckpts, 1, tokens), jnp.float32),
+        ),
+        grid=(ckpts, blocks),
+        in_specs=[pl.BlockSpec((groups, 1, size, tile), lambda c, f: (0, c, 0, f))],
+        out_specs=(
+            pl.BlockSpec((1, tile, tokens), lambda c, f: (c, f, 0)),
+            pl.BlockSpec((1, 1, tokens), lambda c, f: (c, 0, 0)),
+        ),
     )(states)
 
 
@@ -130,73 +145,115 @@
 
 
 def merge_kernel(
-    scale_ref, logits_ref, table_ref, labels_ref, ids_ref, hidden_ref, heads_ref, out_ref, resid_ref,
-    *, prior
+    place_ref, scale_ref, logits_ref, table_ref, labels_ref, ids_ref, hidden_ref, heads_ref, *refs, prior
 ):
-    ckpts = logits_ref.shape[0]
-    wide, depth = heads_ref.shape[3], hidden_ref.shape[3]
-    slim = logits_ref.shape[2] - wide
+    outs, wide_rows, slim_rows, resid_ref = refs[:-3], *refs[-3:]
+    ckpts, tokens, lanes = resid_ref.shape
+    wide, depth = heads_ref.shape[3], hidden_ref.shape[1]
+    slim = lanes - wide
     fold = wide // (slim // 2)
 
     @pl.when(pl.program_id(0) == 0)
     def _():
         target = jnp.where(labels_ref[...] == ids_ref[...], 1.0, 0.0)
+        table = table_ref[...].T
         for c in range(ckpts):
-            top, total = table_ref[:, c : c + 1], table_ref[:, ckpts + c : ckpts + c + 1]
+            top, total = table[:, c : c + 1], table[:, ckpts + c : ckpts + c + 1]
             share = jnp.exp(logits_ref[c] - top) * (1.0 / total)
             resid_ref[c] = jnp.square(share - target).astype(jnp.bfloat16)
-
-    hidden = [squared(hidden_ref[:, c].reshape(-1, hidden_ref.shape[3])) for c in range(ckpts)]
 
     def blend(lo, hi, heads_of):
         numer = denom = None
         for c in range(ckpts):
-            product = lax.dot_general(
-                hidden[c], resid_ref[c, :, lo:hi], (((0,), (0,)), ((), ())), preferred_element_type=jnp.float32
-            )
+            product = jnp.dot(hidden_ref[c], resid_ref[c, :, lo:hi], preferred_element_type=jnp.float32)
             weight = (product * scale_ref[c] + prior).astype(jnp.bfloat16).astype(jnp.float32)
             term = weight * heads_of(c).astype(jnp.float32)
             numer = term if numer is None else numer + term
             denom = weight if denom is None else denom + weight
         return numer / denom
 
-    peers, own = out_ref.shape[0], depth // out_ref.shape[0]
-    merged = blend(0, wide, lambda c: heads_ref[c, 0, :depth])
-    out_ref[:, :own] = merged.astype(out_ref.dtype).reshape(peers, own, wide)
-    merged = blend(wide, wide + slim, lambda c: padded([unfolded(heads_ref[c, 0, depth:], fold)], slim))
+    wide_rows[...] = blend(0, wide, lambda c: heads_ref[c, 0, :depth])
+    slim_rows[...] = blend(wide, lanes, lambda c: padded([unfolded(heads_ref[c, 0, depth:], fold)], slim))
+    pair = outs[0].shape[0]
+    halves = len(outs) // ckpts
+    own = depth // (pair * halves)
     height = own // fold
-    for peer in range(peers):
-        pieces = [
-            merged[peer * own + q * height : peer * own + (q + 1) * height, : slim // 2] for q in range(fold)
-        ]
-        block = jnp.concatenate(pieces, axis=1)
-        rest = jnp.zeros((out_ref.shape[1] - own - height, block.shape[1]), jnp.float32)
-        out_ref[peer, own:] = jnp.concatenate([block, rest], axis=0).astype(out_ref.dtype)
-
-
-def merge(scales, prior, logits, table, labels, ids, states, heads, depth, ntok):
+    for plane in range(ckpts):
+
+        @pl.when(pl.program_id(0) == plane)
+        def _():
+            for far in range(pair * halves):
+                out_ref, slot = outs[plane * halves + far // pair], far % pair
+                first = pl.multiple_of((place_ref[1] ^ far) * own, own)
+                out_ref[slot, :own] = wide_rows[pl.ds(first, own)].astype(out_ref.dtype)
+                rows = slim_rows[pl.ds(first, own)]
+                block = jnp.concatenate(
+                    [rows[q * height : (q + 1) * height, : slim // 2] for q in range(fold)], axis=1
+                )
+                rest = jnp.zeros((out_ref.shape[1] - own - height, wide), jnp.float32)
+                out_ref[slot, own:] = jnp.concatenate([block, rest], axis=0).astype(out_ref.dtype)
+
+
+def merge(place, scales, prior, logits, table, labels, ids, hidden_sq, heads, ntok):
     ckpts, blocks, _, width = heads.shape
     tokens, lanes = logits.shape[1:]
-    slim = (lanes - width) // 2
+    depth = hidden_sq.shape[1] // blocks
     own = depth // ntok
-    tall = own + -(-own * slim // width // 16) * 16
+    tall = own + -(-own * (lanes - width) // 2 // width // 16) * 16
+    shape = (2, tall, width)
 
     def whole(x):
-        return pl.BlockSpec(x.shape, lambda i: (0,) * x.ndim)
+        return pl.BlockSpec(x.shape, lambda i, s: (0,) * x.ndim)
 
     return call(
         functools.partial(merge_kernel, prior=prior), "merge",
-        out_shape=jax.ShapeDtypeStruct((blocks * ntok, tall, width), jnp.bfloat16),
-        grid=(blocks,),
-        in_specs=[pl.BlockSpec(memory_space=pltpu.SMEM)]
-        + [whole(x) for x in (logits, table, labels, ids)]
-        + [
-            pl.BlockSpec((*states.shape[:3], depth), lambda i: (0, 0, 0, i)),
-            pl.BlockSpec((ckpts, 1, *heads.shape[2:]), lambda i: (0, i, 0, 0)),
-        ],
-        out_specs=pl.BlockSpec((ntok, tall, width), lambda i: (i, 0, 0)),
-        scratch_shapes=[pltpu.VMEM((ckpts, tokens, lanes), jnp.bfloat16)],
-    )(scales, logits, table, labels, ids, states, heads)
+        out_shape=[jax.ShapeDtypeStruct(shape, jnp.bfloat16)] * (blocks * ntok // 2),
+        grid_spec=pltpu.PrefetchScalarGridSpec(
+            num_scalar_prefetch=1,
+            grid=(blocks,),
+            in_specs=[pl.BlockSpec(memory_space=pltpu.SMEM)]
+            + [whole(x) for x in (logits, table, labels, ids)]
+            + [
+                pl.BlockSpec((ckpts, depth, tokens), lambda i, s: (0, s[0] ^ i, 0)),
+                pl.BlockSpec((ckpts, 1, *heads.shape[2:]), lambda i, s: (0, s[0] ^ i, 0, 0)),
+            ],
+            out_specs=[pl.BlockSpec(shape, lambda i, s: (0, 0, 0))] * (blocks * ntok // 2),
+            scratch_shapes=[
+                pltpu.VMEM((depth, width), jnp.float32),
+                pltpu.VMEM((depth, lanes - width), jnp.float32),
+                pltpu.VMEM((ckpts, tokens, lanes), jnp.bfloat16),
+            ],
+        ),
+    )(place, scales, logits, table, labels, ids, hidden_sq, heads)
+
+
+def assemble_kernel(mine_ref, *refs, sources):
+    arrays, out_ref = refs[:-1], refs[-1]
+    own, columns = out_ref.shape
+    wide = arrays[0].shape[2]
+    narrow = columns // len(sources) - wide
+    fold = wide // narrow
+    height = own // fold
+    mine = mine_ref[0]
+    slim = []
+    for r, (array, slot) in enumerate(sources):
+        out_ref[:, pl.ds(pl.multiple_of((mine ^ r) * wide, wide), wide)] = arrays[array][slot, :own]
+        slim.append(unfolded(arrays[array][slot, own:].astype(jnp.float32)[:height], fold))
+    for r in range(0, len(sources), 2):
+        ours, theirs = slim[r], slim[r + 1]
+        odd = mine % 2 == 1
+        pair = jnp.concatenate([jnp.where(odd, theirs, ours), jnp.where(odd, ours, theirs)], axis=1)
+        first = len(sources) * wide + (mine ^ r) // 2 * 2 * narrow
+        out_ref[:, pl.ds(pl.multiple_of(first, 2 * narrow), 2 * narrow)] = pair.astype(out_ref.dtype)
+
+
+def assemble(mine, arrays, sources, own, columns):
+    return call(
+        functools.partial(assemble_kernel, sources=sources), "assemble", VMEM // 2,
+        out_shape=jax.ShapeDtypeStruct((own, columns), jnp.bfloat16),
+        in_specs=[pl.BlockSpec(memory_space=pltpu.SMEM)] + [pl.BlockSpec(memory_space=pltpu.VMEM)] * len(arrays),
+        out_specs=pl.BlockSpec(memory_space=pltpu.VMEM),
+    )(mine.astype(jnp.int32)[None], *arrays)
 
 
 def after(value, *earlier):
@@ -278,7 +335,7 @@
     ids = jnp.concatenate(
         [base + mine * wide + jnp.arange(wide), base + split + mine * narrow + jnp.arange(narrow), pad]
     ).astype(jnp.int32)[None]
-    hidden_rows = row_sums(states, features)
+    hidden_sq, hidden_rows = squares(states, features, ntok)
     logits, stats = score(after(states, hidden_rows), features, columns_in, labels, ids)
     top, total, off, hit = everywhere(stats[:, :4].transpose(1, 0, 2))
     resid_rows = off / (total * total) + jnp.square(hit / total - 1.0)
@@ -288,20 +345,27 @@
     ratio = vocab_total / tokens
     shrink = 2.0 ** -math.ceil(math.log2(max(ratio, 1.0)))
     scales = jnp.float32(ratio * shrink) / level
-    table = jnp.concatenate([top, total]).T
-
-    out = exchange(
-        merge(
-            scales, prior_weight * shrink, logits, table, labels, ids, states,
-            columns_in, depth, ntok,
-        )
-    )
-    own_rows = depth // ntok
-    height = own_rows // fold
-    narrow_out = out[:, own_rows : own_rows + height].reshape(peers, height, fold, narrow).transpose(2, 1, 0, 3)
-    return jnp.concatenate(
-        [out[:, :own_rows].transpose(1, 0, 2).reshape(own_rows, -1), narrow_out.reshape(own_rows, -1)], axis=1
-    )
+    table = jnp.concatenate([top, total])
+
+    place = jnp.stack([lax.axis_index("ckpt"), lax.axis_index("tok")]).astype(jnp.int32)
+    parts = merge(
+        place, scales, prior_weight * shrink, logits, table, labels, ids, hidden_sq, columns_in, ntok
+    )
+    arrays, sources, seconds = [], {}, []
+    for half in reversed(range(peers // 2)):
+        r, part = 2 * half, parts[half]
+        if r:
+            part = lax.ppermute(part, BOTH, [(g, g ^ r) for g in range(peers)])
+        sources[r] = (len(arrays), 0)
+        arrays.append(part)
+        seconds.append((r + 1, part))
+        if half in (peers // 4, 0):
+            handed = other(jnp.stack([x[1] for _, x in seconds]), "tok", 1)
+            for slot, (s, _) in enumerate(seconds):
+                sources[s] = (len(arrays), slot)
+            arrays.append(handed)
+            seconds = []
+    return assemble(mine, arrays, [sources[r] for r in range(peers)], depth // ntok, columns)
 
 
 def solution(mesh):

time: 280 us -> 275 us (0.982)
  blocking collectives: 49.7 us -> 0 us
  starting transfers between devices: 25.3 us -> 48.1 us
  waiting for transfers between devices: 133 us -> 144 us
  Pallas kernels: 38.9 us -> 48.9 us
    all_to_all x1 -> x0, blocking collectives: 49.7 us -> none  [exchange(): return lax.all_to_all(x, BOTH, 0, 0, tiled=True)]
    ppermute x0 -> x7, waiting for transfers between devices: none -> 18.2 us  [shards(): part = lax.ppermute(part, BOTH, [(g, g ^ r) for g in range(peers)])]
    ppermute x7 -> x9, starting transfers between devices: 12.5 us -> 25.9 us  [other(): lax.ppermute(x, axis, [(i, i ^ far) for i in range(lax.axis_size(axis))])]
    pallas_call x2 -> x3, Pallas kernels: 20.3 us -> 30.3 us  [the longest x1 14.7 us: squares(): call(square_kernel, 'squares', out_shape=(jax.ShapeDtypeStruct((ckpts, fe...]
    ppermute x0 -> x7, starting transfers between devices: none -> 9.35 us  [shards(): part = lax.ppermute(part, BOTH, [(g, g ^ r) for g in range(peers)])]
    all_to_all x1, waiting for transfers between devices: 32.2 us -> 24.4 us  [exchange(): return lax.all_to_all(x, BOTH, 0, 0, tiled=True)]
    ppermute x7 -> x9, waiting for transfers between devices: 91.8 us -> 93.2 us  [other(): lax.ppermute(x, axis, [(i, i ^ far) for i in range(lax.axis_size(axis))])]
  transfers between devices with their start and end apart: 13 -> 22, of which waited for: 12 -> 17; matrix products, arithmetic and copies ran while one was open for 7% -> 8% of each run, Pallas kernels for 5% -> 8%
where the time goes in v4:
time: 275 us; the launch traced here: 271 us
  waiting for transfers between devices  144 us (52%)
  Pallas kernels  48.9 us (18%)
  starting transfers between devices  48.1 us (17%)
  other arithmetic  23.9 us (9%)
  local copies, waits for them, and re-layouts  5.72 us (2%)
    ppermute x9, waiting for transfers between devices, other(): lax.ppermute(x, axis, [(i, i ^ far) for i in range(lax.axis_size(axis))])  93.2 us
    ppermute x9, starting transfers between devices, other(): lax.ppermute(x, axis, [(i, i ^ far) for i in range(lax.axis_size(axis))])  25.9 us
    all_to_all x1, waiting for transfers between devices, exchange(): return lax.all_to_all(x, BOTH, 0, 0, tiled=True)  24.4 us
    ppermute x7, waiting for transfers between devices, shards(): part = lax.ppermute(part, BOTH, [(g, g ^ r) for g in range(peers)])  18.2 us
    pallas_call x1, Pallas kernels, squares(): call(square_kernel, 'squares', out_shape=(jax.ShapeDtypeStruct((ckpts, fe...  14.7 us
    pallas_call x1, Pallas kernels, merge(): call(functools.partial(merge_kernel, prior=prior), 'merge', out_shape=[ja...  14.1 us
    pallas_call x1, Pallas kernels, score(): call(score_kernel, 'score', out_shape=(jax.ShapeDtypeStruct((ckpts, token...  11 us
    concatenate x3, other arithmetic, paired(): return jnp.concatenate([jnp.where(upper, y, x), jnp.where(upper, x, y)])  9.51 us
  transfers between devices with their start and end apart: 22, of which 17 were waited for; matrix products, arithmetic and copies ran while one was open for 8% of the time, Pallas kernels for 8%

profile of v4, /device:TPU:9, one launch (start us, length us, event | category | flops | bytes accessed | tf_op | source)
XLA Modules:
  0.0 270.6 jit_solution(16075404095369422918)
XLA Ops:
  1.8 2.5 collective-permute-start.1
  4.5 7.6 %pack.1 = bf16[16,5,160,256]{3,2,1,0:T(8,128)(2,1)} custom-call(bf16[640,5120]{1,0:T(8,128)(2,1)} %bitcast.278, bf16[640,5120]{1,0:T(8,128)(2,1)} %bitcast.279, bf16[640,5120]{1,0:T(8,128)(2,1)} %bitcast.280, bf16[640,5120]{1,0:T(8,128)(2,1)} %bitcast.281), custom_call_target="tpu_custom_call" | custom-call | tf_op jit(solution)/shard_map/pack/pallas_call | solution.py:44
  12.0 3.5 %collective-permute-done.2 = bf16[1,64,2688]{2,1,0:T(8,128)(2,1)S(1)} collective-permute-done((bf16[1,64,2688]{2,1,0:T(8,128)(2,1)S(1)}, bf16[1,64,2688]{2,1,0:T(8,128)(2,1)S(1)}, u32[]{:S(2)}, u32[]{:S(2)}) %collective-permute-start.2) | collective-permute-done | bytes 344096 | tf_op jit(solution)/shard_map/ppermute | solution.py:307
  15.6 3.6 %collective-permute-done.1 = bf16[1,64,2688]{2,1,0:T(8,128)(2,1)S(1)} collective-permute-done((bf16[1,64,2688]{2,1,0:T(8,128)(2,1)S(1)}, bf16[1,64,2688]{2,1,0:T(8,128)(2,1)S(1)}, u32[]{:S(2)}, u32[]{:S(2)}) %collective-permute-start.1) | collective-permute-done | bytes 344096 | tf_op jit(solution)/shard_map/ppermute | solution.py:307
  19.2 14.6 %collective-permute-done = bf16[1,64,2688]{2,1,0:T(8,128)(2,1)S(1)} collective-permute-done((bf16[1,64,2688]{2,1,0:T(8,128)(2,1)S(1)}, bf16[1,64,2688]{2,1,0:T(8,128)(2,1)S(1)}, u32[]{:S(2)}, u32[]{:S(2)}) %collective-permute-start) | collective-permute-done | bytes 344096 | tf_op jit(solution)/shard_map/ppermute | solution.py:307
  34.2 1.3 collective-permute-start.3
  35.5 6.1 %all-to-all-start = ((bf16[16,800,256]{2,1,0:T(8,128)(2,1)}), bf16[16,800,256]{2,1,0:T(8,128)(2,1)}, u32[]{:S(2)}, u32[]{:S(2)}) async-start(bf16[16,800,256]{2,1,0:T(8,128)(2,1)} %bitcast.282), calls=%async_computation | async-start | bytes 13107200 | tf_op jit(solution)/shard_map/all_to_all | solution.py:264
  41.6 1.2 collective-permute-start.5
  42.8 37.9 %collective-permute-done.3 = bf16[1,4,64,2688]{3,2,1,0:T(8,128)(2,1)S(1)} collective-permute-done((bf16[1,4,64,2688]{3,2,1,0:T(8,128)(2,1)S(1)}, bf16[1,4,64,2688]{3,2,1,0:T(8,128)(2,1)S(1)}, u32[]{:S(2)}, u32[]{:S(2)}) %collective-permute-start.3) | collective-permute-done | bytes 1376288 | tf_op jit(solution)/shard_map/ppermute | solution.py:307
  80.7 1.2 collective-permute-start.4
  82.0 1.6 broadcast_select_fusion.5
  83.6 23.9 %collective-permute-done.4 = bf16[1,4,64,2688]{3,2,1,0:T(8,128)(2,1)} collective-permute-done((bf16[1,4,64,2688]{3,2,1,0:T(8,128)(2,1)S(1)}, bf16[1,4,64,2688]{3,2,1,0:T(8,128)(2,1)}, u32[]{:S(2)}, u32[]{:S(2)}) %collective-permute-start.4) | collective-permute-done | bytes 1376288 | tf_op jit(solution)/shard_map/ppermute | solution.py:307
  107.4 1.6 broadcast_select_fusion.7
  109.8 3.3 %pad_maximum_fusion.1 = bf16[4,4,64,2688]{3,2,1,0:T(8,128)(2,1)} fusion(bf16[2,4,64,2688]{3,2,1,0:T(8,128)(2,1)S(1)} %get-tuple-element.47, bf16[2,4,64,2688]{3,2,1,0:T(8,128)(2,1)S(1)} %get-tuple-element.46), kind=kLoop, calls=%fused_computation.3 | loop fusion | flops 2752512 | bytes 11010048 | tf_op jit(solution)/shard_map/concatenate | solution.py:311
  113.8 6.0 %collective-permute-start.6 = (bf16[4,4,64,2688]{3,2,1,0:T(8,128)(2,1)}, bf16[4,4,64,2688]{3,2,1,0:T(8,128)(2,1)}, u32[]{:S(2)}, u32[]{:S(2)}) collective-permute-start(bf16[4,4,64,2688]{3,2,1,0:T(8,128)(2,1)} %pad_maximum_fusion.1), channel_id=1, source_target_pairs={{0,2},{2,0},{4,6},{6,4},{1,3},{3,1},{5,7},{7,5},{8,10},{10,8},{12,... | collective-permute-start | bytes 16515080 | tf_op jit(solution)/shard_map/ppermute | solution.py:307
  120.5 8.3 %collective-permute-done.6 = bf16[4,4,64,2688]{3,2,1,0:T(8,128)(2,1)} collective-permute-done((bf16[4,4,64,2688]{3,2,1,0:T(8,128)(2,1)}, bf16[4,4,64,2688]{3,2,1,0:T(8,128)(2,1)}, u32[]{:S(2)}, u32[]{:S(2)}) %collective-permute-start.6) | collective-permute-done | bytes 5505056 | tf_op jit(solution)/shard_map/ppermute | solution.py:307
  128.8 5.0 %broadcast_select_fusion.1 = (bf16[4,4,64,2688]{3,2,1,0:T(8,128)(2,1)S(1)}, bf16[4,4,64,2688]{3,2,1,0:T(8,128)(2,1)S(1)}) fusion(bf16[4,4,64,2688]{3,2,1,0:T(8,128)(2,1)} %collective-permute-done.6, pred[]{:T(512)S(6)} %eq.28, bf16[2,4,64,2688]{3,2,1,0:T(8,128)(2,1)} %copy-done.5, bf16[2,4,64,2688]{3,2,1,0:T(8,128)(2,1)} %copy-done.4), kind=kLoop, calls=%fused_computation.5 | loop fusion | flops 8257536 | bytes 22020096 | tf_op jit(solution)/shard_map/jit(_where)/select_n | solution.py:311
  133.8 2.4 copy-done.3
  136.2 5.3 %pad_maximum_fusion.states_ref = bf16[8,4,64,2688]{3,2,1,0:T(8,128)(2,1)} fusion(bf16[4,4,64,2688]{3,2,1,0:T(8,128)(2,1)S(1)} %get-tuple-element.45, bf16[4,4,64,2688]{3,2,1,0:T(8,128)(2,1)S(1)} %get-tuple-element.44), kind=kLoop, calls=%fused_computation.1 | loop fusion | flops 5505024 | bytes 22020096 | tf_op jit(solution)/shard_map/concatenate | solution.py:311
  141.5 14.7 %squares.1 = (bf16[4,2560,512]{2,1,0:T(8,128)(2,1)}, f32[4,1,512]{2,1,0:T(1,128)}) custom-call(bf16[8,4,64,2688]{3,2,1,0:T(8,128)(2,1)} %pad_maximum_fusion.states_ref), custom_call_target="tpu_custom_call" | custom-call | tf_op jit(solution)/shard_map/squares/pallas_call | solution.py:75
  157.1 0.9 fusion.3.labels_ref
  158.0 24.4 %all-to-all-done = bf16[16,800,256]{2,1,0:T(8,128)(2,1)} async-done(((bf16[16,800,256]{2,1,0:T(8,128)(2,1)}), bf16[16,800,256]{2,1,0:T(8,128)(2,1)}, u32[]{:S(2)}, u32[]{:S(2)}) %all-to-all-start) | async-done | bytes 6553632 | tf_op jit(solution)/shard_map/all_to_all | solution.py:264
  182.4 11.0 %score.1 = (f32[4,512,384]{2,1,0:T(8,128)}, f32[4,8,512]{2,1,0:T(8,128)}) custom-call(bf16[8,4,64,2688]{3,2,1,0:T(8,128)(2,1)} %pad_maximum_fusion.states_ref, bf16[4,4,800,256]{3,2,1,0:T(8,128)(2,1)} %bitcast.11.heads_ref, s32[512,1]{1,0:T(8,128)} %fusion.3.labels_ref, s32[1,384]{1,0:T(1,128)} %broadcast_in_dim.17.ids_ref), custom_call_target="tpu_custom_call" | custom-call | tf_op jit(solution)/shard_map/score/pallas_call | solution.py:127
  193.4 0.9 copy.9
  194.3 1.0 collective-permute-start.7
  195.3 0.9 collective-permute-done.7
  196.3 2.8 %collective-permute-start.8 = (f32[4,4,512]{2,1,0:T(4,128)S(1)}, f32[4,4,512]{2,1,0:T(4,128)S(1)}, u32[]{:S(2)}, u32[]{:S(2)}) collective-permute-start(f32[4,4,512]{2,1,0:T(4,128)S(1)} %pad_maximum_fusion.8), channel_id=1, source_target_pairs={{0,4},{2,6},{4,0},{6,2},{1,5},{3,7},{5,1},{7,3},{8,12},{10,14},{12... | collective-permute-start | bytes 98312 | tf_op jit(solution)/shard_map/ppermute | solution.py:279
  199.1 1.3 collective-permute-done.8
  200.5 1.3 collective-permute-start.9
  201.8 1.5 collective-permute-done.9
  203.5 2.8 %collective-permute-done.10 = f32[4,4,512]{2,1,0:T(4,128)S(1)} collective-permute-done((f32[4,4,512]{2,1,0:T(4,128)S(1)}, f32[4,4,512]{2,1,0:T(4,128)S(1)}, u32[]{:S(2)}, u32[]{:S(2)}) %collective-permute-start.10) | collective-permute-done | bytes 32800 | tf_op jit(solution)/shard_map/ppermute | solution.py:279
  206.2 1.5 collective-permute-start.11
  208.4 1.5 collective-permute-done.11
  211.4 14.1 %merge.1 = (bf16[2,208,256]{2,1,0:T(8,128)(2,1)}, bf16[2,208,256]{2,1,0:T(8,128)(2,1)}, bf16[2,208,256]{2,1,0:T(8,128)(2,1)}, bf16[2,208,256]{2,1,0:T(8,128)(2,1...) custom-call(s32[2]{0:T(128)} %pad_add_fusion.1.place_ref, ...), custom_call_target="tpu_custom_call" | custom-call | tf_op jit(solution)/shard_map/merge/pallas_call | solution.py:208
  225.4 1.2 collective-permute-start.17
  226.7 1.5 collective-permute-start.18
  228.1 1.6 collective-permute-start.12
  229.7 1.1 collective-permute-start.13
  231.3 2.7 collective-permute-start.14
  234.0 1.3 collective-permute-start.15
  235.3 0.9 slice.153
  236.3 2.8 %collective-permute-done.19.refs_7_ = bf16[2,208,256]{2,1,0:T(8,128)(2,1)S(1)} collective-permute-done((bf16[2,208,256]{2,1,0:T(8,128)(2,1)}, bf16[2,208,256]{2,1,0:T(8,128)(2,1)S(1)}, u32[]{:S(2)}, u32[]{:S(2)}) %collective-permute-start.19) | collective-permute-done | bytes 213024 | tf_op jit(solution)/shard_map/ppermute | solution.py:358
  239.1 9.1 %collective-permute-start.20 = (bf16[4,208,256]{2,1,0:T(8,128)(2,1)S(1)}, bf16[4,208,256]{2,1,0:T(8,128)(2,1)S(1)}, u32[]{:S(2)}, u32[]{:S(2)}) collective-permute-start(bf16[4,208,256]{2,1,0:T(8,128)(2,1)S(1)} %pad_maximum_fusion.7), channel_id=1, source_target_pairs={{0,2},{2,0},{4,6},{6,4},{1,3},{3,1},{5,7},{7,5},{8,10},{10,8},{12,... | collective-permute-start | bytes 1277960 | tf_op jit(solution)/shard_map/ppermute | solution.py:307
  248.3 10.3 %collective-permute-done.14.refs_2_ = bf16[2,208,256]{2,1,0:T(8,128)(2,1)S(1)} collective-permute-done((bf16[2,208,256]{2,1,0:T(8,128)(2,1)}, bf16[2,208,256]{2,1,0:T(8,128)(2,1)S(1)}, u32[]{:S(2)}, u32[]{:S(2)}) %collective-permute-start.14) | collective-permute-done | bytes 213024 | tf_op jit(solution)/shard_map/ppermute | solution.py:358
  258.6 4.6 %collective-permute-done.15.refs_3_ = bf16[2,208,256]{2,1,0:T(8,128)(2,1)S(1)} collective-permute-done((bf16[2,208,256]{2,1,0:T(8,128)(2,1)}, bf16[2,208,256]{2,1,0:T(8,128)(2,1)S(1)}, u32[]{:S(2)}, u32[]{:S(2)}) %collective-permute-start.15) | collective-permute-done | bytes 213024 | tf_op jit(solution)/shard_map/ppermute | solution.py:358
  263.2 4.4 %collective-permute-start.16 = (bf16[4,208,256]{2,1,0:T(8,128)(2,1)S(1)}, bf16[4,208,256]{2,1,0:T(8,128)(2,1)S(1)}, u32[]{:S(2)}, u32[]{:S(2)}) collective-permute-start(bf16[4,208,256]{2,1,0:T(8,128)(2,1)S(1)} %pad_maximum_fusion.6), channel_id=1, source_target_pairs={{0,2},{2,0},{4,6},{6,4},{1,3},{3,1},{5,7},{7,5},{8,10},{10,8},{12,... | collective-permute-start | bytes 1277960 | tf_op jit(solution)/shard_map/ppermute | solution.py:307
  267.6 1.4 collective-permute-done.16.refs_4_
  269.0 1.6 assemble.1
  (66 shorter events, 8.6 us)
Async XLA Ops:
  0.0 1.7 copy-start
  1.8 13.7 %collective-permute-start.2 = (bf16[1,64,2688]{2,1,0:T(8,128)(2,1)S(1)}, bf16[1,64,2688]{2,1,0:T(8,128)(2,1)S(1)}, u32[]{:S(2)}, u32[]{:S(2)}) collective-permute-start(bf16[1,64,2688]{2,1,0:T(8,128)(2,1)S(1)} %fusion.2), channel_id=1, source_target_pairs={{0,8},{8,0},{16,24},{24,16},{1,9},{9,1},{17,25},{25,17},{2,10},{10... | collective-permute-start | bytes 1032200 | tf_op jit(solution)/shard_map/ppermute | solution.py:307
  1.8 17.4 %collective-permute-start.1 = (bf16[1,64,2688]{2,1,0:T(8,128)(2,1)S(1)}, bf16[1,64,2688]{2,1,0:T(8,128)(2,1)S(1)}, u32[]{:S(2)}, u32[]{:S(2)}) collective-permute-start(bf16[1,64,2688]{2,1,0:T(8,128)(2,1)S(1)} %fusion.2), channel_id=1, source_target_pairs={{0,16},{8,24},{16,0},{24,8},{1,17},{9,25},{17,1},{25,9},{2,18},{10... | collective-permute-start | bytes 1032200 | tf_op jit(solution)/shard_map/ppermute | solution.py:307
  4.3 29.5 %collective-permute-start = (bf16[1,64,2688]{2,1,0:T(8,128)(2,1)S(1)}, bf16[1,64,2688]{2,1,0:T(8,128)(2,1)S(1)}, u32[]{:S(2)}, u32[]{:S(2)}) collective-permute-start(bf16[1,64,2688]{2,1,0:T(8,128)(2,1)S(1)} %fusion.2), channel_id=1, source_target_pairs={{0,24},{8,16},{16,8},{24,0},{1,25},{9,17},{17,9},{25,1},{2,26},{10... | collective-permute-start | bytes 1032200 | tf_op jit(solution)/shard_map/ppermute | solution.py:307
  34.2 46.5 %collective-permute-start.3 = (bf16[1,4,64,2688]{3,2,1,0:T(8,128)(2,1)S(1)}, bf16[1,4,64,2688]{3,2,1,0:T(8,128)(2,1)S(1)}, u32[]{:S(2)}, u32[]{:S(2)}) collective-permute-start(bf16[1,4,64,2688]{3,2,1,0:T(8,128)(2,1)S(1)} %maximum_bitcast_fusion), channel_id=1, source_target_pairs={{0,4},{2,6},{4,0},{6,2},{1,5},{3,7},{5,1},{7,3},{8,12},{10,14},{12... | collective-permute-start | bytes 4128776 | tf_op jit(solution)/shard_map/ppermute | solution.py:307
  35.5 146.9 %all-to-all-start = ((bf16[16,800,256]{2,1,0:T(8,128)(2,1)}), bf16[16,800,256]{2,1,0:T(8,128)(2,1)}, u32[]{:S(2)}, u32[]{:S(2)}) async-start(bf16[16,800,256]{2,1,0:T(8,128)(2,1)} %bitcast.282), calls=%async_computation | async-start | bytes 13107200 | tf_op jit(solution)/shard_map/all_to_all | solution.py:264
  41.6 40.4 %collective-permute-start.5 = (bf16[1,4,64,2688]{3,2,1,0:T(8,128)(2,1)S(1)}, bf16[1,4,64,2688]{3,2,1,0:T(8,128)(2,1)}, u32[]{:S(2)}, u32[]{:S(2)}) collective-permute-start(bf16[1,4,64,2688]{3,2,1,0:T(8,128)(2,1)S(1)} %maximum_bitcast_fusion), channel_id=1, source_target_pairs={{0,1},{1,0},{2,3},{3,2},{4,5},{5,4},{6,7},{7,6},{8,9},{9,8},{10,11... | collective-permute-start | bytes 4128776 | tf_op jit(solution)/shard_map/ppermute | solution.py:307
  80.7 26.7 %collective-permute-start.4 = (bf16[1,4,64,2688]{3,2,1,0:T(8,128)(2,1)S(1)}, bf16[1,4,64,2688]{3,2,1,0:T(8,128)(2,1)}, u32[]{:S(2)}, u32[]{:S(2)}) collective-permute-start(bf16[1,4,64,2688]{3,2,1,0:T(8,128)(2,1)S(1)} %collective-permute-done.3), channel_id=1, source_target_pairs={{0,1},{1,0},{2,3},{3,2},{4,5},{5,4},{6,7},{7,6},{8,9},{9,8},{10,11... | collective-permute-start | bytes 4128776 | tf_op jit(solution)/shard_map/ppermute | solution.py:307
  109.7 3.3 %copy-start.4 = (bf16[2,4,64,2688]{3,2,1,0:T(8,128)(2,1)}, bf16[2,4,64,2688]{3,2,1,0:T(8,128)(2,1)S(1)}, u32[]{:S(2)}) copy-start(bf16[2,4,64,2688]{3,2,1,0:T(8,128)(2,1)S(1)} %get-tuple-element.46) | copy-start | bytes 8257540
  109.7 4.1 %copy-start.5 = (bf16[2,4,64,2688]{3,2,1,0:T(8,128)(2,1)}, bf16[2,4,64,2688]{3,2,1,0:T(8,128)(2,1)S(1)}, u32[]{:S(2)}) copy-start(bf16[2,4,64,2688]{3,2,1,0:T(8,128)(2,1)S(1)} %get-tuple-element.47) | copy-start | bytes 8257540
  113.8 15.0 %collective-permute-start.6 = (bf16[4,4,64,2688]{3,2,1,0:T(8,128)(2,1)}, bf16[4,4,64,2688]{3,2,1,0:T(8,128)(2,1)}, u32[]{:S(2)}, u32[]{:S(2)}) collective-permute-start(bf16[4,4,64,2688]{3,2,1,0:T(8,128)(2,1)} %pad_maximum_fusion.1), channel_id=1, source_target_pairs={{0,2},{2,0},{4,6},{6,4},{1,3},{3,1},{5,7},{7,5},{8,10},{10,8},{12,... | collective-permute-start | bytes 16515080 | tf_op jit(solution)/shard_map/ppermute | solution.py:307
  133.8 2.4 copy-start.3
  182.4 27.5 %copy-start.6 = (f32[4,1,512]{2,1,0:T(1,128)S(1)}, f32[4,1,512]{2,1,0:T(1,128)}, u32[]{:S(2)}) copy-start(f32[4,1,512]{2,1,0:T(1,128)} %get-tuple-element.20) | copy-start | bytes 24580
  194.3 1.9 collective-permute-start.7
  196.3 4.2 %collective-permute-start.8 = (f32[4,4,512]{2,1,0:T(4,128)S(1)}, f32[4,4,512]{2,1,0:T(4,128)S(1)}, u32[]{:S(2)}, u32[]{:S(2)}) collective-permute-start(f32[4,4,512]{2,1,0:T(4,128)S(1)} %pad_maximum_fusion.8), channel_id=1, source_target_pairs={{0,4},{2,6},{4,0},{6,2},{1,5},{3,7},{5,1},{7,3},{8,12},{10,14},{12... | collective-permute-start | bytes 98312 | tf_op jit(solution)/shard_map/ppermute | solution.py:279
  200.5 2.8 %collective-permute-start.9 = (f32[4,4,512]{2,1,0:T(4,128)S(1)}, f32[4,4,512]{2,1,0:T(4,128)S(1)}, u32[]{:S(2)}, u32[]{:S(2)}) collective-permute-start(f32[4,4,512]{2,1,0:T(4,128)S(1)} %pad_maximum_fusion.9), channel_id=1, source_target_pairs={{0,1},{1,0},{2,3},{3,2},{4,5},{5,4},{6,7},{7,6},{8,9},{9,8},{10,11... | collective-permute-start | bytes 98312 | tf_op jit(solution)/shard_map/ppermute | solution.py:279
  203.4 2.8 %collective-permute-start.10 = (f32[4,4,512]{2,1,0:T(4,128)S(1)}, f32[4,4,512]{2,1,0:T(4,128)S(1)}, u32[]{:S(2)}, u32[]{:S(2)}) collective-permute-start(f32[4,4,512]{2,1,0:T(4,128)S(1)} %pad_maximum_fusion.10), channel_id=1, source_target_pairs={{0,8},{8,0},{16,24},{24,16},{1,9},{9,1},{17,25},{25,17},{2,10},{10... | collective-permute-start | bytes 98312 | tf_op jit(solution)/shard_map/ppermute | solution.py:279
  206.2 3.7 %collective-permute-start.11 = (f32[4,4,512]{2,1,0:T(4,128)S(1)}, f32[4,4,512]{2,1,0:T(4,128)S(1)}, u32[]{:S(2)}, u32[]{:S(2)}) collective-permute-start(f32[4,4,512]{2,1,0:T(4,128)S(1)} %pad_maximum_fusion.11), channel_id=1, source_target_pairs={{0,16},{8,24},{16,0},{24,8},{1,17},{9,25},{17,1},{25,9},{2,18},{10... | collective-permute-start | bytes 98312 | tf_op jit(solution)/shard_map/ppermute | solution.py:279
  225.4 43.5 %copy-start.2 = (bf16[2,208,256]{2,1,0:T(8,128)(2,1)S(1)}, bf16[2,208,256]{2,1,0:T(8,128)(2,1)}, u32[]{:S(2)}) copy-start(bf16[2,208,256]{2,1,0:T(8,128)(2,1)} %get-tuple-element.32.refs_8_) | copy-start | bytes 638980
  225.4 5.9 %collective-permute-start.17 = (bf16[2,208,256]{2,1,0:T(8,128)(2,1)}, bf16[2,208,256]{2,1,0:T(8,128)(2,1)S(1)}, u32[]{:S(2)}, u32[]{:S(2)}) collective-permute-start(bf16[2,208,256]{2,1,0:T(8,128)(2,1)} %get-tuple-element.29), channel_id=1, source_target_pairs={{0,12},{2,14},{4,8},{6,10},{8,4},{10,6},{12,0},{14,2},{16,28},{18,... | collective-permute-start | bytes 638984 | tf_op jit(solution)/shard_map/ppermute | solution.py:358
  226.7 7.4 %collective-permute-start.18 = (bf16[2,208,256]{2,1,0:T(8,128)(2,1)}, bf16[2,208,256]{2,1,0:T(8,128)(2,1)S(1)}, u32[]{:S(2)}, u32[]{:S(2)}) collective-permute-start(bf16[2,208,256]{2,1,0:T(8,128)(2,1)} %get-tuple-element.30), channel_id=1, source_target_pairs={{0,8},{2,10},{4,12},{6,14},{8,0},{10,2},{12,4},{14,6},{16,24},{18,... | collective-permute-start | bytes 638984 | tf_op jit(solution)/shard_map/ppermute | solution.py:358
  228.1 10.9 %collective-permute-start.19 = (bf16[2,208,256]{2,1,0:T(8,128)(2,1)}, bf16[2,208,256]{2,1,0:T(8,128)(2,1)S(1)}, u32[]{:S(2)}, u32[]{:S(2)}) collective-permute-start(bf16[2,208,256]{2,1,0:T(8,128)(2,1)} %get-tuple-element.31), channel_id=1, source_target_pairs={{0,4},{2,6},{4,0},{6,2},{8,12},{10,14},{12,8},{14,10},{16,20},{18,... | collective-permute-start | bytes 638984 | tf_op jit(solution)/shard_map/ppermute | solution.py:358
  228.1 20.1 %collective-permute-start.12 = (bf16[2,208,256]{2,1,0:T(8,128)(2,1)}, bf16[2,208,256]{2,1,0:T(8,128)(2,1)S(1)}, u32[]{:S(2)}, u32[]{:S(2)}) collective-permute-start(bf16[2,208,256]{2,1,0:T(8,128)(2,1)} %get-tuple-element.25), channel_id=1, source_target_pairs={{0,28},{2,30},{4,24},{6,26},{8,20},{10,22},{12,16},{14,18},{16,12}... | collective-permute-start | bytes 638984 | tf_op jit(solution)/shard_map/ppermute | solution.py:358
  229.7 18.5 %collective-permute-start.13 = (bf16[2,208,256]{2,1,0:T(8,128)(2,1)}, bf16[2,208,256]{2,1,0:T(8,128)(2,1)S(1)}, u32[]{:S(2)}, u32[]{:S(2)}) collective-permute-start(bf16[2,208,256]{2,1,0:T(8,128)(2,1)} %get-tuple-element.26), channel_id=1, source_target_pairs={{0,24},{2,26},{4,28},{6,30},{8,16},{10,18},{12,20},{14,22},{16,8},... | collective-permute-start | bytes 638984 | tf_op jit(solution)/shard_map/ppermute | solution.py:358
  231.3 27.2 %collective-permute-start.14 = (bf16[2,208,256]{2,1,0:T(8,128)(2,1)}, bf16[2,208,256]{2,1,0:T(8,128)(2,1)S(1)}, u32[]{:S(2)}, u32[]{:S(2)}) collective-permute-start(bf16[2,208,256]{2,1,0:T(8,128)(2,1)} %get-tuple-element.27), channel_id=1, source_target_pairs={{0,20},{2,22},{4,16},{6,18},{8,28},{10,30},{12,24},{14,26},{16,4},... | collective-permute-start | bytes 638984 | tf_op jit(solution)/shard_map/ppermute | solution.py:358
  234.0 29.1 %collective-permute-start.15 = (bf16[2,208,256]{2,1,0:T(8,128)(2,1)}, bf16[2,208,256]{2,1,0:T(8,128)(2,1)S(1)}, u32[]{:S(2)}, u32[]{:S(2)}) collective-permute-start(bf16[2,208,256]{2,1,0:T(8,128)(2,1)} %get-tuple-element.28), channel_id=1, source_target_pairs={{0,16},{2,18},{4,20},{6,22},{8,24},{10,26},{12,28},{14,30},{16,0},... | collective-permute-start | bytes 638984 | tf_op jit(solution)/shard_map/ppermute | solution.py:358
  239.1 28.4 %collective-permute-start.20 = (bf16[4,208,256]{2,1,0:T(8,128)(2,1)S(1)}, bf16[4,208,256]{2,1,0:T(8,128)(2,1)S(1)}, u32[]{:S(2)}, u32[]{:S(2)}) collective-permute-start(bf16[4,208,256]{2,1,0:T(8,128)(2,1)S(1)} %pad_maximum_fusion.7), channel_id=1, source_target_pairs={{0,2},{2,0},{4,6},{6,4},{1,3},{3,1},{5,7},{7,5},{8,10},{10,8},{12,... | collective-permute-start | bytes 1277960 | tf_op jit(solution)/shard_map/ppermute | solution.py:307
  248.2 22.3 %copy-start.1 = (bf16[1,128,2560]{2,1,0:T(8,128)(2,1)S(1)}, bf16[1,128,2560]{2,1,0:T(8,128)(2,1)}, u32[]{:S(2)}) copy-start(bf16[1,128,2560]{2,1,0:T(8,128)(2,1)} %param.4) | copy-start | bytes 1966084
  263.2 5.8 %collective-permute-start.16 = (bf16[4,208,256]{2,1,0:T(8,128)(2,1)S(1)}, bf16[4,208,256]{2,1,0:T(8,128)(2,1)S(1)}, u32[]{:S(2)}, u32[]{:S(2)}) collective-permute-start(bf16[4,208,256]{2,1,0:T(8,128)(2,1)S(1)} %pad_maximum_fusion.6), channel_id=1, source_target_pairs={{0,2},{2,0},{4,6},{6,4},{1,3},{3,1},{5,7},{7,5},{8,10},{10,8},{12,... | collective-permute-start | bytes 1277960 | tf_op jit(solution)/shard_map/ppermute | solution.py:307

commit v5 on v4

--- a/solution.py
+++ b/solution.py
@@ -9,7 +9,7 @@
 from jax.sharding import PartitionSpec as P
 
 prior_weight = 0.05
-VMEM = 56 * 1024 * 1024
+VMEM = 30 * 1024 * 1024
 BOTH = ("ckpt", "tok")
 
 
@@ -17,6 +17,10 @@
     return pl.pallas_call(
         kernel, name=name, compiler_params=pltpu.CompilerParams(vmem_limit_bytes=vmem), **options
     )
+
+
+def in_hbm(x):
+    return pltpu.with_memory_space_constraint(x, pltpu.HBM)
 
 
 def pack_kernel(*refs):
@@ -47,7 +51,7 @@
         grid=(steps,),
         in_specs=[part(q) for q in range(fold)],
         out_specs=pl.BlockSpec((peers, fold + 1, tall, wide), lambda i: (0, 0, i, 0)),
-    )(*([rows] * fold))
+    )(*([in_hbm(rows)] * fold))
     return out.reshape(peers, depth + height, wide)
 
 
@@ -127,7 +131,7 @@
     return call(
         score_kernel, "score",
         out_shape=(
-            jax.ShapeDtypeStruct((ckpts, tokens, lanes), jnp.float32),
+            pltpu.HBM((ckpts, tokens, lanes), jnp.float32),
             jax.ShapeDtypeStruct((ckpts, 8, tokens), jnp.float32),
         ),
         grid=(ckpts,),
@@ -141,7 +145,7 @@
             pl.BlockSpec((1, tokens, lanes), lambda c: (c, 0, 0)),
             pl.BlockSpec((1, 8, tokens), lambda c: (c, 0, 0)),
         ),
-    )(states, heads, labels, ids)
+    )(in_hbm(states), in_hbm(heads), labels, ids)
 
 
 def merge_kernel(
@@ -224,7 +228,7 @@
                 pltpu.VMEM((ckpts, tokens, lanes), jnp.bfloat16),
             ],
         ),
-    )(place, scales, logits, table, labels, ids, hidden_sq, heads)
+    )(place, scales, in_hbm(logits), table, labels, ids, hidden_sq, in_hbm(heads))
 
 
 def assemble_kernel(mine_ref, *refs, sources):
@@ -249,7 +253,7 @@
 
 def assemble(mine, arrays, sources, own, columns):
     return call(
-        functools.partial(assemble_kernel, sources=sources), "assemble", VMEM // 2,
+        functools.partial(assemble_kernel, sources=sources), "assemble",
         out_shape=jax.ShapeDtypeStruct((own, columns), jnp.bfloat16),
         in_specs=[pl.BlockSpec(memory_space=pltpu.SMEM)] + [pl.BlockSpec(memory_space=pltpu.VMEM)] * len(arrays),
         out_specs=pl.BlockSpec(memory_space=pltpu.VMEM),

time: 275 us -> 272 us (0.989)
  waiting for transfers between devices: 144 us -> 161 us
  Pallas kernels: 48.9 us -> 36.3 us
  other arithmetic: 23.9 us -> 15.8 us
    all_to_all x1, waiting for transfers between devices: 24.4 us -> 38.7 us  [exchange(): return lax.all_to_all(x, BOTH, 0, 0, tiled=True)]
    pallas_call x1, Pallas kernels: 14.7 us -> 5.83 us  [squares(): call(square_kernel, 'squares', out_shape=(jax.ShapeDtypeStruct((ckpts, fe...]
    concatenate x3, other arithmetic: 9.51 us -> 4.53 us  [paired(): return jnp.concatenate([jnp.where(upper, y, x), jnp.where(upper, x, y)])]
    unnamed x14 -> x18, local copies, waits for them, and re-layouts: 3.13 us -> 6.56 us
    pallas_call x1, Pallas kernels: 7.56 us -> 4.76 us  [pack(): call(pack_kernel, 'pack', out_shape=jax.ShapeDtypeStruct((peers, fold + 1...]
  transfers between devices with their start and end apart: 22 -> 22, of which waited for: 17 -> 17; matrix products, arithmetic and copies ran while one was open for 8% -> 5% of each run, Pallas kernels for 8% -> 4%
where the time goes in v5:
time: 272 us; the launch traced here: 267 us
  waiting for transfers between devices  161 us (59%)
  starting transfers between devices  47.2 us (17%)
  Pallas kernels  36.3 us (13%)
  other arithmetic  15.8 us (6%)
  local copies, waits for them, and re-layouts  6.83 us (3%)
    ppermute x9, waiting for transfers between devices, other(): lax.ppermute(x, axis, [(i, i ^ far) for i in range(lax.axis_size(axis))])  93.8 us
    all_to_all x1, waiting for transfers between devices, exchange(): return lax.all_to_all(x, BOTH, 0, 0, tiled=True)  38.7 us
    ppermute x9, starting transfers between devices, other(): lax.ppermute(x, axis, [(i, i ^ far) for i in range(lax.axis_size(axis))])  25.1 us
    ppermute x7, waiting for transfers between devices, shards(): part = lax.ppermute(part, BOTH, [(g, g ^ r) for g in range(peers)])  19.6 us
    pallas_call x1, Pallas kernels, score(): call(score_kernel, 'score', out_shape=(pltpu.HBM((ckpts, tokens, lanes),...  12 us
    pallas_call x1, Pallas kernels, merge(): call(functools.partial(merge_kernel, prior=prior), 'merge', out_shape=[ja...  12 us
    ppermute x7, starting transfers between devices, shards(): part = lax.ppermute(part, BOTH, [(g, g ^ r) for g in range(peers)])  9.36 us
    select_n x7, other arithmetic, paired(): return jnp.concatenate([jnp.where(upper, y, x), jnp.where(upper, x, y)])  8.7 us
  transfers between devices with their start and end apart: 22, of which 17 were waited for; matrix products, arithmetic and copies ran while one was open for 5% of the time, Pallas kernels for 4%

profile of v5, /device:TPU:9, one launch (start us, length us, event | category | flops | bytes accessed | tf_op | source)
XLA Modules:
  0.0 267.3 jit_solution(2552556312632963558)
XLA Ops:
  0.0 0.8 fusion.46
  0.8 0.7 fusion.48
  1.8 2.5 collective-permute-start.1
  4.5 4.8 %pack.1 = bf16[16,5,160,256]{3,2,1,0:T(8,128)(2,1)S(1)} custom-call(bf16[640,5120]{1,0:T(8,128)(2,1)} %bitcast.281, bf16[640,5120]{1,0:T(8,128)(2,1)} %bitcast.282, bf16[640,5120]{1,0:T(8,128)(2,1)} %bitcast.283, bf16[640,5120]{1,0:T(8,128)(2,1)} %bitcast.284), custom_call_target="tpu_custom_call" | custom-call | tf_op jit(solution)/shard_map/pack/pallas_call | solution.py:48
  9.2 2.7 %copy-done.3 = bf16[16,5,160,256]{3,2,1,0:T(8,128)(2,1)} copy-done((bf16[16,5,160,256]{3,2,1,0:T(8,128)(2,1)}, bf16[16,5,160,256]{3,2,1,0:T(8,128)(2,1)S(1)}, u32[]{:S(2)}) %copy-start.3) | copy-done | bytes 6553624
  11.9 3.5 %collective-permute-done.2 = bf16[1,64,2688]{2,1,0:T(8,128)(2,1)S(1)} collective-permute-done((bf16[1,64,2688]{2,1,0:T(8,128)(2,1)S(1)}, bf16[1,64,2688]{2,1,0:T(8,128)(2,1)S(1)}, u32[]{:S(2)}, u32[]{:S(2)}) %collective-permute-start.2) | collective-permute-done | bytes 344096 | tf_op jit(solution)/shard_map/ppermute | solution.py:311
  15.6 3.6 %collective-permute-done.1 = bf16[1,64,2688]{2,1,0:T(8,128)(2,1)S(1)} collective-permute-done((bf16[1,64,2688]{2,1,0:T(8,128)(2,1)S(1)}, bf16[1,64,2688]{2,1,0:T(8,128)(2,1)S(1)}, u32[]{:S(2)}, u32[]{:S(2)}) %collective-permute-start.1) | collective-permute-done | bytes 344096 | tf_op jit(solution)/shard_map/ppermute | solution.py:311
  19.2 14.6 %collective-permute-done = bf16[1,64,2688]{2,1,0:T(8,128)(2,1)S(1)} collective-permute-done((bf16[1,64,2688]{2,1,0:T(8,128)(2,1)S(1)}, bf16[1,64,2688]{2,1,0:T(8,128)(2,1)S(1)}, u32[]{:S(2)}, u32[]{:S(2)}) %collective-permute-start) | collective-permute-done | bytes 344096 | tf_op jit(solution)/shard_map/ppermute | solution.py:311
  34.2 1.3 collective-permute-start.3
  35.5 6.1 %all-to-all-start = ((bf16[16,800,256]{2,1,0:T(8,128)(2,1)}), bf16[16,800,256]{2,1,0:T(8,128)(2,1)}, u32[]{:S(2)}, u32[]{:S(2)}) async-start(bf16[16,800,256]{2,1,0:T(8,128)(2,1)} %bitcast.278), calls=%async_computation | async-start | bytes 13107200 | tf_op jit(solution)/shard_map/all_to_all | solution.py:268
  41.6 1.2 collective-permute-start.5
  42.8 37.9 %collective-permute-done.3 = bf16[1,4,64,2688]{3,2,1,0:T(8,128)(2,1)S(1)} collective-permute-done((bf16[1,4,64,2688]{3,2,1,0:T(8,128)(2,1)S(1)}, bf16[1,4,64,2688]{3,2,1,0:T(8,128)(2,1)S(1)}, u32[]{:S(2)}, u32[]{:S(2)}) %collective-permute-start.3) | collective-permute-done | bytes 1376288 | tf_op jit(solution)/shard_map/ppermute | solution.py:311
  80.7 1.2 collective-permute-start.4
  82.0 1.6 broadcast_select_fusion.5
  83.6 23.9 %collective-permute-done.4 = bf16[1,4,64,2688]{3,2,1,0:T(8,128)(2,1)} collective-permute-done((bf16[1,4,64,2688]{3,2,1,0:T(8,128)(2,1)S(1)}, bf16[1,4,64,2688]{3,2,1,0:T(8,128)(2,1)}, u32[]{:S(2)}, u32[]{:S(2)}) %collective-permute-start.4) | collective-permute-done | bytes 1376288 | tf_op jit(solution)/shard_map/ppermute | solution.py:311
  107.4 1.6 broadcast_select_fusion.7
  109.7 3.3 %pad_maximum_fusion.1 = bf16[4,4,64,2688]{3,2,1,0:T(8,128)(2,1)} fusion(bf16[2,4,64,2688]{3,2,1,0:T(8,128)(2,1)S(1)} %get-tuple-element.47, bf16[2,4,64,2688]{3,2,1,0:T(8,128)(2,1)S(1)} %get-tuple-element.46), kind=kLoop, calls=%fused_computation.3 | loop fusion | flops 2752512 | bytes 11010048 | tf_op jit(solution)/shard_map/concatenate | solution.py:315
  113.0 6.0 %collective-permute-start.6 = (bf16[4,4,64,2688]{3,2,1,0:T(8,128)(2,1)}, bf16[4,4,64,2688]{3,2,1,0:T(8,128)(2,1)}, u32[]{:S(2)}, u32[]{:S(2)}) collective-permute-start(bf16[4,4,64,2688]{3,2,1,0:T(8,128)(2,1)} %pad_maximum_fusion.1), channel_id=1, source_target_pairs={{0,2},{2,0},{4,6},{6,4},{1,3},{3,1},{5,7},{7,5},{8,10},{10,8},{12,... | collective-permute-start | bytes 16515080 | tf_op jit(solution)/shard_map/ppermute | solution.py:311
  119.1 8.9 %collective-permute-done.6 = bf16[4,4,64,2688]{3,2,1,0:T(8,128)(2,1)} collective-permute-done((bf16[4,4,64,2688]{3,2,1,0:T(8,128)(2,1)}, bf16[4,4,64,2688]{3,2,1,0:T(8,128)(2,1)}, u32[]{:S(2)}, u32[]{:S(2)}) %collective-permute-start.6) | collective-permute-done | bytes 5505056 | tf_op jit(solution)/shard_map/ppermute | solution.py:311
  128.0 4.4 %broadcast_select_fusion.1 = (bf16[4,4,64,2688]{3,2,1,0:T(8,128)(2,1)S(1)}, bf16[4,4,64,2688]{3,2,1,0:T(8,128)(2,1)S(1)}) fusion(bf16[4,4,64,2688]{3,2,1,0:T(8,128)(2,1)} %collective-permute-done.6, pred[]{:T(512)S(6)} %eq.28, bf16[2,4,64,2688]{3,2,1,0:T(8,128)(2,1)} %copy-done.5, bf16[2,4,64,2688]{3,2,1,0:T(8,128)(2,1)S(1)} %get-tuple-element.46), kind=kLoop, calls=%fused_computation.5 | loop fusion | flops 8257536 | bytes 22020096 | tf_op jit(solution)/shard_map/jit(_where)/select_n | solution.py:315
  132.5 1.2 pad_maximum_fusion.states_ref
  133.7 5.8 %squares.1 = (bf16[4,2560,512]{2,1,0:T(8,128)(2,1)S(1)}, f32[4,1,512]{2,1,0:T(1,128)S(1)}) custom-call(bf16[8,4,64,2688]{3,2,1,0:T(8,128)(2,1)S(1)} %pad_maximum_fusion.states_ref), custom_call_target="tpu_custom_call" | custom-call | tf_op jit(solution)/shard_map/squares/pallas_call | solution.py:79
  139.6 3.8 %copy-done.4 = bf16[4,2560,512]{2,1,0:T(8,128)(2,1)} copy-done((bf16[4,2560,512]{2,1,0:T(8,128)(2,1)}, bf16[4,2560,512]{2,1,0:T(8,128)(2,1)S(1)}, u32[]{:S(2)}) %copy-start.4) | copy-done | bytes 10485784
  143.7 38.7 %all-to-all-done = bf16[16,800,256]{2,1,0:T(8,128)(2,1)} async-done(((bf16[16,800,256]{2,1,0:T(8,128)(2,1)}), bf16[16,800,256]{2,1,0:T(8,128)(2,1)}, u32[]{:S(2)}, u32[]{:S(2)}) %all-to-all-start) | async-done | bytes 6553632 | tf_op jit(solution)/shard_map/all_to_all | solution.py:268
  182.5 12.0 %score.1 = (f32[4,512,384]{2,1,0:T(8,128)}, f32[4,8,512]{2,1,0:T(8,128)S(1)}) custom-call(bf16[8,4,64,2688]{3,2,1,0:T(8,128)(2,1)} %copy-done.2, bf16[4,4,800,256]{3,2,1,0:T(8,128)(2,1)} %bitcast.11.heads_ref, s32[512,1]{1,0:T(8,128)S(1)} %fusion.3.labels_ref, s32[1,384]{1,0:T(1,128)S(1)} %broadcast_in_dim.17.ids_ref), custom_call_target="tpu_custom_call" | custom-call | tf_op jit(solution)/shard_map/score/pallas_call | solution.py:131
  194.6 1.0 collective-permute-start.7
  195.6 0.9 collective-permute-done.7
  196.5 2.8 %collective-permute-start.8 = (f32[4,4,512]{2,1,0:T(4,128)S(1)}, f32[4,4,512]{2,1,0:T(4,128)S(1)}, u32[]{:S(2)}, u32[]{:S(2)}) collective-permute-start(f32[4,4,512]{2,1,0:T(4,128)S(1)} %pad_maximum_fusion.8), channel_id=1, source_target_pairs={{0,4},{2,6},{4,0},{6,2},{1,5},{3,7},{5,1},{7,3},{8,12},{10,14},{12... | collective-permute-start | bytes 98312 | tf_op jit(solution)/shard_map/ppermute | solution.py:283
  199.3 1.3 collective-permute-done.8
  200.7 1.3 collective-permute-start.9
  202.0 1.5 collective-permute-done.9
  203.7 2.8 %collective-permute-done.10 = f32[4,4,512]{2,1,0:T(4,128)S(1)} collective-permute-done((f32[4,4,512]{2,1,0:T(4,128)S(1)}, f32[4,4,512]{2,1,0:T(4,128)S(1)}, u32[]{:S(2)}, u32[]{:S(2)}) %collective-permute-start.10) | collective-permute-done | bytes 32800 | tf_op jit(solution)/shard_map/ppermute | solution.py:283
  206.5 1.5 collective-permute-start.11
  208.1 2.1 collective-permute-done.11
  210.5 12.0 %merge.1 = (bf16[2,208,256]{2,1,0:T(8,128)(2,1)S(1)}, bf16[2,208,256]{2,1,0:T(8,128)(2,1)S(1)}, bf16[2,208,256]{2,1,0:T(8,128)(2,1)S(1)}, bf16[2,208,256]{2,1,0:...) custom-call(s32[2]{0:T(128)S(1)} %pad_add_fusion.1.place_ref, ...), custom_call_target="tpu_custom_call" | custom-call | tf_op jit(solution)/shard_map/merge/pallas_call | solution.py:212
  222.5 1.3 collective-permute-start.17
  223.7 1.5 collective-permute-start.18
  225.2 1.6 collective-permute-start.12
  226.8 1.1 collective-permute-start.13
  228.2 2.7 %collective-permute-start.14 = (bf16[2,208,256]{2,1,0:T(8,128)(2,1)S(1)}, bf16[2,208,256]{2,1,0:T(8,128)(2,1)S(1)}, u32[]{:S(2)}, u32[]{:S(2)}) collective-permute-start(bf16[2,208,256]{2,1,0:T(8,128)(2,1)S(1)} %get-tuple-element.27), channel_id=1, source_target_pairs={{0,20},{2,22},{4,16},{6,18},{8,28},{10,30},{12,24},{14,26},{16,4},... | collective-permute-start | bytes 638984 | tf_op jit(solution)/shard_map/ppermute | solution.py:362
  230.9 1.3 collective-permute-start.15
  232.3 3.7 %collective-permute-done.19.refs_7_ = bf16[2,208,256]{2,1,0:T(8,128)(2,1)S(1)} collective-permute-done((bf16[2,208,256]{2,1,0:T(8,128)(2,1)S(1)}, bf16[2,208,256]{2,1,0:T(8,128)(2,1)S(1)}, u32[]{:S(2)}, u32[]{:S(2)}) %collective-permute-start.19) | collective-permute-done | bytes 213024 | tf_op jit(solution)/shard_map/ppermute | solution.py:362
  236.0 8.2 %collective-permute-start.20 = (bf16[4,208,256]{2,1,0:T(8,128)(2,1)S(1)}, bf16[4,208,256]{2,1,0:T(8,128)(2,1)S(1)}, u32[]{:S(2)}, u32[]{:S(2)}) collective-permute-start(bf16[4,208,256]{2,1,0:T(8,128)(2,1)S(1)} %pad_maximum_fusion.7), channel_id=1, source_target_pairs={{0,2},{2,0},{4,6},{6,4},{1,3},{3,1},{5,7},{7,5},{8,10},{10,8},{12,... | collective-permute-start | bytes 1277960 | tf_op jit(solution)/shard_map/ppermute | solution.py:311
  244.3 11.0 %collective-permute-done.14.refs_2_ = bf16[2,208,256]{2,1,0:T(8,128)(2,1)S(1)} collective-permute-done((bf16[2,208,256]{2,1,0:T(8,128)(2,1)S(1)}, bf16[2,208,256]{2,1,0:T(8,128)(2,1)S(1)}, u32[]{:S(2)}, u32[]{:S(2)}) %collective-permute-start.14) | collective-permute-done | bytes 213024 | tf_op jit(solution)/shard_map/ppermute | solution.py:362
  255.3 4.6 %collective-permute-done.15.refs_3_ = bf16[2,208,256]{2,1,0:T(8,128)(2,1)S(1)} collective-permute-done((bf16[2,208,256]{2,1,0:T(8,128)(2,1)S(1)}, bf16[2,208,256]{2,1,0:T(8,128)(2,1)S(1)}, u32[]{:S(2)}, u32[]{:S(2)}) %collective-permute-start.15) | collective-permute-done | bytes 213024 | tf_op jit(solution)/shard_map/ppermute | solution.py:362
  260.0 4.4 %collective-permute-start.16 = (bf16[4,208,256]{2,1,0:T(8,128)(2,1)S(1)}, bf16[4,208,256]{2,1,0:T(8,128)(2,1)S(1)}, u32[]{:S(2)}, u32[]{:S(2)}) collective-permute-start(bf16[4,208,256]{2,1,0:T(8,128)(2,1)S(1)} %pad_maximum_fusion.6), channel_id=1, source_target_pairs={{0,2},{2,0},{4,6},{6,4},{1,3},{3,1},{5,7},{7,5},{8,10},{10,8},{12,... | collective-permute-start | bytes 1277960 | tf_op jit(solution)/shard_map/ppermute | solution.py:311
  264.3 1.4 collective-permute-done.16.refs_4_
  265.7 1.6 assemble.1
  (71 shorter events, 3.1 us)
Async XLA Ops:
  0.0 1.7 copy-start
  1.8 13.7 %collective-permute-start.2 = (bf16[1,64,2688]{2,1,0:T(8,128)(2,1)S(1)}, bf16[1,64,2688]{2,1,0:T(8,128)(2,1)S(1)}, u32[]{:S(2)}, u32[]{:S(2)}) collective-permute-start(bf16[1,64,2688]{2,1,0:T(8,128)(2,1)S(1)} %fusion.2), channel_id=1, source_target_pairs={{0,8},{8,0},{16,24},{24,16},{1,9},{9,1},{17,25},{25,17},{2,10},{10... | collective-permute-start | bytes 1032200 | tf_op jit(solution)/shard_map/ppermute | solution.py:311
  1.8 17.4 %collective-permute-start.1 = (bf16[1,64,2688]{2,1,0:T(8,128)(2,1)S(1)}, bf16[1,64,2688]{2,1,0:T(8,128)(2,1)S(1)}, u32[]{:S(2)}, u32[]{:S(2)}) collective-permute-start(bf16[1,64,2688]{2,1,0:T(8,128)(2,1)S(1)} %fusion.2), channel_id=1, source_target_pairs={{0,16},{8,24},{16,0},{24,8},{1,17},{9,25},{17,1},{25,9},{2,18},{10... | collective-permute-start | bytes 1032200 | tf_op jit(solution)/shard_map/ppermute | solution.py:311
  4.3 29.5 %collective-permute-start = (bf16[1,64,2688]{2,1,0:T(8,128)(2,1)S(1)}, bf16[1,64,2688]{2,1,0:T(8,128)(2,1)S(1)}, u32[]{:S(2)}, u32[]{:S(2)}) collective-permute-start(bf16[1,64,2688]{2,1,0:T(8,128)(2,1)S(1)} %fusion.2), channel_id=1, source_target_pairs={{0,24},{8,16},{16,8},{24,0},{1,25},{9,17},{17,9},{25,1},{2,26},{10... | collective-permute-start | bytes 1032200 | tf_op jit(solution)/shard_map/ppermute | solution.py:311
  9.2 2.7 %copy-start.3 = (bf16[16,5,160,256]{3,2,1,0:T(8,128)(2,1)}, bf16[16,5,160,256]{3,2,1,0:T(8,128)(2,1)S(1)}, u32[]{:S(2)}) copy-start(bf16[16,5,160,256]{3,2,1,0:T(8,128)(2,1)S(1)} %pack.1) | copy-start | bytes 19660804
  34.2 46.5 %collective-permute-start.3 = (bf16[1,4,64,2688]{3,2,1,0:T(8,128)(2,1)S(1)}, bf16[1,4,64,2688]{3,2,1,0:T(8,128)(2,1)S(1)}, u32[]{:S(2)}, u32[]{:S(2)}) collective-permute-start(bf16[1,4,64,2688]{3,2,1,0:T(8,128)(2,1)S(1)} %maximum_bitcast_fusion), channel_id=1, source_target_pairs={{0,4},{2,6},{4,0},{6,2},{1,5},{3,7},{5,1},{7,3},{8,12},{10,14},{12... | collective-permute-start | bytes 4128776 | tf_op jit(solution)/shard_map/ppermute | solution.py:311
  35.5 146.9 %all-to-all-start = ((bf16[16,800,256]{2,1,0:T(8,128)(2,1)}), bf16[16,800,256]{2,1,0:T(8,128)(2,1)}, u32[]{:S(2)}, u32[]{:S(2)}) async-start(bf16[16,800,256]{2,1,0:T(8,128)(2,1)} %bitcast.278), calls=%async_computation | async-start | bytes 13107200 | tf_op jit(solution)/shard_map/all_to_all | solution.py:268
  41.6 40.4 %collective-permute-start.5 = (bf16[1,4,64,2688]{3,2,1,0:T(8,128)(2,1)S(1)}, bf16[1,4,64,2688]{3,2,1,0:T(8,128)(2,1)}, u32[]{:S(2)}, u32[]{:S(2)}) collective-permute-start(bf16[1,4,64,2688]{3,2,1,0:T(8,128)(2,1)S(1)} %maximum_bitcast_fusion), channel_id=1, source_target_pairs={{0,1},{1,0},{2,3},{3,2},{4,5},{5,4},{6,7},{7,6},{8,9},{9,8},{10,11... | collective-permute-start | bytes 4128776 | tf_op jit(solution)/shard_map/ppermute | solution.py:311
  80.7 26.7 %collective-permute-start.4 = (bf16[1,4,64,2688]{3,2,1,0:T(8,128)(2,1)S(1)}, bf16[1,4,64,2688]{3,2,1,0:T(8,128)(2,1)}, u32[]{:S(2)}, u32[]{:S(2)}) collective-permute-start(bf16[1,4,64,2688]{3,2,1,0:T(8,128)(2,1)S(1)} %collective-permute-done.3), channel_id=1, source_target_pairs={{0,1},{1,0},{2,3},{3,2},{4,5},{5,4},{6,7},{7,6},{8,9},{9,8},{10,11... | collective-permute-start | bytes 4128776 | tf_op jit(solution)/shard_map/ppermute | solution.py:311
  109.7 3.3 %copy-start.5 = (bf16[2,4,64,2688]{3,2,1,0:T(8,128)(2,1)}, bf16[2,4,64,2688]{3,2,1,0:T(8,128)(2,1)S(1)}, u32[]{:S(2)}) copy-start(bf16[2,4,64,2688]{3,2,1,0:T(8,128)(2,1)S(1)} %get-tuple-element.47) | copy-start | bytes 8257540
  113.0 15.0 %collective-permute-start.6 = (bf16[4,4,64,2688]{3,2,1,0:T(8,128)(2,1)}, bf16[4,4,64,2688]{3,2,1,0:T(8,128)(2,1)}, u32[]{:S(2)}, u32[]{:S(2)}) collective-permute-start(bf16[4,4,64,2688]{3,2,1,0:T(8,128)(2,1)} %pad_maximum_fusion.1), channel_id=1, source_target_pairs={{0,2},{2,0},{4,6},{6,4},{1,3},{3,1},{5,7},{7,5},{8,10},{10,8},{12,... | collective-permute-start | bytes 16515080 | tf_op jit(solution)/shard_map/ppermute | solution.py:311
  133.7 5.8 %copy-start.2 = (bf16[8,4,64,2688]{3,2,1,0:T(8,128)(2,1)}, bf16[8,4,64,2688]{3,2,1,0:T(8,128)(2,1)S(1)}, u32[]{:S(2)}) copy-start(bf16[8,4,64,2688]{3,2,1,0:T(8,128)(2,1)S(1)} %pad_maximum_fusion.states_ref) | copy-start | bytes 33030148
  139.6 3.9 %copy-start.4 = (bf16[4,2560,512]{2,1,0:T(8,128)(2,1)}, bf16[4,2560,512]{2,1,0:T(8,128)(2,1)S(1)}, u32[]{:S(2)}) copy-start(bf16[4,2560,512]{2,1,0:T(8,128)(2,1)S(1)} %get-tuple-element.24.hidden_ref) | copy-start | bytes 31457284
  182.4 28.0 %slice-start = ((s8[10485760]{0:T(1024)(128)(4,1)}), s8[4194304]{0:T(1024)(128)(4,1)S(1)}, s32[]{:S(2)}) async-start(s8[10485760]{0:T(1024)(128)(4,1)} %bitcast.279), calls=%async_computation.1 | async-start | bytes 8388608
  182.4 28.0 %slice-start.1 = ((s8[10485760]{0:T(1024)(128)(4,1)}), s8[4194304]{0:T(1024)(128)(4,1)S(1)}, s32[]{:S(2)}) async-start(s8[10485760]{0:T(1024)(128)(4,1)} %bitcast.279), calls=%async_computation.2 | async-start | bytes 8388608
  182.5 28.0 %slice-start.2 = ((s8[10485760]{0:T(1024)(128)(4,1)}), s8[2097152]{0:T(1024)(128)(4,1)S(1)}, s32[]{:S(2)}) async-start(s8[10485760]{0:T(1024)(128)(4,1)} %bitcast.279), calls=%async_computation.3 | async-start | bytes 4194304
  194.6 1.9 collective-permute-start.7
  196.5 4.1 %collective-permute-start.8 = (f32[4,4,512]{2,1,0:T(4,128)S(1)}, f32[4,4,512]{2,1,0:T(4,128)S(1)}, u32[]{:S(2)}, u32[]{:S(2)}) collective-permute-start(f32[4,4,512]{2,1,0:T(4,128)S(1)} %pad_maximum_fusion.8), channel_id=1, source_target_pairs={{0,4},{2,6},{4,0},{6,2},{1,5},{3,7},{5,1},{7,3},{8,12},{10,14},{12... | collective-permute-start | bytes 98312 | tf_op jit(solution)/shard_map/ppermute | solution.py:283
  200.7 2.8 %collective-permute-start.9 = (f32[4,4,512]{2,1,0:T(4,128)S(1)}, f32[4,4,512]{2,1,0:T(4,128)S(1)}, u32[]{:S(2)}, u32[]{:S(2)}) collective-permute-start(f32[4,4,512]{2,1,0:T(4,128)S(1)} %pad_maximum_fusion.9), channel_id=1, source_target_pairs={{0,1},{1,0},{2,3},{3,2},{4,5},{5,4},{6,7},{7,6},{8,9},{9,8},{10,11... | collective-permute-start | bytes 98312 | tf_op jit(solution)/shard_map/ppermute | solution.py:283
  203.6 2.8 %collective-permute-start.10 = (f32[4,4,512]{2,1,0:T(4,128)S(1)}, f32[4,4,512]{2,1,0:T(4,128)S(1)}, u32[]{:S(2)}, u32[]{:S(2)}) collective-permute-start(f32[4,4,512]{2,1,0:T(4,128)S(1)} %pad_maximum_fusion.10), channel_id=1, source_target_pairs={{0,8},{8,0},{16,24},{24,16},{1,9},{9,1},{17,25},{25,17},{2,10},{10... | collective-permute-start | bytes 98312 | tf_op jit(solution)/shard_map/ppermute | solution.py:283
  206.5 3.7 %collective-permute-start.11 = (f32[4,4,512]{2,1,0:T(4,128)S(1)}, f32[4,4,512]{2,1,0:T(4,128)S(1)}, u32[]{:S(2)}, u32[]{:S(2)}) collective-permute-start(f32[4,4,512]{2,1,0:T(4,128)S(1)} %pad_maximum_fusion.11), channel_id=1, source_target_pairs={{0,16},{8,24},{16,0},{24,8},{1,17},{9,25},{17,1},{25,9},{2,18},{10... | collective-permute-start | bytes 98312 | tf_op jit(solution)/shard_map/ppermute | solution.py:283
  222.5 5.7 %collective-permute-start.17 = (bf16[2,208,256]{2,1,0:T(8,128)(2,1)S(1)}, bf16[2,208,256]{2,1,0:T(8,128)(2,1)S(1)}, u32[]{:S(2)}, u32[]{:S(2)}) collective-permute-start(bf16[2,208,256]{2,1,0:T(8,128)(2,1)S(1)} %get-tuple-element.29), channel_id=1, source_target_pairs={{0,12},{2,14},{4,8},{6,10},{8,4},{10,6},{12,0},{14,2},{16,28},{18,... | collective-permute-start | bytes 638984 | tf_op jit(solution)/shard_map/ppermute | solution.py:362
  223.7 7.2 %collective-permute-start.18 = (bf16[2,208,256]{2,1,0:T(8,128)(2,1)S(1)}, bf16[2,208,256]{2,1,0:T(8,128)(2,1)S(1)}, u32[]{:S(2)}, u32[]{:S(2)}) collective-permute-start(bf16[2,208,256]{2,1,0:T(8,128)(2,1)S(1)} %get-tuple-element.30), channel_id=1, source_target_pairs={{0,8},{2,10},{4,12},{6,14},{8,0},{10,2},{12,4},{14,6},{16,24},{18,... | collective-permute-start | bytes 638984 | tf_op jit(solution)/shard_map/ppermute | solution.py:362
  225.2 10.7 %collective-permute-start.19 = (bf16[2,208,256]{2,1,0:T(8,128)(2,1)S(1)}, bf16[2,208,256]{2,1,0:T(8,128)(2,1)S(1)}, u32[]{:S(2)}, u32[]{:S(2)}) collective-permute-start(bf16[2,208,256]{2,1,0:T(8,128)(2,1)S(1)} %get-tuple-element.31), channel_id=1, source_target_pairs={{0,4},{2,6},{4,0},{6,2},{8,12},{10,14},{12,8},{14,10},{16,20},{18,... | collective-permute-start | bytes 638984 | tf_op jit(solution)/shard_map/ppermute | solution.py:362
  225.2 19.0 %collective-permute-start.12 = (bf16[2,208,256]{2,1,0:T(8,128)(2,1)S(1)}, bf16[2,208,256]{2,1,0:T(8,128)(2,1)S(1)}, u32[]{:S(2)}, u32[]{:S(2)}) collective-permute-start(bf16[2,208,256]{2,1,0:T(8,128)(2,1)S(1)} %get-tuple-element.25), channel_id=1, source_target_pairs={{0,28},{2,30},{4,24},{6,26},{8,20},{10,22},{12,16},{14,18},{16,12}... | collective-permute-start | bytes 638984 | tf_op jit(solution)/shard_map/ppermute | solution.py:362
  226.8 17.5 %collective-permute-start.13 = (bf16[2,208,256]{2,1,0:T(8,128)(2,1)S(1)}, bf16[2,208,256]{2,1,0:T(8,128)(2,1)S(1)}, u32[]{:S(2)}, u32[]{:S(2)}) collective-permute-start(bf16[2,208,256]{2,1,0:T(8,128)(2,1)S(1)} %get-tuple-element.26), channel_id=1, source_target_pairs={{0,24},{2,26},{4,28},{6,30},{8,16},{10,18},{12,20},{14,22},{16,8},... | collective-permute-start | bytes 638984 | tf_op jit(solution)/shard_map/ppermute | solution.py:362
  228.2 27.1 %collective-permute-start.14 = (bf16[2,208,256]{2,1,0:T(8,128)(2,1)S(1)}, bf16[2,208,256]{2,1,0:T(8,128)(2,1)S(1)}, u32[]{:S(2)}, u32[]{:S(2)}) collective-permute-start(bf16[2,208,256]{2,1,0:T(8,128)(2,1)S(1)} %get-tuple-element.27), channel_id=1, source_target_pairs={{0,20},{2,22},{4,16},{6,18},{8,28},{10,30},{12,24},{14,26},{16,4},... | collective-permute-start | bytes 638984 | tf_op jit(solution)/shard_map/ppermute | solution.py:362
  230.9 29.0 %collective-permute-start.15 = (bf16[2,208,256]{2,1,0:T(8,128)(2,1)S(1)}, bf16[2,208,256]{2,1,0:T(8,128)(2,1)S(1)}, u32[]{:S(2)}, u32[]{:S(2)}) collective-permute-start(bf16[2,208,256]{2,1,0:T(8,128)(2,1)S(1)} %get-tuple-element.28), channel_id=1, source_target_pairs={{0,16},{2,18},{4,20},{6,22},{8,24},{10,26},{12,28},{14,30},{16,0},... | collective-permute-start | bytes 638984 | tf_op jit(solution)/shard_map/ppermute | solution.py:362
  236.0 28.3 %collective-permute-start.20 = (bf16[4,208,256]{2,1,0:T(8,128)(2,1)S(1)}, bf16[4,208,256]{2,1,0:T(8,128)(2,1)S(1)}, u32[]{:S(2)}, u32[]{:S(2)}) collective-permute-start(bf16[4,208,256]{2,1,0:T(8,128)(2,1)S(1)} %pad_maximum_fusion.7), channel_id=1, source_target_pairs={{0,2},{2,0},{4,6},{6,4},{1,3},{3,1},{5,7},{7,5},{8,10},{10,8},{12,... | collective-permute-start | bytes 1277960 | tf_op jit(solution)/shard_map/ppermute | solution.py:311
  244.2 23.1 %copy-start.1 = (bf16[1,128,2560]{2,1,0:T(8,128)(2,1)S(1)}, bf16[1,128,2560]{2,1,0:T(8,128)(2,1)}, u32[]{:S(2)}) copy-start(bf16[1,128,2560]{2,1,0:T(8,128)(2,1)} %param.4) | copy-start | bytes 1966084
  260.0 5.8 %collective-permute-start.16 = (bf16[4,208,256]{2,1,0:T(8,128)(2,1)S(1)}, bf16[4,208,256]{2,1,0:T(8,128)(2,1)S(1)}, u32[]{:S(2)}, u32[]{:S(2)}) collective-permute-start(bf16[4,208,256]{2,1,0:T(8,128)(2,1)S(1)} %pad_maximum_fusion.6), channel_id=1, source_target_pairs={{0,2},{2,0},{4,6},{6,4},{1,3},{3,1},{5,7},{7,5},{8,10},{10,8},{12,... | collective-permute-start | bytes 1277960 | tf_op jit(solution)/shard_map/ppermute | solution.py:311

commit v6 on v5

--- a/solution.py
+++ b/solution.py
@@ -131,7 +131,7 @@
     return call(
         score_kernel, "score",
         out_shape=(
-            pltpu.HBM((ckpts, tokens, lanes), jnp.float32),
+            pltpu.VMEM((ckpts, tokens, lanes), jnp.float32),
             jax.ShapeDtypeStruct((ckpts, 8, tokens), jnp.float32),
         ),
         grid=(ckpts,),
@@ -153,7 +153,8 @@
 ):
     outs, wide_rows, slim_rows, resid_ref = refs[:-3], *refs[-3:]
     ckpts, tokens, lanes = resid_ref.shape
-    wide, depth = heads_ref.shape[3], hidden_ref.shape[1]
+    wide, depth = heads_ref.shape[3], hidden_ref.shape[1] // heads_ref.shape[0]
+    first_row = pl.multiple_of((place_ref[0] ^ pl.program_id(0)) * depth, depth)
     slim = lanes - wide
     fold = wide // (slim // 2)
 
@@ -169,7 +170,7 @@
     def blend(lo, hi, heads_of):
         numer = denom = None
         for c in range(ckpts):
-            product = jnp.dot(hidden_ref[c], resid_ref[c, :, lo:hi], preferred_element_type=jnp.float32)
+            product = jnp.dot(hidden_ref[c, pl.ds(first_row, depth)], resid_ref[c, :, lo:hi], preferred_element_type=jnp.float32)
             weight = (product * scale_ref[c] + prior).astype(jnp.bfloat16).astype(jnp.float32)
             term = weight * heads_of(c).astype(jnp.float32)
             numer = term if numer is None else numer + term
@@ -218,7 +219,7 @@
             in_specs=[pl.BlockSpec(memory_space=pltpu.SMEM)]
             + [whole(x) for x in (logits, table, labels, ids)]
             + [
-                pl.BlockSpec((ckpts, depth, tokens), lambda i, s: (0, s[0] ^ i, 0)),
+                pl.BlockSpec(memory_space=pltpu.VMEM),
                 pl.BlockSpec((ckpts, 1, *heads.shape[2:]), lambda i, s: (0, s[0] ^ i, 0, 0)),
             ],
             out_specs=[pl.BlockSpec(shape, lambda i, s: (0, 0, 0))] * (blocks * ntok // 2),
@@ -228,7 +229,7 @@
                 pltpu.VMEM((ckpts, tokens, lanes), jnp.bfloat16),
             ],
         ),
-    )(place, scales, in_hbm(logits), table, labels, ids, hidden_sq, in_hbm(heads))
+    )(place, scales, pltpu.with_memory_space_constraint(logits, pltpu.VMEM), table, labels, ids, hidden_sq, in_hbm(heads))
 
 
 def assemble_kernel(mine_ref, *refs, sources):
@@ -305,7 +306,7 @@
     label = lax.dynamic_slice_in_dim(targets, lax.axis_index("vocab") * size, size, 0)[:, None]
     digits = jnp.concatenate([label % 256, label // 256 % 256, label // 65536], axis=1)
     digits = jnp.pad(digits.astype(hidden.dtype), ((0, 0), (0, 125)))
-    own = jnp.concatenate([own, digits], axis=1)[None]
+    own = own[None]
 
     def other(x, axis, far):
         return lax.ppermute(x, axis, [(i, i ^ far) for i in range(lax.axis_size(axis))])
@@ -320,7 +321,8 @@
     states = paired(
         paired(planes[0], planes[3], "ckpt", 1), paired(planes[1], planes[2], "ckpt", 1), "ckpt", 2
     )[None]
-    states = after(states, packed)
+    digits = jnp.broadcast_to(digits, (1, ckpts, *digits.shape))
+    states = after(jnp.concatenate([states, digits], axis=3), packed)
     chains = [states, other(states, "tok", 2)]
     for i in (0, 1):
         far = 1

time: 272 us -> 268 us (0.985)
  waiting for transfers between devices: 161 us -> 158 us
    unnamed x18 -> x19, local copies, waits for them, and re-layouts: 6.56 us -> 5.44 us
  transfers between devices with their start and end apart: 22 -> 22, of which waited for: 17 -> 17; matrix products, arithmetic and copies ran while one was open for 5% -> 6% of each run, Pallas kernels for 4% -> 4%
where the time goes in v6:
time: 268 us; the launch traced here: 263 us
  waiting for transfers between devices  158 us (59%)
  starting transfers between devices  47.3 us (18%)
  Pallas kernels  34.4 us (13%)
  other arithmetic  16.6 us (6%)
  local copies, waits for them, and re-layouts  6.58 us (2%)
    ppermute x9, waiting for transfers between devices, other(): lax.ppermute(x, axis, [(i, i ^ far) for i in range(lax.axis_size(axis))])  93.4 us
    all_to_all x1, waiting for transfers between devices, exchange(): return lax.all_to_all(x, BOTH, 0, 0, tiled=True)  36.4 us
    ppermute x9, starting transfers between devices, other(): lax.ppermute(x, axis, [(i, i ^ far) for i in range(lax.axis_size(axis))])  25.1 us
    ppermute x7, waiting for transfers between devices, shards(): part = lax.ppermute(part, BOTH, [(g, g ^ r) for g in range(peers)])  19.6 us
    pallas_call x1, Pallas kernels, score(): call(score_kernel, 'score', out_shape=(pltpu.VMEM((ckpts, tokens, lanes),...  11.6 us
    pallas_call x1, Pallas kernels, merge(): call(functools.partial(merge_kernel, prior=prior), 'merge', out_shape=[ja...  10.5 us
    ppermute x7, starting transfers between devices, shards(): part = lax.ppermute(part, BOTH, [(g, g ^ r) for g in range(peers)])  9.36 us
    select_n x7, other arithmetic, paired(): return jnp.concatenate([jnp.where(upper, y, x), jnp.where(upper, x, y)])  8.61 us
  transfers between devices with their start and end apart: 22, of which 17 were waited for; matrix products, arithmetic and copies ran while one was open for 6% of the time, Pallas kernels for 4%

profile of v6, /device:TPU:9, one launch (start us, length us, event | category | flops | bytes accessed | tf_op | source)
XLA Modules:
  0.0 263.3 jit_solution(5334061586999055823)
XLA Ops:
  0.0 1.0 constant_dynamic-slice_fusion
  1.1 2.5 collective-permute-start.1
  5.3 4.8 %pack.1 = bf16[16,5,160,256]{3,2,1,0:T(8,128)(2,1)S(1)} custom-call(bf16[640,5120]{1,0:T(8,128)(2,1)} %bitcast.273, bf16[640,5120]{1,0:T(8,128)(2,1)} %bitcast.274, bf16[640,5120]{1,0:T(8,128)(2,1)} %bitcast.275, bf16[640,5120]{1,0:T(8,128)(2,1)} %bitcast.276), custom_call_target="tpu_custom_call" | custom-call | tf_op jit(solution)/shard_map/pack/pallas_call | solution.py:48
  10.2 3.8 %collective-permute-done.2 = bf16[1,64,2560]{2,1,0:T(8,128)(2,1)S(1)} collective-permute-done((bf16[1,64,2560]{2,1,0:T(8,128)(2,1)S(1)}, bf16[1,64,2560]{2,1,0:T(8,128)(2,1)S(1)}, u32[]{:S(2)}, u32[]{:S(2)}) %collective-permute-start.2) | collective-permute-done | bytes 327712 | tf_op jit(solution)/shard_map/ppermute | solution.py:312
  14.1 3.6 %collective-permute-done.1 = bf16[1,64,2560]{2,1,0:T(8,128)(2,1)S(1)} collective-permute-done((bf16[1,64,2560]{2,1,0:T(8,128)(2,1)S(1)}, bf16[1,64,2560]{2,1,0:T(8,128)(2,1)S(1)}, u32[]{:S(2)}, u32[]{:S(2)}) %collective-permute-start.1) | collective-permute-done | bytes 327712 | tf_op jit(solution)/shard_map/ppermute | solution.py:312
  17.7 13.9 %collective-permute-done = bf16[1,64,2560]{2,1,0:T(8,128)(2,1)S(1)} collective-permute-done((bf16[1,64,2560]{2,1,0:T(8,128)(2,1)S(1)}, bf16[1,64,2560]{2,1,0:T(8,128)(2,1)S(1)}, u32[]{:S(2)}, u32[]{:S(2)}) %collective-permute-start) | collective-permute-done | bytes 327712 | tf_op jit(solution)/shard_map/ppermute | solution.py:312
  32.1 1.3 collective-permute-start.3
  33.4 6.1 %all-to-all-start = ((bf16[16,800,256]{2,1,0:T(8,128)(2,1)}), bf16[16,800,256]{2,1,0:T(8,128)(2,1)}, u32[]{:S(2)}, u32[]{:S(2)}) async-start(bf16[16,800,256]{2,1,0:T(8,128)(2,1)} %bitcast.270), calls=%async_computation | async-start | bytes 13107200 | tf_op jit(solution)/shard_map/all_to_all | solution.py:269
  39.5 1.2 collective-permute-start.5
  40.7 37.9 %collective-permute-done.3 = bf16[1,4,64,2688]{3,2,1,0:T(8,128)(2,1)S(1)} collective-permute-done((bf16[1,4,64,2688]{3,2,1,0:T(8,128)(2,1)S(1)}, bf16[1,4,64,2688]{3,2,1,0:T(8,128)(2,1)S(1)}, u32[]{:S(2)}, u32[]{:S(2)}) %collective-permute-start.3) | collective-permute-done | bytes 1376288 | tf_op jit(solution)/shard_map/ppermute | solution.py:312
  78.6 1.2 collective-permute-start.4
  79.8 1.6 broadcast_select_fusion.5
  81.4 23.9 %collective-permute-done.4 = bf16[1,4,64,2688]{3,2,1,0:T(8,128)(2,1)} collective-permute-done((bf16[1,4,64,2688]{3,2,1,0:T(8,128)(2,1)S(1)}, bf16[1,4,64,2688]{3,2,1,0:T(8,128)(2,1)}, u32[]{:S(2)}, u32[]{:S(2)}) %collective-permute-start.4) | collective-permute-done | bytes 1376288 | tf_op jit(solution)/shard_map/ppermute | solution.py:312
  105.3 1.6 broadcast_select_fusion.7
  107.6 3.3 %pad_maximum_fusion.1 = bf16[4,4,64,2688]{3,2,1,0:T(8,128)(2,1)} fusion(bf16[2,4,64,2688]{3,2,1,0:T(8,128)(2,1)S(1)} %get-tuple-element.47, bf16[2,4,64,2688]{3,2,1,0:T(8,128)(2,1)S(1)} %get-tuple-element.46), kind=kLoop, calls=%fused_computation.3 | loop fusion | flops 2752512 | bytes 11010048 | tf_op jit(solution)/shard_map/concatenate | solution.py:316
  110.9 6.0 %collective-permute-start.6 = (bf16[4,4,64,2688]{3,2,1,0:T(8,128)(2,1)}, bf16[4,4,64,2688]{3,2,1,0:T(8,128)(2,1)}, u32[]{:S(2)}, u32[]{:S(2)}) collective-permute-start(bf16[4,4,64,2688]{3,2,1,0:T(8,128)(2,1)} %pad_maximum_fusion.1), channel_id=1, source_target_pairs={{0,2},{2,0},{4,6},{6,4},{1,3},{3,1},{5,7},{7,5},{8,10},{10,8},{12,... | collective-permute-start | bytes 16515080 | tf_op jit(solution)/shard_map/ppermute | solution.py:312
  117.0 8.9 %collective-permute-done.6 = bf16[4,4,64,2688]{3,2,1,0:T(8,128)(2,1)} collective-permute-done((bf16[4,4,64,2688]{3,2,1,0:T(8,128)(2,1)}, bf16[4,4,64,2688]{3,2,1,0:T(8,128)(2,1)}, u32[]{:S(2)}, u32[]{:S(2)}) %collective-permute-start.6) | collective-permute-done | bytes 5505056 | tf_op jit(solution)/shard_map/ppermute | solution.py:312
  125.9 4.4 %broadcast_select_fusion.1 = (bf16[4,4,64,2688]{3,2,1,0:T(8,128)(2,1)S(1)}, bf16[4,4,64,2688]{3,2,1,0:T(8,128)(2,1)S(1)}) fusion(bf16[4,4,64,2688]{3,2,1,0:T(8,128)(2,1)} %collective-permute-done.6, pred[]{:T(512)S(6)} %eq.28, bf16[2,4,64,2688]{3,2,1,0:T(8,128)(2,1)} %copy-done.4, bf16[2,4,64,2688]{3,2,1,0:T(8,128)(2,1)S(1)} %get-tuple-element.46), kind=kLoop, calls=%fused_computation.5 | loop fusion | flops 8257536 | bytes 22020096 | tf_op jit(solution)/shard_map/jit(_where)/select_n | solution.py:316
  130.3 2.4 copy-done.3
  132.7 1.2 pad_maximum_fusion.states_ref
  133.9 5.8 %squares.1 = (bf16[4,2560,512]{2,1,0:T(8,128)(2,1)S(1)}, f32[4,1,512]{2,1,0:T(1,128)S(1)}) custom-call(bf16[8,4,64,2688]{3,2,1,0:T(8,128)(2,1)S(1)} %pad_maximum_fusion.states_ref), custom_call_target="tpu_custom_call" | custom-call | tf_op jit(solution)/shard_map/squares/pallas_call | solution.py:79
  139.8 0.9 fusion.2
  140.7 2.9 %copy-done.2 = bf16[4,2560,512]{2,1,0:T(8,128)(2,1)} copy-done((bf16[4,2560,512]{2,1,0:T(8,128)(2,1)}, bf16[4,2560,512]{2,1,0:T(8,128)(2,1)S(1)}, u32[]{:S(2)}) %copy-start.2) | copy-done | bytes 10485784
  143.9 36.4 %all-to-all-done = bf16[16,800,256]{2,1,0:T(8,128)(2,1)} async-done(((bf16[16,800,256]{2,1,0:T(8,128)(2,1)}), bf16[16,800,256]{2,1,0:T(8,128)(2,1)}, u32[]{:S(2)}, u32[]{:S(2)}) %all-to-all-start) | async-done | bytes 6553632 | tf_op jit(solution)/shard_map/all_to_all | solution.py:269
  180.3 11.6 %score.1 = (f32[4,512,384]{2,1,0:T(8,128)S(1)}, f32[4,8,512]{2,1,0:T(8,128)S(1)}) custom-call(bf16[8,4,64,2688]{3,2,1,0:T(8,128)(2,1)} %copy-done, bf16[4,4,800,256]{3,2,1,0:T(8,128)(2,1)} %bitcast.9.heads_ref, s32[512,1]{1,0:T(8,128)S(1)} %fusion.labels_ref, s32[1,384]{1,0:T(1,128)S(1)} %broadcast_in_dim.18.ids_ref), custom_call_target="tpu_custom_call" | custom-call | tf_op jit(solution)/shard_map/score/pallas_call | solution.py:131
  192.1 1.0 collective-permute-start.7
  193.1 0.9 collective-permute-done.7
  194.0 2.8 %collective-permute-start.8 = (f32[4,4,512]{2,1,0:T(4,128)S(1)}, f32[4,4,512]{2,1,0:T(4,128)S(1)}, u32[]{:S(2)}, u32[]{:S(2)}) collective-permute-start(f32[4,4,512]{2,1,0:T(4,128)S(1)} %pad_maximum_fusion.9), channel_id=1, source_target_pairs={{0,4},{2,6},{4,0},{6,2},{1,5},{3,7},{5,1},{7,3},{8,12},{10,14},{12... | collective-permute-start | bytes 98312 | tf_op jit(solution)/shard_map/ppermute | solution.py:284
  196.8 1.3 collective-permute-done.8
  198.2 1.3 collective-permute-start.9
  199.5 1.5 collective-permute-done.9
  201.2 2.8 %collective-permute-done.10 = f32[4,4,512]{2,1,0:T(4,128)S(1)} collective-permute-done((f32[4,4,512]{2,1,0:T(4,128)S(1)}, f32[4,4,512]{2,1,0:T(4,128)S(1)}, u32[]{:S(2)}, u32[]{:S(2)}) %collective-permute-start.10) | collective-permute-done | bytes 32800 | tf_op jit(solution)/shard_map/ppermute | solution.py:284
  204.0 1.5 collective-permute-start.11
  205.6 2.1 collective-permute-done.11
  207.9 10.5 %merge.1 = (bf16[2,208,256]{2,1,0:T(8,128)(2,1)S(1)}, bf16[2,208,256]{2,1,0:T(8,128)(2,1)S(1)}, bf16[2,208,256]{2,1,0:T(8,128)(2,1)S(1)}, bf16[2,208,256]{2,1,0:...) custom-call(s32[2]{0:T(128)S(1)} %pad_add_fusion.1.place_ref, ...), custom_call_target="tpu_custom_call" | custom-call | tf_op jit(solution)/shard_map/merge/pallas_call | solution.py:213
  218.5 1.3 collective-permute-start.17
  219.7 1.5 collective-permute-start.18
  221.2 1.6 collective-permute-start.12
  222.7 1.1 collective-permute-start.13
  224.2 2.7 %collective-permute-start.14 = (bf16[2,208,256]{2,1,0:T(8,128)(2,1)S(1)}, bf16[2,208,256]{2,1,0:T(8,128)(2,1)S(1)}, u32[]{:S(2)}, u32[]{:S(2)}) collective-permute-start(bf16[2,208,256]{2,1,0:T(8,128)(2,1)S(1)} %get-tuple-element.27), channel_id=1, source_target_pairs={{0,20},{2,22},{4,16},{6,18},{8,28},{10,30},{12,24},{14,26},{16,4},... | collective-permute-start | bytes 638984 | tf_op jit(solution)/shard_map/ppermute | solution.py:364
  226.9 1.3 collective-permute-start.15
  228.2 3.6 %collective-permute-done.19.refs_7_ = bf16[2,208,256]{2,1,0:T(8,128)(2,1)S(1)} collective-permute-done((bf16[2,208,256]{2,1,0:T(8,128)(2,1)S(1)}, bf16[2,208,256]{2,1,0:T(8,128)(2,1)S(1)}, u32[]{:S(2)}, u32[]{:S(2)}) %collective-permute-start.19) | collective-permute-done | bytes 213024 | tf_op jit(solution)/shard_map/ppermute | solution.py:364
  232.0 8.2 %collective-permute-start.20 = (bf16[4,208,256]{2,1,0:T(8,128)(2,1)S(1)}, bf16[4,208,256]{2,1,0:T(8,128)(2,1)S(1)}, u32[]{:S(2)}, u32[]{:S(2)}) collective-permute-start(bf16[4,208,256]{2,1,0:T(8,128)(2,1)S(1)} %pad_maximum_fusion.8), channel_id=1, source_target_pairs={{0,2},{2,0},{4,6},{6,4},{1,3},{3,1},{5,7},{7,5},{8,10},{10,8},{12,... | collective-permute-start | bytes 1277960 | tf_op jit(solution)/shard_map/ppermute | solution.py:312
  240.2 11.1 %collective-permute-done.14.refs_2_ = bf16[2,208,256]{2,1,0:T(8,128)(2,1)S(1)} collective-permute-done((bf16[2,208,256]{2,1,0:T(8,128)(2,1)S(1)}, bf16[2,208,256]{2,1,0:T(8,128)(2,1)S(1)}, u32[]{:S(2)}, u32[]{:S(2)}) %collective-permute-start.14) | collective-permute-done | bytes 213024 | tf_op jit(solution)/shard_map/ppermute | solution.py:364
  251.3 4.6 %collective-permute-done.15.refs_3_ = bf16[2,208,256]{2,1,0:T(8,128)(2,1)S(1)} collective-permute-done((bf16[2,208,256]{2,1,0:T(8,128)(2,1)S(1)}, bf16[2,208,256]{2,1,0:T(8,128)(2,1)S(1)}, u32[]{:S(2)}, u32[]{:S(2)}) %collective-permute-start.15) | collective-permute-done | bytes 213024 | tf_op jit(solution)/shard_map/ppermute | solution.py:364
  255.9 4.4 %collective-permute-start.16 = (bf16[4,208,256]{2,1,0:T(8,128)(2,1)S(1)}, bf16[4,208,256]{2,1,0:T(8,128)(2,1)S(1)}, u32[]{:S(2)}, u32[]{:S(2)}) collective-permute-start(bf16[4,208,256]{2,1,0:T(8,128)(2,1)S(1)} %pad_maximum_fusion.7), channel_id=1, source_target_pairs={{0,2},{2,0},{4,6},{6,4},{1,3},{3,1},{5,7},{7,5},{8,10},{10,8},{12,... | collective-permute-start | bytes 1277960 | tf_op jit(solution)/shard_map/ppermute | solution.py:312
  260.3 1.4 collective-permute-done.16.refs_4_
  261.7 1.6 assemble.1
  (73 shorter events, 4.6 us)
Async XLA Ops:
  1.0 13.0 %collective-permute-start.2 = (bf16[1,64,2560]{2,1,0:T(8,128)(2,1)S(1)}, bf16[1,64,2560]{2,1,0:T(8,128)(2,1)S(1)}, u32[]{:S(2)}, u32[]{:S(2)}) collective-permute-start(bf16[1,64,2560]{2,1,0:T(8,128)(2,1)S(1)} %constant_dynamic-slice_fusion), channel_id=1, source_target_pairs={{0,8},{8,0},{16,24},{24,16},{1,9},{9,1},{17,25},{25,17},{2,10},{10... | collective-permute-start | bytes 983048 | tf_op jit(solution)/shard_map/ppermute | solution.py:312
  1.1 16.6 %collective-permute-start.1 = (bf16[1,64,2560]{2,1,0:T(8,128)(2,1)S(1)}, bf16[1,64,2560]{2,1,0:T(8,128)(2,1)S(1)}, u32[]{:S(2)}, u32[]{:S(2)}) collective-permute-start(bf16[1,64,2560]{2,1,0:T(8,128)(2,1)S(1)} %constant_dynamic-slice_fusion), channel_id=1, source_target_pairs={{0,16},{8,24},{16,0},{24,8},{1,17},{9,25},{17,1},{25,9},{2,18},{10... | collective-permute-start | bytes 983048 | tf_op jit(solution)/shard_map/ppermute | solution.py:312
  3.5 28.1 %collective-permute-start = (bf16[1,64,2560]{2,1,0:T(8,128)(2,1)S(1)}, bf16[1,64,2560]{2,1,0:T(8,128)(2,1)S(1)}, u32[]{:S(2)}, u32[]{:S(2)}) collective-permute-start(bf16[1,64,2560]{2,1,0:T(8,128)(2,1)S(1)} %constant_dynamic-slice_fusion), channel_id=1, source_target_pairs={{0,24},{8,16},{16,8},{24,0},{1,25},{9,17},{17,9},{25,1},{2,26},{10... | collective-permute-start | bytes 983048 | tf_op jit(solution)/shard_map/ppermute | solution.py:312
  5.3 8.7 %copy-start.5 = (bf16[1,128,2560]{2,1,0:T(8,128)(2,1)S(1)}, bf16[1,128,2560]{2,1,0:T(8,128)(2,1)}, u32[]{:S(2)}) copy-start(bf16[1,128,2560]{2,1,0:T(8,128)(2,1)} %param.4) | copy-start | bytes 1966084
  10.2 21.8 %copy-start.1 = (bf16[16,5,160,256]{3,2,1,0:T(8,128)(2,1)}, bf16[16,5,160,256]{3,2,1,0:T(8,128)(2,1)S(1)}, u32[]{:S(2)}) copy-start(bf16[16,5,160,256]{3,2,1,0:T(8,128)(2,1)S(1)} %pack.1) | copy-start | bytes 19660804
  32.1 46.5 %collective-permute-start.3 = (bf16[1,4,64,2688]{3,2,1,0:T(8,128)(2,1)S(1)}, bf16[1,4,64,2688]{3,2,1,0:T(8,128)(2,1)S(1)}, u32[]{:S(2)}, u32[]{:S(2)}) collective-permute-start(bf16[1,4,64,2688]{3,2,1,0:T(8,128)(2,1)S(1)} %pad_maximum_fusion.4), channel_id=1, source_target_pairs={{0,4},{2,6},{4,0},{6,2},{1,5},{3,7},{5,1},{7,3},{8,12},{10,14},{12... | collective-permute-start | bytes 4128776 | tf_op jit(solution)/shard_map/ppermute | solution.py:312
  33.4 146.9 %all-to-all-start = ((bf16[16,800,256]{2,1,0:T(8,128)(2,1)}), bf16[16,800,256]{2,1,0:T(8,128)(2,1)}, u32[]{:S(2)}, u32[]{:S(2)}) async-start(bf16[16,800,256]{2,1,0:T(8,128)(2,1)} %bitcast.270), calls=%async_computation | async-start | bytes 13107200 | tf_op jit(solution)/shard_map/all_to_all | solution.py:269
  39.5 40.4 %collective-permute-start.5 = (bf16[1,4,64,2688]{3,2,1,0:T(8,128)(2,1)S(1)}, bf16[1,4,64,2688]{3,2,1,0:T(8,128)(2,1)}, u32[]{:S(2)}, u32[]{:S(2)}) collective-permute-start(bf16[1,4,64,2688]{3,2,1,0:T(8,128)(2,1)S(1)} %pad_maximum_fusion.4), channel_id=1, source_target_pairs={{0,1},{1,0},{2,3},{3,2},{4,5},{5,4},{6,7},{7,6},{8,9},{9,8},{10,11... | collective-permute-start | bytes 4128776 | tf_op jit(solution)/shard_map/ppermute | solution.py:312
  78.6 26.7 %collective-permute-start.4 = (bf16[1,4,64,2688]{3,2,1,0:T(8,128)(2,1)S(1)}, bf16[1,4,64,2688]{3,2,1,0:T(8,128)(2,1)}, u32[]{:S(2)}, u32[]{:S(2)}) collective-permute-start(bf16[1,4,64,2688]{3,2,1,0:T(8,128)(2,1)S(1)} %collective-permute-done.3), channel_id=1, source_target_pairs={{0,1},{1,0},{2,3},{3,2},{4,5},{5,4},{6,7},{7,6},{8,9},{9,8},{10,11... | collective-permute-start | bytes 4128776 | tf_op jit(solution)/shard_map/ppermute | solution.py:312
  107.6 3.3 %copy-start.4 = (bf16[2,4,64,2688]{3,2,1,0:T(8,128)(2,1)}, bf16[2,4,64,2688]{3,2,1,0:T(8,128)(2,1)S(1)}, u32[]{:S(2)}) copy-start(bf16[2,4,64,2688]{3,2,1,0:T(8,128)(2,1)S(1)} %get-tuple-element.47) | copy-start | bytes 8257540
  110.9 15.0 %collective-permute-start.6 = (bf16[4,4,64,2688]{3,2,1,0:T(8,128)(2,1)}, bf16[4,4,64,2688]{3,2,1,0:T(8,128)(2,1)}, u32[]{:S(2)}, u32[]{:S(2)}) collective-permute-start(bf16[4,4,64,2688]{3,2,1,0:T(8,128)(2,1)} %pad_maximum_fusion.1), channel_id=1, source_target_pairs={{0,2},{2,0},{4,6},{6,4},{1,3},{3,1},{5,7},{7,5},{8,10},{10,8},{12,... | collective-permute-start | bytes 16515080 | tf_op jit(solution)/shard_map/ppermute | solution.py:312
  130.3 2.4 copy-start.3
  133.9 5.8 %copy-start = (bf16[8,4,64,2688]{3,2,1,0:T(8,128)(2,1)}, bf16[8,4,64,2688]{3,2,1,0:T(8,128)(2,1)S(1)}, u32[]{:S(2)}) copy-start(bf16[8,4,64,2688]{3,2,1,0:T(8,128)(2,1)S(1)} %pad_maximum_fusion.states_ref) | copy-start | bytes 33030148
  139.8 3.9 %copy-start.2 = (bf16[4,2560,512]{2,1,0:T(8,128)(2,1)}, bf16[4,2560,512]{2,1,0:T(8,128)(2,1)S(1)}, u32[]{:S(2)}) copy-start(bf16[4,2560,512]{2,1,0:T(8,128)(2,1)S(1)} %get-tuple-element.24.hidden_ref) | copy-start | bytes 31457284
  180.3 27.6 %slice-start = ((s8[10485760]{0:T(1024)(128)(4,1)}), s8[4194304]{0:T(1024)(128)(4,1)S(1)}, s32[]{:S(2)}) async-start(s8[10485760]{0:T(1024)(128)(4,1)} %bitcast.271), calls=%async_computation.1 | async-start | bytes 8388608
  180.3 27.6 %slice-start.1 = ((s8[10485760]{0:T(1024)(128)(4,1)}), s8[4194304]{0:T(1024)(128)(4,1)S(1)}, s32[]{:S(2)}) async-start(s8[10485760]{0:T(1024)(128)(4,1)} %bitcast.271), calls=%async_computation.2 | async-start | bytes 8388608
  180.3 27.6 %slice-start.2 = ((s8[10485760]{0:T(1024)(128)(4,1)}), s8[2097152]{0:T(1024)(128)(4,1)S(1)}, s32[]{:S(2)}) async-start(s8[10485760]{0:T(1024)(128)(4,1)} %bitcast.271), calls=%async_computation.3 | async-start | bytes 4194304
  192.1 1.9 collective-permute-start.7
  194.0 4.1 %collective-permute-start.8 = (f32[4,4,512]{2,1,0:T(4,128)S(1)}, f32[4,4,512]{2,1,0:T(4,128)S(1)}, u32[]{:S(2)}, u32[]{:S(2)}) collective-permute-start(f32[4,4,512]{2,1,0:T(4,128)S(1)} %pad_maximum_fusion.9), channel_id=1, source_target_pairs={{0,4},{2,6},{4,0},{6,2},{1,5},{3,7},{5,1},{7,3},{8,12},{10,14},{12... | collective-permute-start | bytes 98312 | tf_op jit(solution)/shard_map/ppermute | solution.py:284
  198.2 2.8 %collective-permute-start.9 = (f32[4,4,512]{2,1,0:T(4,128)S(1)}, f32[4,4,512]{2,1,0:T(4,128)S(1)}, u32[]{:S(2)}, u32[]{:S(2)}) collective-permute-start(f32[4,4,512]{2,1,0:T(4,128)S(1)} %pad_maximum_fusion.10), channel_id=1, source_target_pairs={{0,1},{1,0},{2,3},{3,2},{4,5},{5,4},{6,7},{7,6},{8,9},{9,8},{10,11... | collective-permute-start | bytes 98312 | tf_op jit(solution)/shard_map/ppermute | solution.py:284
  201.1 2.8 %collective-permute-start.10 = (f32[4,4,512]{2,1,0:T(4,128)S(1)}, f32[4,4,512]{2,1,0:T(4,128)S(1)}, u32[]{:S(2)}, u32[]{:S(2)}) collective-permute-start(f32[4,4,512]{2,1,0:T(4,128)S(1)} %pad_maximum_fusion.11), channel_id=1, source_target_pairs={{0,8},{8,0},{16,24},{24,16},{1,9},{9,1},{17,25},{25,17},{2,10},{10... | collective-permute-start | bytes 98312 | tf_op jit(solution)/shard_map/ppermute | solution.py:284
  204.0 3.7 %collective-permute-start.11 = (f32[4,4,512]{2,1,0:T(4,128)S(1)}, f32[4,4,512]{2,1,0:T(4,128)S(1)}, u32[]{:S(2)}, u32[]{:S(2)}) collective-permute-start(f32[4,4,512]{2,1,0:T(4,128)S(1)} %pad_maximum_fusion.12), channel_id=1, source_target_pairs={{0,16},{8,24},{16,0},{24,8},{1,17},{9,25},{17,1},{25,9},{2,18},{10... | collective-permute-start | bytes 98312 | tf_op jit(solution)/shard_map/ppermute | solution.py:284
  218.5 5.7 %collective-permute-start.17 = (bf16[2,208,256]{2,1,0:T(8,128)(2,1)S(1)}, bf16[2,208,256]{2,1,0:T(8,128)(2,1)S(1)}, u32[]{:S(2)}, u32[]{:S(2)}) collective-permute-start(bf16[2,208,256]{2,1,0:T(8,128)(2,1)S(1)} %get-tuple-element.29), channel_id=1, source_target_pairs={{0,12},{2,14},{4,8},{6,10},{8,4},{10,6},{12,0},{14,2},{16,28},{18,... | collective-permute-start | bytes 638984 | tf_op jit(solution)/shard_map/ppermute | solution.py:364
  219.7 7.1 %collective-permute-start.18 = (bf16[2,208,256]{2,1,0:T(8,128)(2,1)S(1)}, bf16[2,208,256]{2,1,0:T(8,128)(2,1)S(1)}, u32[]{:S(2)}, u32[]{:S(2)}) collective-permute-start(bf16[2,208,256]{2,1,0:T(8,128)(2,1)S(1)} %get-tuple-element.30), channel_id=1, source_target_pairs={{0,8},{2,10},{4,12},{6,14},{8,0},{10,2},{12,4},{14,6},{16,24},{18,... | collective-permute-start | bytes 638984 | tf_op jit(solution)/shard_map/ppermute | solution.py:364
  221.2 10.7 %collective-permute-start.19 = (bf16[2,208,256]{2,1,0:T(8,128)(2,1)S(1)}, bf16[2,208,256]{2,1,0:T(8,128)(2,1)S(1)}, u32[]{:S(2)}, u32[]{:S(2)}) collective-permute-start(bf16[2,208,256]{2,1,0:T(8,128)(2,1)S(1)} %get-tuple-element.31), channel_id=1, source_target_pairs={{0,4},{2,6},{4,0},{6,2},{8,12},{10,14},{12,8},{14,10},{16,20},{18,... | collective-permute-start | bytes 638984 | tf_op jit(solution)/shard_map/ppermute | solution.py:364
  221.2 19.0 %collective-permute-start.12 = (bf16[2,208,256]{2,1,0:T(8,128)(2,1)S(1)}, bf16[2,208,256]{2,1,0:T(8,128)(2,1)S(1)}, u32[]{:S(2)}, u32[]{:S(2)}) collective-permute-start(bf16[2,208,256]{2,1,0:T(8,128)(2,1)S(1)} %get-tuple-element.25), channel_id=1, source_target_pairs={{0,28},{2,30},{4,24},{6,26},{8,20},{10,22},{12,16},{14,18},{16,12}... | collective-permute-start | bytes 638984 | tf_op jit(solution)/shard_map/ppermute | solution.py:364
  222.7 17.5 %collective-permute-start.13 = (bf16[2,208,256]{2,1,0:T(8,128)(2,1)S(1)}, bf16[2,208,256]{2,1,0:T(8,128)(2,1)S(1)}, u32[]{:S(2)}, u32[]{:S(2)}) collective-permute-start(bf16[2,208,256]{2,1,0:T(8,128)(2,1)S(1)} %get-tuple-element.26), channel_id=1, source_target_pairs={{0,24},{2,26},{4,28},{6,30},{8,16},{10,18},{12,20},{14,22},{16,8},... | collective-permute-start | bytes 638984 | tf_op jit(solution)/shard_map/ppermute | solution.py:364
  224.2 27.1 %collective-permute-start.14 = (bf16[2,208,256]{2,1,0:T(8,128)(2,1)S(1)}, bf16[2,208,256]{2,1,0:T(8,128)(2,1)S(1)}, u32[]{:S(2)}, u32[]{:S(2)}) collective-permute-start(bf16[2,208,256]{2,1,0:T(8,128)(2,1)S(1)} %get-tuple-element.27), channel_id=1, source_target_pairs={{0,20},{2,22},{4,16},{6,18},{8,28},{10,30},{12,24},{14,26},{16,4},... | collective-permute-start | bytes 638984 | tf_op jit(solution)/shard_map/ppermute | solution.py:364
  226.9 29.0 %collective-permute-start.15 = (bf16[2,208,256]{2,1,0:T(8,128)(2,1)S(1)}, bf16[2,208,256]{2,1,0:T(8,128)(2,1)S(1)}, u32[]{:S(2)}, u32[]{:S(2)}) collective-permute-start(bf16[2,208,256]{2,1,0:T(8,128)(2,1)S(1)} %get-tuple-element.28), channel_id=1, source_target_pairs={{0,16},{2,18},{4,20},{6,22},{8,24},{10,26},{12,28},{14,30},{16,0},... | collective-permute-start | bytes 638984 | tf_op jit(solution)/shard_map/ppermute | solution.py:364
  232.0 28.3 %collective-permute-start.20 = (bf16[4,208,256]{2,1,0:T(8,128)(2,1)S(1)}, bf16[4,208,256]{2,1,0:T(8,128)(2,1)S(1)}, u32[]{:S(2)}, u32[]{:S(2)}) collective-permute-start(bf16[4,208,256]{2,1,0:T(8,128)(2,1)S(1)} %pad_maximum_fusion.8), channel_id=1, source_target_pairs={{0,2},{2,0},{4,6},{6,4},{1,3},{3,1},{5,7},{7,5},{8,10},{10,8},{12,... | collective-permute-start | bytes 1277960 | tf_op jit(solution)/shard_map/ppermute | solution.py:312
  255.9 5.8 %collective-permute-start.16 = (bf16[4,208,256]{2,1,0:T(8,128)(2,1)S(1)}, bf16[4,208,256]{2,1,0:T(8,128)(2,1)S(1)}, u32[]{:S(2)}, u32[]{:S(2)}) collective-permute-start(bf16[4,208,256]{2,1,0:T(8,128)(2,1)S(1)} %pad_maximum_fusion.7), channel_id=1, source_target_pairs={{0,2},{2,0},{4,6},{6,4},{1,3},{3,1},{5,7},{7,5},{8,10},{10,8},{12,... | collective-permute-start | bytes 1277960 | tf_op jit(solution)/shard_map/ppermute | solution.py:312

commit v7 on v6

--- a/solution.py
+++ b/solution.py
@@ -179,7 +179,7 @@
 
     wide_rows[...] = blend(0, wide, lambda c: heads_ref[c, 0, :depth])
     slim_rows[...] = blend(wide, lanes, lambda c: padded([unfolded(heads_ref[c, 0, depth:], fold)], slim))
-    pair = outs[0].shape[0]
+    pair = 2
     halves = len(outs) // ckpts
     own = depth // (pair * halves)
     height = own // fold
@@ -187,16 +187,18 @@
 
         @pl.when(pl.program_id(0) == plane)
         def _():
-            for far in range(pair * halves):
-                out_ref, slot = outs[plane * halves + far // pair], far % pair
-                first = pl.multiple_of((place_ref[1] ^ far) * own, own)
-                out_ref[slot, :own] = wide_rows[pl.ds(first, own)].astype(out_ref.dtype)
-                rows = slim_rows[pl.ds(first, own)]
-                block = jnp.concatenate(
-                    [rows[q * height : (q + 1) * height, : slim // 2] for q in range(fold)], axis=1
-                )
-                rest = jnp.zeros((out_ref.shape[1] - own - height, wide), jnp.float32)
-                out_ref[slot, own:] = jnp.concatenate([block, rest], axis=0).astype(out_ref.dtype)
+            for half in range(halves):
+                out_ref, folded = outs[plane * halves + half], []
+                for slot in range(pair):
+                    first = pl.multiple_of((place_ref[1] ^ (half * pair + slot)) * own, own)
+                    out_ref[slot * own : (slot + 1) * own] = wide_rows[pl.ds(first, own)].astype(out_ref.dtype)
+                    rows = slim_rows[pl.ds(first, own)]
+                    folded.append(
+                        jnp.concatenate(
+                            [rows[q * height : (q + 1) * height, : slim // 2] for q in range(fold)], axis=1
+                        )
+                    )
+                out_ref[pair * own :] = jnp.concatenate(folded, axis=0).astype(out_ref.dtype)
 
 
 def merge(place, scales, prior, logits, table, labels, ids, hidden_sq, heads, ntok):
@@ -204,8 +206,7 @@
     tokens, lanes = logits.shape[1:]
     depth = hidden_sq.shape[1] // blocks
     own = depth // ntok
-    tall = own + -(-own * (lanes - width) // 2 // width // 16) * 16
-    shape = (2, tall, width)
+    shape = (2 * own + own * (lanes - width) // width, width)
 
     def whole(x):
         return pl.BlockSpec(x.shape, lambda i, s: (0,) * x.ndim)
@@ -222,7 +223,7 @@
                 pl.BlockSpec(memory_space=pltpu.VMEM),
                 pl.BlockSpec((ckpts, 1, *heads.shape[2:]), lambda i, s: (0, s[0] ^ i, 0, 0)),
             ],
-            out_specs=[pl.BlockSpec(shape, lambda i, s: (0, 0, 0))] * (blocks * ntok // 2),
+            out_specs=[pl.BlockSpec(shape, lambda i, s: (0, 0))] * (blocks * ntok // 2),
             scratch_shapes=[
                 pltpu.VMEM((depth, width), jnp.float32),
                 pltpu.VMEM((depth, lanes - width), jnp.float32),
@@ -235,15 +236,20 @@
 def assemble_kernel(mine_ref, *refs, sources):
     arrays, out_ref = refs[:-1], refs[-1]
     own, columns = out_ref.shape
-    wide = arrays[0].shape[2]
+    wide = arrays[0].shape[-1]
     narrow = columns // len(sources) - wide
     fold = wide // narrow
     height = own // fold
     mine = mine_ref[0]
     slim = []
     for r, (array, slot) in enumerate(sources):
-        out_ref[:, pl.ds(pl.multiple_of((mine ^ r) * wide, wide), wide)] = arrays[array][slot, :own]
-        slim.append(unfolded(arrays[array][slot, own:].astype(jnp.float32)[:height], fold))
+        ref = arrays[array]
+        if slot is None:
+            block, rest = ref[:own], ref[2 * own :]
+        else:
+            block, rest = ref[slot, :own], ref[slot, own:]
+        out_ref[:, pl.ds(pl.multiple_of((mine ^ r) * wide, wide), wide)] = block
+        slim.append(unfolded(rest.astype(jnp.float32)[:height], fold))
     for r in range(0, len(sources), 2):
         ours, theirs = slim[r], slim[r + 1]
         odd = mine % 2 == 1
@@ -362,11 +368,22 @@
         r, part = 2 * half, parts[half]
         if r:
             part = lax.ppermute(part, BOTH, [(g, g ^ r) for g in range(peers)])
-        sources[r] = (len(arrays), 0)
+        sources[r] = (len(arrays), None)
         arrays.append(part)
         seconds.append((r + 1, part))
         if half in (peers // 4, 0):
-            handed = other(jnp.stack([x[1] for _, x in seconds]), "tok", 1)
+            own_rows = depth // ntok
+            height = own_rows // fold
+            pad = jnp.zeros((-height % 16, wide), jnp.bfloat16)
+            handed = other(
+                jnp.stack(
+                    [
+                        jnp.concatenate([x[own_rows : 2 * own_rows], x[2 * own_rows + height :], pad])
+                        for _, x in seconds
+                    ]
+                ),
+                "tok", 1,
+            )
             for slot, (s, _) in enumerate(seconds):
                 sources[s] = (len(arrays), slot)
             arrays.append(handed)

time: 268 us -> 267 us (level)
  starting transfers between devices: 47.3 us -> 38.6 us
  waiting for transfers between devices: 158 us -> 166 us
    ppermute x7, waiting for transfers between devices: 19.6 us -> 27.6 us  [shards(): part = lax.ppermute(part, BOTH, [(g, g ^ r) for g in range(peers)])]
    ppermute x9, starting transfers between devices: 25.1 us -> 18 us  [other(): lax.ppermute(x, axis, [(i, i ^ far) for i in range(lax.axis_size(axis))])]
  transfers between devices with their start and end apart: 22 -> 22, of which waited for: 17 -> 18; matrix products, arithmetic and copies ran while one was open for 6% -> 6% of each run, Pallas kernels for 4% -> 4%
where the time goes in v7:
time: 267 us; the launch traced here: 264 us
  waiting for transfers between devices  166 us (62%)
  starting transfers between devices  38.6 us (14%)
  Pallas kernels  34.5 us (13%)
  other arithmetic  16.8 us (6%)
  local copies, waits for them, and re-layouts  6.68 us (3%)
    ppermute x9, waiting for transfers between devices, other(): lax.ppermute(x, axis, [(i, i ^ far) for i in range(lax.axis_size(axis))])  93.9 us
    all_to_all x1, waiting for transfers between devices, exchange(): return lax.all_to_all(x, BOTH, 0, 0, tiled=True)  36.4 us
    ppermute x7, waiting for transfers between devices, shards(): part = lax.ppermute(part, BOTH, [(g, g ^ r) for g in range(peers)])  27.6 us
    ppermute x9, starting transfers between devices, other(): lax.ppermute(x, axis, [(i, i ^ far) for i in range(lax.axis_size(axis))])  18 us
    pallas_call x1, Pallas kernels, score(): call(score_kernel, 'score', out_shape=(pltpu.VMEM((ckpts, tokens, lanes),...  11.7 us
    pallas_call x1, Pallas kernels, merge(): call(functools.partial(merge_kernel, prior=prior), 'merge', out_shape=[ja...  10.6 us
    select_n x7, other arithmetic, paired(): return jnp.concatenate([jnp.where(upper, y, x), jnp.where(upper, x, y)])  8.63 us
    ppermute x5, waiting for transfers between devices, everywhere(): other = lax.ppermute(stats, axis, [(i, i ^ far) for i in range(size)])  8.56 us
  transfers between devices with their start and end apart: 22, of which 18 were waited for; matrix products, arithmetic and copies ran while one was open for 6% of the time, Pallas kernels for 4%

profile of v7, /device:TPU:9, one launch (start us, length us, event | category | flops | bytes accessed | tf_op | source)
XLA Modules:
  0.0 263.5 jit_solution(11967197076161465430)
XLA Ops:
  0.0 1.0 constant_dynamic-slice_fusion
  1.1 2.5 collective-permute-start.1
  3.7 0.7 fusion.43
  4.4 0.7 fusion.45
  5.3 4.8 %pack.1 = bf16[16,5,160,256]{3,2,1,0:T(8,128)(2,1)S(1)} custom-call(bf16[640,5120]{1,0:T(8,128)(2,1)} %bitcast.289, bf16[640,5120]{1,0:T(8,128)(2,1)} %bitcast.290, bf16[640,5120]{1,0:T(8,128)(2,1)} %bitcast.291, bf16[640,5120]{1,0:T(8,128)(2,1)} %bitcast.292), custom_call_target="tpu_custom_call" | custom-call | tf_op jit(solution)/shard_map/pack/pallas_call | solution.py:48
  10.2 3.8 %collective-permute-done.2 = bf16[1,64,2560]{2,1,0:T(8,128)(2,1)S(1)} collective-permute-done((bf16[1,64,2560]{2,1,0:T(8,128)(2,1)S(1)}, bf16[1,64,2560]{2,1,0:T(8,128)(2,1)S(1)}, u32[]{:S(2)}, u32[]{:S(2)}) %collective-permute-start.2) | collective-permute-done | bytes 327712 | tf_op jit(solution)/shard_map/ppermute | solution.py:318
  14.1 3.6 %collective-permute-done.1 = bf16[1,64,2560]{2,1,0:T(8,128)(2,1)S(1)} collective-permute-done((bf16[1,64,2560]{2,1,0:T(8,128)(2,1)S(1)}, bf16[1,64,2560]{2,1,0:T(8,128)(2,1)S(1)}, u32[]{:S(2)}, u32[]{:S(2)}) %collective-permute-start.1) | collective-permute-done | bytes 327712 | tf_op jit(solution)/shard_map/ppermute | solution.py:318
  17.7 13.9 %collective-permute-done = bf16[1,64,2560]{2,1,0:T(8,128)(2,1)S(1)} collective-permute-done((bf16[1,64,2560]{2,1,0:T(8,128)(2,1)S(1)}, bf16[1,64,2560]{2,1,0:T(8,128)(2,1)S(1)}, u32[]{:S(2)}, u32[]{:S(2)}) %collective-permute-start) | collective-permute-done | bytes 327712 | tf_op jit(solution)/shard_map/ppermute | solution.py:318
  32.1 1.3 collective-permute-start.3
  33.4 6.1 %all-to-all-start = ((bf16[16,800,256]{2,1,0:T(8,128)(2,1)}), bf16[16,800,256]{2,1,0:T(8,128)(2,1)}, u32[]{:S(2)}, u32[]{:S(2)}) async-start(bf16[16,800,256]{2,1,0:T(8,128)(2,1)} %bitcast.286), calls=%async_computation | async-start | bytes 13107200 | tf_op jit(solution)/shard_map/all_to_all | solution.py:275
  39.5 1.2 collective-permute-start.5
  40.7 37.9 %collective-permute-done.3 = bf16[1,4,64,2688]{3,2,1,0:T(8,128)(2,1)S(1)} collective-permute-done((bf16[1,4,64,2688]{3,2,1,0:T(8,128)(2,1)S(1)}, bf16[1,4,64,2688]{3,2,1,0:T(8,128)(2,1)S(1)}, u32[]{:S(2)}, u32[]{:S(2)}) %collective-permute-start.3) | collective-permute-done | bytes 1376288 | tf_op jit(solution)/shard_map/ppermute | solution.py:318
  78.6 1.2 collective-permute-start.4
  79.8 1.6 broadcast_select_fusion.5
  81.4 23.9 %collective-permute-done.4 = bf16[1,4,64,2688]{3,2,1,0:T(8,128)(2,1)} collective-permute-done((bf16[1,4,64,2688]{3,2,1,0:T(8,128)(2,1)S(1)}, bf16[1,4,64,2688]{3,2,1,0:T(8,128)(2,1)}, u32[]{:S(2)}, u32[]{:S(2)}) %collective-permute-start.4) | collective-permute-done | bytes 1376288 | tf_op jit(solution)/shard_map/ppermute | solution.py:318
  105.3 1.6 broadcast_select_fusion.7
  106.9 0.7 broadcast_select_fusion.3
  107.6 3.3 %pad_maximum_fusion.1 = bf16[4,4,64,2688]{3,2,1,0:T(8,128)(2,1)} fusion(bf16[2,4,64,2688]{3,2,1,0:T(8,128)(2,1)S(1)} %get-tuple-element.47, bf16[2,4,64,2688]{3,2,1,0:T(8,128)(2,1)S(1)} %get-tuple-element.46), kind=kLoop, calls=%fused_computation.3 | loop fusion | flops 2752512 | bytes 11010048 | tf_op jit(solution)/shard_map/concatenate | solution.py:322
  110.9 6.0 %collective-permute-start.6 = (bf16[4,4,64,2688]{3,2,1,0:T(8,128)(2,1)}, bf16[4,4,64,2688]{3,2,1,0:T(8,128)(2,1)}, u32[]{:S(2)}, u32[]{:S(2)}) collective-permute-start(bf16[4,4,64,2688]{3,2,1,0:T(8,128)(2,1)} %pad_maximum_fusion.1), channel_id=1, source_target_pairs={{0,2},{2,0},{4,6},{6,4},{1,3},{3,1},{5,7},{7,5},{8,10},{10,8},{12,... | collective-permute-start | bytes 16515080 | tf_op jit(solution)/shard_map/ppermute | solution.py:318
  117.0 8.9 %collective-permute-done.6 = bf16[4,4,64,2688]{3,2,1,0:T(8,128)(2,1)} collective-permute-done((bf16[4,4,64,2688]{3,2,1,0:T(8,128)(2,1)}, bf16[4,4,64,2688]{3,2,1,0:T(8,128)(2,1)}, u32[]{:S(2)}, u32[]{:S(2)}) %collective-permute-start.6) | collective-permute-done | bytes 5505056 | tf_op jit(solution)/shard_map/ppermute | solution.py:318
  125.9 4.4 %broadcast_select_fusion.1 = (bf16[4,4,64,2688]{3,2,1,0:T(8,128)(2,1)S(1)}, bf16[4,4,64,2688]{3,2,1,0:T(8,128)(2,1)S(1)}) fusion(bf16[4,4,64,2688]{3,2,1,0:T(8,128)(2,1)} %collective-permute-done.6, pred[]{:T(512)S(6)} %eq.28, bf16[2,4,64,2688]{3,2,1,0:T(8,128)(2,1)} %copy-done.4, bf16[2,4,64,2688]{3,2,1,0:T(8,128)(2,1)S(1)} %get-tuple-element.46), kind=kLoop, calls=%fused_computation.5 | loop fusion | flops 8257536 | bytes 22020096 | tf_op jit(solution)/shard_map/jit(_where)/select_n | solution.py:322
  130.4 2.4 copy-done.3
  132.7 1.2 pad_maximum_fusion.states_ref
  133.9 5.8 %squares.1 = (bf16[4,2560,512]{2,1,0:T(8,128)(2,1)S(1)}, f32[4,1,512]{2,1,0:T(1,128)S(1)}) custom-call(bf16[8,4,64,2688]{3,2,1,0:T(8,128)(2,1)S(1)} %pad_maximum_fusion.states_ref), custom_call_target="tpu_custom_call" | custom-call | tf_op jit(solution)/shard_map/squares/pallas_call | solution.py:79
  139.8 0.9 fusion.2
  140.7 2.9 %copy-done.2 = bf16[4,2560,512]{2,1,0:T(8,128)(2,1)} copy-done((bf16[4,2560,512]{2,1,0:T(8,128)(2,1)}, bf16[4,2560,512]{2,1,0:T(8,128)(2,1)S(1)}, u32[]{:S(2)}) %copy-start.2) | copy-done | bytes 10485784
  143.9 36.4 %all-to-all-done = bf16[16,800,256]{2,1,0:T(8,128)(2,1)} async-done(((bf16[16,800,256]{2,1,0:T(8,128)(2,1)}), bf16[16,800,256]{2,1,0:T(8,128)(2,1)}, u32[]{:S(2)}, u32[]{:S(2)}) %all-to-all-start) | async-done | bytes 6553632 | tf_op jit(solution)/shard_map/all_to_all | solution.py:275
  180.4 11.7 %score.1 = (f32[4,512,384]{2,1,0:T(8,128)S(1)}, f32[4,8,512]{2,1,0:T(8,128)S(1)}) custom-call(bf16[8,4,64,2688]{3,2,1,0:T(8,128)(2,1)} %copy-done, bf16[4,4,800,256]{3,2,1,0:T(8,128)(2,1)} %bitcast.9.heads_ref, s32[512,1]{1,0:T(8,128)S(1)} %fusion.labels_ref, s32[1,384]{1,0:T(1,128)S(1)} %broadcast_in_dim.18.ids_ref), custom_call_target="tpu_custom_call" | custom-call | tf_op jit(solution)/shard_map/score/pallas_call | solution.py:131
  192.1 1.0 collective-permute-start.7
  193.1 0.9 collective-permute-done.7
  194.0 2.8 %collective-permute-start.8 = (f32[4,4,512]{2,1,0:T(4,128)S(1)}, f32[4,4,512]{2,1,0:T(4,128)S(1)}, u32[]{:S(2)}, u32[]{:S(2)}) collective-permute-start(f32[4,4,512]{2,1,0:T(4,128)S(1)} %pad_maximum_fusion.9), channel_id=1, source_target_pairs={{0,4},{2,6},{4,0},{6,2},{1,5},{3,7},{5,1},{7,3},{8,12},{10,14},{12... | collective-permute-start | bytes 98312 | tf_op jit(solution)/shard_map/ppermute | solution.py:290
  196.8 1.3 collective-permute-done.8
  198.2 1.3 collective-permute-start.9
  199.5 1.5 collective-permute-done.9
  201.2 2.8 %collective-permute-done.10 = f32[4,4,512]{2,1,0:T(4,128)S(1)} collective-permute-done((f32[4,4,512]{2,1,0:T(4,128)S(1)}, f32[4,4,512]{2,1,0:T(4,128)S(1)}, u32[]{:S(2)}, u32[]{:S(2)}) %collective-permute-start.10) | collective-permute-done | bytes 32800 | tf_op jit(solution)/shard_map/ppermute | solution.py:290
  204.0 1.5 collective-permute-start.11
  205.6 2.1 collective-permute-done.11
  208.0 10.6 %merge.1 = (bf16[400,256]{1,0:T(8,128)(2,1)S(1)}, bf16[400,256]{1,0:T(8,128)(2,1)S(1)}, bf16[400,256]{1,0:T(8,128)(2,1)S(1)}, bf16[400,256]{1,0:T(8,128)(2,1)S(1...) custom-call(s32[2]{0:T(128)S(1)} %pad_add_fusion.1.place_ref, ...), custom_call_target="tpu_custom_call" | custom-call | tf_op jit(solution)/shard_map/merge/pallas_call | solution.py:214
  218.6 1.6 collective-permute-start.12
  220.2 1.1 collective-permute-start.13
  221.3 3.0 %collective-permute-start.14 = (bf16[400,256]{1,0:T(8,128)(2,1)S(1)}, bf16[400,256]{1,0:T(8,128)(2,1)S(1)}, u32[]{:S(2)}, u32[]{:S(2)}) collective-permute-start(bf16[400,256]{1,0:T(8,128)(2,1)S(1)} %get-tuple-element.27), channel_id=1, source_target_pairs={{0,20},{2,22},{4,16},{6,18},{8,28},{10,30},{12,24},{14,26},{16,4},... | collective-permute-start | bytes 614408 | tf_op jit(solution)/shard_map/ppermute | solution.py:370
  224.5 1.8 collective-permute-start.17
  226.3 17.9 %collective-permute-done.12.refs_0_ = bf16[400,256]{1,0:T(8,128)(2,1)S(1)} collective-permute-done((bf16[400,256]{1,0:T(8,128)(2,1)S(1)}, bf16[400,256]{1,0:T(8,128)(2,1)S(1)}, u32[]{:S(2)}, u32[]{:S(2)}) %collective-permute-start.12) | collective-permute-done | bytes 204832 | tf_op jit(solution)/shard_map/ppermute | solution.py:370
  244.3 4.7 %collective-permute-done.13.refs_1_ = bf16[400,256]{1,0:T(8,128)(2,1)S(1)} collective-permute-done((bf16[400,256]{1,0:T(8,128)(2,1)S(1)}, bf16[400,256]{1,0:T(8,128)(2,1)S(1)}, u32[]{:S(2)}, u32[]{:S(2)}) %collective-permute-start.13) | collective-permute-done | bytes 204832 | tf_op jit(solution)/shard_map/ppermute | solution.py:370
  249.7 4.4 %collective-permute-done.15.refs_3_ = bf16[400,256]{1,0:T(8,128)(2,1)S(1)} collective-permute-done((bf16[400,256]{1,0:T(8,128)(2,1)S(1)}, bf16[400,256]{1,0:T(8,128)(2,1)S(1)}, u32[]{:S(2)}, u32[]{:S(2)}) %collective-permute-start.15) | collective-permute-done | bytes 204832 | tf_op jit(solution)/shard_map/ppermute | solution.py:370
  254.5 5.4 %collective-permute-start.16 = (bf16[4,208,256]{2,1,0:T(8,128)(2,1)S(1)}, bf16[4,208,256]{2,1,0:T(8,128)(2,1)S(1)}, u32[]{:S(2)}, u32[]{:S(2)}) collective-permute-start(bf16[4,208,256]{2,1,0:T(8,128)(2,1)S(1)} %pad_maximum_fusion.7), channel_id=1, source_target_pairs={{0,2},{2,0},{4,6},{6,4},{1,3},{3,1},{5,7},{7,5},{8,10},{10,8},{12,... | collective-permute-start | bytes 1277960 | tf_op jit(solution)/shard_map/ppermute | solution.py:318
  260.1 1.3 collective-permute-done.16.refs_4_
  261.9 1.6 assemble.1
  (84 shorter events, 3.8 us)
Async XLA Ops:
  1.0 13.0 %collective-permute-start.2 = (bf16[1,64,2560]{2,1,0:T(8,128)(2,1)S(1)}, bf16[1,64,2560]{2,1,0:T(8,128)(2,1)S(1)}, u32[]{:S(2)}, u32[]{:S(2)}) collective-permute-start(bf16[1,64,2560]{2,1,0:T(8,128)(2,1)S(1)} %constant_dynamic-slice_fusion), channel_id=1, source_target_pairs={{0,8},{8,0},{16,24},{24,16},{1,9},{9,1},{17,25},{25,17},{2,10},{10... | collective-permute-start | bytes 983048 | tf_op jit(solution)/shard_map/ppermute | solution.py:318
  1.1 16.6 %collective-permute-start.1 = (bf16[1,64,2560]{2,1,0:T(8,128)(2,1)S(1)}, bf16[1,64,2560]{2,1,0:T(8,128)(2,1)S(1)}, u32[]{:S(2)}, u32[]{:S(2)}) collective-permute-start(bf16[1,64,2560]{2,1,0:T(8,128)(2,1)S(1)} %constant_dynamic-slice_fusion), channel_id=1, source_target_pairs={{0,16},{8,24},{16,0},{24,8},{1,17},{9,25},{17,1},{25,9},{2,18},{10... | collective-permute-start | bytes 983048 | tf_op jit(solution)/shard_map/ppermute | solution.py:318
  3.5 28.1 %collective-permute-start = (bf16[1,64,2560]{2,1,0:T(8,128)(2,1)S(1)}, bf16[1,64,2560]{2,1,0:T(8,128)(2,1)S(1)}, u32[]{:S(2)}, u32[]{:S(2)}) collective-permute-start(bf16[1,64,2560]{2,1,0:T(8,128)(2,1)S(1)} %constant_dynamic-slice_fusion), channel_id=1, source_target_pairs={{0,24},{8,16},{16,8},{24,0},{1,25},{9,17},{17,9},{25,1},{2,26},{10... | collective-permute-start | bytes 983048 | tf_op jit(solution)/shard_map/ppermute | solution.py:318
  5.3 8.7 %copy-start.5 = (bf16[1,128,2560]{2,1,0:T(8,128)(2,1)S(1)}, bf16[1,128,2560]{2,1,0:T(8,128)(2,1)}, u32[]{:S(2)}) copy-start(bf16[1,128,2560]{2,1,0:T(8,128)(2,1)} %param.4) | copy-start | bytes 1966084
  10.2 21.8 %copy-start.1 = (bf16[16,5,160,256]{3,2,1,0:T(8,128)(2,1)}, bf16[16,5,160,256]{3,2,1,0:T(8,128)(2,1)S(1)}, u32[]{:S(2)}) copy-start(bf16[16,5,160,256]{3,2,1,0:T(8,128)(2,1)S(1)} %pack.1) | copy-start | bytes 19660804
  32.1 46.5 %collective-permute-start.3 = (bf16[1,4,64,2688]{3,2,1,0:T(8,128)(2,1)S(1)}, bf16[1,4,64,2688]{3,2,1,0:T(8,128)(2,1)S(1)}, u32[]{:S(2)}, u32[]{:S(2)}) collective-permute-start(bf16[1,4,64,2688]{3,2,1,0:T(8,128)(2,1)S(1)} %pad_maximum_fusion.4), channel_id=1, source_target_pairs={{0,4},{2,6},{4,0},{6,2},{1,5},{3,7},{5,1},{7,3},{8,12},{10,14},{12... | collective-permute-start | bytes 4128776 | tf_op jit(solution)/shard_map/ppermute | solution.py:318
  33.4 147.0 %all-to-all-start = ((bf16[16,800,256]{2,1,0:T(8,128)(2,1)}), bf16[16,800,256]{2,1,0:T(8,128)(2,1)}, u32[]{:S(2)}, u32[]{:S(2)}) async-start(bf16[16,800,256]{2,1,0:T(8,128)(2,1)} %bitcast.286), calls=%async_computation | async-start | bytes 13107200 | tf_op jit(solution)/shard_map/all_to_all | solution.py:275
  39.5 40.4 %collective-permute-start.5 = (bf16[1,4,64,2688]{3,2,1,0:T(8,128)(2,1)S(1)}, bf16[1,4,64,2688]{3,2,1,0:T(8,128)(2,1)}, u32[]{:S(2)}, u32[]{:S(2)}) collective-permute-start(bf16[1,4,64,2688]{3,2,1,0:T(8,128)(2,1)S(1)} %pad_maximum_fusion.4), channel_id=1, source_target_pairs={{0,1},{1,0},{2,3},{3,2},{4,5},{5,4},{6,7},{7,6},{8,9},{9,8},{10,11... | collective-permute-start | bytes 4128776 | tf_op jit(solution)/shard_map/ppermute | solution.py:318
  78.6 26.7 %collective-permute-start.4 = (bf16[1,4,64,2688]{3,2,1,0:T(8,128)(2,1)S(1)}, bf16[1,4,64,2688]{3,2,1,0:T(8,128)(2,1)}, u32[]{:S(2)}, u32[]{:S(2)}) collective-permute-start(bf16[1,4,64,2688]{3,2,1,0:T(8,128)(2,1)S(1)} %collective-permute-done.3), channel_id=1, source_target_pairs={{0,1},{1,0},{2,3},{3,2},{4,5},{5,4},{6,7},{7,6},{8,9},{9,8},{10,11... | collective-permute-start | bytes 4128776 | tf_op jit(solution)/shard_map/ppermute | solution.py:318
  107.6 3.3 %copy-start.4 = (bf16[2,4,64,2688]{3,2,1,0:T(8,128)(2,1)}, bf16[2,4,64,2688]{3,2,1,0:T(8,128)(2,1)S(1)}, u32[]{:S(2)}) copy-start(bf16[2,4,64,2688]{3,2,1,0:T(8,128)(2,1)S(1)} %get-tuple-element.47) | copy-start | bytes 8257540
  110.9 15.0 %collective-permute-start.6 = (bf16[4,4,64,2688]{3,2,1,0:T(8,128)(2,1)}, bf16[4,4,64,2688]{3,2,1,0:T(8,128)(2,1)}, u32[]{:S(2)}, u32[]{:S(2)}) collective-permute-start(bf16[4,4,64,2688]{3,2,1,0:T(8,128)(2,1)} %pad_maximum_fusion.1), channel_id=1, source_target_pairs={{0,2},{2,0},{4,6},{6,4},{1,3},{3,1},{5,7},{7,5},{8,10},{10,8},{12,... | collective-permute-start | bytes 16515080 | tf_op jit(solution)/shard_map/ppermute | solution.py:318
  130.3 2.4 copy-start.3
  133.9 5.8 %copy-start = (bf16[8,4,64,2688]{3,2,1,0:T(8,128)(2,1)}, bf16[8,4,64,2688]{3,2,1,0:T(8,128)(2,1)S(1)}, u32[]{:S(2)}) copy-start(bf16[8,4,64,2688]{3,2,1,0:T(8,128)(2,1)S(1)} %pad_maximum_fusion.states_ref) | copy-start | bytes 33030148
  139.8 3.9 %copy-start.2 = (bf16[4,2560,512]{2,1,0:T(8,128)(2,1)}, bf16[4,2560,512]{2,1,0:T(8,128)(2,1)S(1)}, u32[]{:S(2)}) copy-start(bf16[4,2560,512]{2,1,0:T(8,128)(2,1)S(1)} %get-tuple-element.24.hidden_ref) | copy-start | bytes 31457284
  180.3 27.6 %slice-start = ((s8[10485760]{0:T(1024)(128)(4,1)}), s8[4194304]{0:T(1024)(128)(4,1)S(1)}, s32[]{:S(2)}) async-start(s8[10485760]{0:T(1024)(128)(4,1)} %bitcast.287), calls=%async_computation.1 | async-start | bytes 8388608
  180.3 27.6 %slice-start.1 = ((s8[10485760]{0:T(1024)(128)(4,1)}), s8[4194304]{0:T(1024)(128)(4,1)S(1)}, s32[]{:S(2)}) async-start(s8[10485760]{0:T(1024)(128)(4,1)} %bitcast.287), calls=%async_computation.2 | async-start | bytes 8388608
  180.4 27.6 %slice-start.2 = ((s8[10485760]{0:T(1024)(128)(4,1)}), s8[2097152]{0:T(1024)(128)(4,1)S(1)}, s32[]{:S(2)}) async-start(s8[10485760]{0:T(1024)(128)(4,1)} %bitcast.287), calls=%async_computation.3 | async-start | bytes 4194304
  192.1 1.9 collective-permute-start.7
  194.0 4.1 %collective-permute-start.8 = (f32[4,4,512]{2,1,0:T(4,128)S(1)}, f32[4,4,512]{2,1,0:T(4,128)S(1)}, u32[]{:S(2)}, u32[]{:S(2)}) collective-permute-start(f32[4,4,512]{2,1,0:T(4,128)S(1)} %pad_maximum_fusion.9), channel_id=1, source_target_pairs={{0,4},{2,6},{4,0},{6,2},{1,5},{3,7},{5,1},{7,3},{8,12},{10,14},{12... | collective-permute-start | bytes 98312 | tf_op jit(solution)/shard_map/ppermute | solution.py:290
  198.2 2.8 %collective-permute-start.9 = (f32[4,4,512]{2,1,0:T(4,128)S(1)}, f32[4,4,512]{2,1,0:T(4,128)S(1)}, u32[]{:S(2)}, u32[]{:S(2)}) collective-permute-start(f32[4,4,512]{2,1,0:T(4,128)S(1)} %pad_maximum_fusion.10), channel_id=1, source_target_pairs={{0,1},{1,0},{2,3},{3,2},{4,5},{5,4},{6,7},{7,6},{8,9},{9,8},{10,11... | collective-permute-start | bytes 98312 | tf_op jit(solution)/shard_map/ppermute | solution.py:290
  201.1 2.8 %collective-permute-start.10 = (f32[4,4,512]{2,1,0:T(4,128)S(1)}, f32[4,4,512]{2,1,0:T(4,128)S(1)}, u32[]{:S(2)}, u32[]{:S(2)}) collective-permute-start(f32[4,4,512]{2,1,0:T(4,128)S(1)} %pad_maximum_fusion.11), channel_id=1, source_target_pairs={{0,8},{8,0},{16,24},{24,16},{1,9},{9,1},{17,25},{25,17},{2,10},{10... | collective-permute-start | bytes 98312 | tf_op jit(solution)/shard_map/ppermute | solution.py:290
  204.0 3.7 %collective-permute-start.11 = (f32[4,4,512]{2,1,0:T(4,128)S(1)}, f32[4,4,512]{2,1,0:T(4,128)S(1)}, u32[]{:S(2)}, u32[]{:S(2)}) collective-permute-start(f32[4,4,512]{2,1,0:T(4,128)S(1)} %pad_maximum_fusion.12), channel_id=1, source_target_pairs={{0,16},{8,24},{16,0},{24,8},{1,17},{9,25},{17,1},{25,9},{2,18},{10... | collective-permute-start | bytes 98312 | tf_op jit(solution)/shard_map/ppermute | solution.py:290
  218.6 25.7 %collective-permute-start.12 = (bf16[400,256]{1,0:T(8,128)(2,1)S(1)}, bf16[400,256]{1,0:T(8,128)(2,1)S(1)}, u32[]{:S(2)}, u32[]{:S(2)}) collective-permute-start(bf16[400,256]{1,0:T(8,128)(2,1)S(1)} %get-tuple-element.25), channel_id=1, source_target_pairs={{0,28},{2,30},{4,24},{6,26},{8,20},{10,22},{12,16},{14,18},{16,12}... | collective-permute-start | bytes 614408 | tf_op jit(solution)/shard_map/ppermute | solution.py:370
  220.2 28.8 %collective-permute-start.13 = (bf16[400,256]{1,0:T(8,128)(2,1)S(1)}, bf16[400,256]{1,0:T(8,128)(2,1)S(1)}, u32[]{:S(2)}, u32[]{:S(2)}) collective-permute-start(bf16[400,256]{1,0:T(8,128)(2,1)S(1)} %get-tuple-element.26), channel_id=1, source_target_pairs={{0,24},{2,26},{4,28},{6,30},{8,16},{10,18},{12,20},{14,22},{16,8},... | collective-permute-start | bytes 614408 | tf_op jit(solution)/shard_map/ppermute | solution.py:370
  221.3 28.4 %collective-permute-start.14 = (bf16[400,256]{1,0:T(8,128)(2,1)S(1)}, bf16[400,256]{1,0:T(8,128)(2,1)S(1)}, u32[]{:S(2)}, u32[]{:S(2)}) collective-permute-start(bf16[400,256]{1,0:T(8,128)(2,1)S(1)} %get-tuple-element.27), channel_id=1, source_target_pairs={{0,20},{2,22},{4,16},{6,18},{8,28},{10,30},{12,24},{14,26},{16,4},... | collective-permute-start | bytes 614408 | tf_op jit(solution)/shard_map/ppermute | solution.py:370
  224.2 29.9 %collective-permute-start.15 = (bf16[400,256]{1,0:T(8,128)(2,1)S(1)}, bf16[400,256]{1,0:T(8,128)(2,1)S(1)}, u32[]{:S(2)}, u32[]{:S(2)}) collective-permute-start(bf16[400,256]{1,0:T(8,128)(2,1)S(1)} %get-tuple-element.28), channel_id=1, source_target_pairs={{0,16},{2,18},{4,20},{6,22},{8,24},{10,26},{12,28},{14,30},{16,0},... | collective-permute-start | bytes 614408 | tf_op jit(solution)/shard_map/ppermute | solution.py:370
  224.5 29.6 %collective-permute-start.17 = (bf16[400,256]{1,0:T(8,128)(2,1)S(1)}, bf16[400,256]{1,0:T(8,128)(2,1)S(1)}, u32[]{:S(2)}, u32[]{:S(2)}) collective-permute-start(bf16[400,256]{1,0:T(8,128)(2,1)S(1)} %get-tuple-element.29), channel_id=1, source_target_pairs={{0,12},{2,14},{4,8},{6,10},{8,4},{10,6},{12,0},{14,2},{16,28},{18,... | collective-permute-start | bytes 614408 | tf_op jit(solution)/shard_map/ppermute | solution.py:370
  244.3 9.9 %collective-permute-start.18 = (bf16[400,256]{1,0:T(8,128)(2,1)S(1)}, bf16[400,256]{1,0:T(8,128)(2,1)S(1)}, u32[]{:S(2)}, u32[]{:S(2)}) collective-permute-start(bf16[400,256]{1,0:T(8,128)(2,1)S(1)} %get-tuple-element.30), channel_id=1, source_target_pairs={{0,8},{2,10},{4,12},{6,14},{8,0},{10,2},{12,4},{14,6},{16,24},{18,... | collective-permute-start | bytes 614408 | tf_op jit(solution)/shard_map/ppermute | solution.py:370
  249.0 5.2 %collective-permute-start.19 = (bf16[400,256]{1,0:T(8,128)(2,1)S(1)}, bf16[400,256]{1,0:T(8,128)(2,1)S(1)}, u32[]{:S(2)}, u32[]{:S(2)}) collective-permute-start(bf16[400,256]{1,0:T(8,128)(2,1)S(1)} %get-tuple-element.31), channel_id=1, source_target_pairs={{0,4},{2,6},{4,0},{6,2},{8,12},{10,14},{12,8},{14,10},{16,20},{18,... | collective-permute-start | bytes 614408 | tf_op jit(solution)/shard_map/ppermute | solution.py:370
  254.5 6.8 %collective-permute-start.16 = (bf16[4,208,256]{2,1,0:T(8,128)(2,1)S(1)}, bf16[4,208,256]{2,1,0:T(8,128)(2,1)S(1)}, u32[]{:S(2)}, u32[]{:S(2)}) collective-permute-start(bf16[4,208,256]{2,1,0:T(8,128)(2,1)S(1)} %pad_maximum_fusion.7), channel_id=1, source_target_pairs={{0,2},{2,0},{4,6},{6,4},{1,3},{3,1},{5,7},{7,5},{8,10},{10,8},{12,... | collective-permute-start | bytes 1277960 | tf_op jit(solution)/shard_map/ppermute | solution.py:318
  260.0 1.9 collective-permute-start.20

commit v8 on v7

--- a/solution.py
+++ b/solution.py
@@ -284,7 +284,7 @@
 
 
 def everywhere(stats):
-    for axis in ("tok", "vocab", "ckpt"):
+    for axis in ("tok", "ckpt", "vocab"):
         size, far = lax.axis_size(axis), 1
         while far < size:
             other = lax.ppermute(stats, axis, [(i, i ^ far) for i in range(size)])

time: 267 us -> 267 us (level)
  transfers between devices with their start and end apart: 22 -> 22, of which waited for: 18 -> 17; matrix products, arithmetic and copies ran while one was open for 6% -> 6% of each run, Pallas kernels for 4% -> 4%
where the time goes in v8:
time: 267 us; the launch traced here: 264 us
  waiting for transfers between devices  166 us (62%)
  starting transfers between devices  39.3 us (15%)
  Pallas kernels  34.5 us (13%)
  other arithmetic  16.8 us (6%)
  local copies, waits for them, and re-layouts  6.68 us (3%)
    ppermute x9, waiting for transfers between devices, other(): lax.ppermute(x, axis, [(i, i ^ far) for i in range(lax.axis_size(axis))])  93.9 us
    all_to_all x1, waiting for transfers between devices, exchange(): return lax.all_to_all(x, BOTH, 0, 0, tiled=True)  36.4 us
    ppermute x7, waiting for transfers between devices, shards(): part = lax.ppermute(part, BOTH, [(g, g ^ r) for g in range(peers)])  27 us
    ppermute x9, starting transfers between devices, other(): lax.ppermute(x, axis, [(i, i ^ far) for i in range(lax.axis_size(axis))])  18.2 us
    pallas_call x1, Pallas kernels, score(): call(score_kernel, 'score', out_shape=(pltpu.VMEM((ckpts, tokens, lanes),...  11.7 us
    pallas_call x1, Pallas kernels, merge(): call(functools.partial(merge_kernel, prior=prior), 'merge', out_shape=[ja...  10.6 us
    ppermute x5, waiting for transfers between devices, everywhere(): other = lax.ppermute(stats, axis, [(i, i ^ far) for i in range(size)])  8.67 us
    select_n x7, other arithmetic, paired(): return jnp.concatenate([jnp.where(upper, y, x), jnp.where(upper, x, y)])  8.63 us
  transfers between devices with their start and end apart: 22, of which 17 were waited for; matrix products, arithmetic and copies ran while one was open for 6% of the time, Pallas kernels for 4%

profile of v8, /device:TPU:9, one launch (start us, length us, event | category | flops | bytes accessed | tf_op | source)
XLA Modules:
  0.0 263.8 jit_solution(6689038479218179609)
XLA Ops:
  0.0 1.0 constant_dynamic-slice_fusion
  1.1 2.5 collective-permute-start.1
  3.7 0.7 fusion.43
  4.4 0.7 fusion.45
  5.3 4.8 %pack.1 = bf16[16,5,160,256]{3,2,1,0:T(8,128)(2,1)S(1)} custom-call(bf16[640,5120]{1,0:T(8,128)(2,1)} %bitcast.289, bf16[640,5120]{1,0:T(8,128)(2,1)} %bitcast.290, bf16[640,5120]{1,0:T(8,128)(2,1)} %bitcast.291, bf16[640,5120]{1,0:T(8,128)(2,1)} %bitcast.292), custom_call_target="tpu_custom_call" | custom-call | tf_op jit(solution)/shard_map/pack/pallas_call | solution.py:48
  10.2 3.8 %collective-permute-done.2 = bf16[1,64,2560]{2,1,0:T(8,128)(2,1)S(1)} collective-permute-done((bf16[1,64,2560]{2,1,0:T(8,128)(2,1)S(1)}, bf16[1,64,2560]{2,1,0:T(8,128)(2,1)S(1)}, u32[]{:S(2)}, u32[]{:S(2)}) %collective-permute-start.2) | collective-permute-done | bytes 327712 | tf_op jit(solution)/shard_map/ppermute | solution.py:318
  14.1 3.6 %collective-permute-done.1 = bf16[1,64,2560]{2,1,0:T(8,128)(2,1)S(1)} collective-permute-done((bf16[1,64,2560]{2,1,0:T(8,128)(2,1)S(1)}, bf16[1,64,2560]{2,1,0:T(8,128)(2,1)S(1)}, u32[]{:S(2)}, u32[]{:S(2)}) %collective-permute-start.1) | collective-permute-done | bytes 327712 | tf_op jit(solution)/shard_map/ppermute | solution.py:318
  17.7 13.9 %collective-permute-done = bf16[1,64,2560]{2,1,0:T(8,128)(2,1)S(1)} collective-permute-done((bf16[1,64,2560]{2,1,0:T(8,128)(2,1)S(1)}, bf16[1,64,2560]{2,1,0:T(8,128)(2,1)S(1)}, u32[]{:S(2)}, u32[]{:S(2)}) %collective-permute-start) | collective-permute-done | bytes 327712 | tf_op jit(solution)/shard_map/ppermute | solution.py:318
  32.1 1.3 collective-permute-start.3
  33.4 6.1 %all-to-all-start = ((bf16[16,800,256]{2,1,0:T(8,128)(2,1)}), bf16[16,800,256]{2,1,0:T(8,128)(2,1)}, u32[]{:S(2)}, u32[]{:S(2)}) async-start(bf16[16,800,256]{2,1,0:T(8,128)(2,1)} %bitcast.286), calls=%async_computation | async-start | bytes 13107200 | tf_op jit(solution)/shard_map/all_to_all | solution.py:275
  39.5 1.2 collective-permute-start.5
  40.7 37.9 %collective-permute-done.3 = bf16[1,4,64,2688]{3,2,1,0:T(8,128)(2,1)S(1)} collective-permute-done((bf16[1,4,64,2688]{3,2,1,0:T(8,128)(2,1)S(1)}, bf16[1,4,64,2688]{3,2,1,0:T(8,128)(2,1)S(1)}, u32[]{:S(2)}, u32[]{:S(2)}) %collective-permute-start.3) | collective-permute-done | bytes 1376288 | tf_op jit(solution)/shard_map/ppermute | solution.py:318
  78.6 1.2 collective-permute-start.4
  79.8 1.6 broadcast_select_fusion.5
  81.4 23.9 %collective-permute-done.4 = bf16[1,4,64,2688]{3,2,1,0:T(8,128)(2,1)} collective-permute-done((bf16[1,4,64,2688]{3,2,1,0:T(8,128)(2,1)S(1)}, bf16[1,4,64,2688]{3,2,1,0:T(8,128)(2,1)}, u32[]{:S(2)}, u32[]{:S(2)}) %collective-permute-start.4) | collective-permute-done | bytes 1376288 | tf_op jit(solution)/shard_map/ppermute | solution.py:318
  105.3 1.6 broadcast_select_fusion.7
  106.9 0.7 broadcast_select_fusion.3
  107.6 3.3 %pad_maximum_fusion.1 = bf16[4,4,64,2688]{3,2,1,0:T(8,128)(2,1)} fusion(bf16[2,4,64,2688]{3,2,1,0:T(8,128)(2,1)S(1)} %get-tuple-element.47, bf16[2,4,64,2688]{3,2,1,0:T(8,128)(2,1)S(1)} %get-tuple-element.46), kind=kLoop, calls=%fused_computation.3 | loop fusion | flops 2752512 | bytes 11010048 | tf_op jit(solution)/shard_map/concatenate | solution.py:322
  110.9 6.0 %collective-permute-start.6 = (bf16[4,4,64,2688]{3,2,1,0:T(8,128)(2,1)}, bf16[4,4,64,2688]{3,2,1,0:T(8,128)(2,1)}, u32[]{:S(2)}, u32[]{:S(2)}) collective-permute-start(bf16[4,4,64,2688]{3,2,1,0:T(8,128)(2,1)} %pad_maximum_fusion.1), channel_id=1, source_target_pairs={{0,2},{2,0},{4,6},{6,4},{1,3},{3,1},{5,7},{7,5},{8,10},{10,8},{12,... | collective-permute-start | bytes 16515080 | tf_op jit(solution)/shard_map/ppermute | solution.py:318
  117.0 8.9 %collective-permute-done.6 = bf16[4,4,64,2688]{3,2,1,0:T(8,128)(2,1)} collective-permute-done((bf16[4,4,64,2688]{3,2,1,0:T(8,128)(2,1)}, bf16[4,4,64,2688]{3,2,1,0:T(8,128)(2,1)}, u32[]{:S(2)}, u32[]{:S(2)}) %collective-permute-start.6) | collective-permute-done | bytes 5505056 | tf_op jit(solution)/shard_map/ppermute | solution.py:318
  125.9 4.4 %broadcast_select_fusion.1 = (bf16[4,4,64,2688]{3,2,1,0:T(8,128)(2,1)S(1)}, bf16[4,4,64,2688]{3,2,1,0:T(8,128)(2,1)S(1)}) fusion(bf16[4,4,64,2688]{3,2,1,0:T(8,128)(2,1)} %collective-permute-done.6, pred[]{:T(512)S(6)} %eq.28, bf16[2,4,64,2688]{3,2,1,0:T(8,128)(2,1)} %copy-done.4, bf16[2,4,64,2688]{3,2,1,0:T(8,128)(2,1)S(1)} %get-tuple-element.46), kind=kLoop, calls=%fused_computation.5 | loop fusion | flops 8257536 | bytes 22020096 | tf_op jit(solution)/shard_map/jit(_where)/select_n | solution.py:322
  130.4 2.4 copy-done.3
  132.7 1.2 pad_maximum_fusion.states_ref
  133.9 5.8 %squares.1 = (bf16[4,2560,512]{2,1,0:T(8,128)(2,1)S(1)}, f32[4,1,512]{2,1,0:T(1,128)S(1)}) custom-call(bf16[8,4,64,2688]{3,2,1,0:T(8,128)(2,1)S(1)} %pad_maximum_fusion.states_ref), custom_call_target="tpu_custom_call" | custom-call | tf_op jit(solution)/shard_map/squares/pallas_call | solution.py:79
  139.8 0.9 fusion.2
  140.7 2.9 %copy-done.2 = bf16[4,2560,512]{2,1,0:T(8,128)(2,1)} copy-done((bf16[4,2560,512]{2,1,0:T(8,128)(2,1)}, bf16[4,2560,512]{2,1,0:T(8,128)(2,1)S(1)}, u32[]{:S(2)}) %copy-start.2) | copy-done | bytes 10485784
  143.9 36.4 %all-to-all-done = bf16[16,800,256]{2,1,0:T(8,128)(2,1)} async-done(((bf16[16,800,256]{2,1,0:T(8,128)(2,1)}), bf16[16,800,256]{2,1,0:T(8,128)(2,1)}, u32[]{:S(2)}, u32[]{:S(2)}) %all-to-all-start) | async-done | bytes 6553632 | tf_op jit(solution)/shard_map/all_to_all | solution.py:275
  180.4 11.7 %score.1 = (f32[4,512,384]{2,1,0:T(8,128)S(1)}, f32[4,8,512]{2,1,0:T(8,128)S(1)}) custom-call(bf16[8,4,64,2688]{3,2,1,0:T(8,128)(2,1)} %copy-done, bf16[4,4,800,256]{3,2,1,0:T(8,128)(2,1)} %bitcast.9.heads_ref, s32[512,1]{1,0:T(8,128)S(1)} %fusion.labels_ref, s32[1,384]{1,0:T(1,128)S(1)} %broadcast_in_dim.18.ids_ref), custom_call_target="tpu_custom_call" | custom-call | tf_op jit(solution)/shard_map/score/pallas_call | solution.py:131
  192.1 1.0 collective-permute-start.7
  193.1 0.9 collective-permute-done.7
  194.0 2.8 %collective-permute-start.8 = (f32[4,4,512]{2,1,0:T(4,128)S(1)}, f32[4,4,512]{2,1,0:T(4,128)S(1)}, u32[]{:S(2)}, u32[]{:S(2)}) collective-permute-start(f32[4,4,512]{2,1,0:T(4,128)S(1)} %pad_maximum_fusion.9), channel_id=1, source_target_pairs={{0,4},{2,6},{4,0},{6,2},{1,5},{3,7},{5,1},{7,3},{8,12},{10,14},{12... | collective-permute-start | bytes 98312 | tf_op jit(solution)/shard_map/ppermute | solution.py:290
  196.8 1.3 collective-permute-done.8
  198.3 2.8 %collective-permute-done.9 = f32[4,4,512]{2,1,0:T(4,128)S(1)} collective-permute-done((f32[4,4,512]{2,1,0:T(4,128)S(1)}, f32[4,4,512]{2,1,0:T(4,128)S(1)}, u32[]{:S(2)}, u32[]{:S(2)}) %collective-permute-start.9) | collective-permute-done | bytes 32800 | tf_op jit(solution)/shard_map/ppermute | solution.py:290
  201.1 1.5 collective-permute-start.10
  202.6 2.2 collective-permute-done.10
  204.9 1.3 collective-permute-start.11
  206.3 1.6 collective-permute-done.11
  208.1 10.6 %merge.1 = (bf16[400,256]{1,0:T(8,128)(2,1)S(1)}, bf16[400,256]{1,0:T(8,128)(2,1)S(1)}, bf16[400,256]{1,0:T(8,128)(2,1)S(1)}, bf16[400,256]{1,0:T(8,128)(2,1)S(1...) custom-call(s32[2]{0:T(128)S(1)} %pad_add_fusion.1.place_ref, ...), custom_call_target="tpu_custom_call" | custom-call | tf_op jit(solution)/shard_map/merge/pallas_call | solution.py:214
  218.7 1.6 collective-permute-start.12
  220.2 1.3 collective-permute-start.13
  221.6 2.9 %collective-permute-start.14 = (bf16[400,256]{1,0:T(8,128)(2,1)S(1)}, bf16[400,256]{1,0:T(8,128)(2,1)S(1)}, u32[]{:S(2)}, u32[]{:S(2)}) collective-permute-start(bf16[400,256]{1,0:T(8,128)(2,1)S(1)} %get-tuple-element.27), channel_id=1, source_target_pairs={{0,20},{2,22},{4,16},{6,18},{8,28},{10,30},{12,24},{14,26},{16,4},... | collective-permute-start | bytes 614408 | tf_op jit(solution)/shard_map/ppermute | solution.py:370
  224.8 1.7 collective-permute-start.17
  226.4 17.7 %collective-permute-done.12.refs_0_ = bf16[400,256]{1,0:T(8,128)(2,1)S(1)} collective-permute-done((bf16[400,256]{1,0:T(8,128)(2,1)S(1)}, bf16[400,256]{1,0:T(8,128)(2,1)S(1)}, u32[]{:S(2)}, u32[]{:S(2)}) %collective-permute-start.12) | collective-permute-done | bytes 204832 | tf_op jit(solution)/shard_map/ppermute | solution.py:370
  244.2 5.0 %collective-permute-done.13.refs_1_ = bf16[400,256]{1,0:T(8,128)(2,1)S(1)} collective-permute-done((bf16[400,256]{1,0:T(8,128)(2,1)S(1)}, bf16[400,256]{1,0:T(8,128)(2,1)S(1)}, u32[]{:S(2)}, u32[]{:S(2)}) %collective-permute-start.13) | collective-permute-done | bytes 204832 | tf_op jit(solution)/shard_map/ppermute | solution.py:370
  249.9 4.2 %collective-permute-done.15.refs_3_ = bf16[400,256]{1,0:T(8,128)(2,1)S(1)} collective-permute-done((bf16[400,256]{1,0:T(8,128)(2,1)S(1)}, bf16[400,256]{1,0:T(8,128)(2,1)S(1)}, u32[]{:S(2)}, u32[]{:S(2)}) %collective-permute-start.15) | collective-permute-done | bytes 204832 | tf_op jit(solution)/shard_map/ppermute | solution.py:370
  254.5 5.7 %collective-permute-start.16 = (bf16[4,208,256]{2,1,0:T(8,128)(2,1)S(1)}, bf16[4,208,256]{2,1,0:T(8,128)(2,1)S(1)}, u32[]{:S(2)}, u32[]{:S(2)}) collective-permute-start(bf16[4,208,256]{2,1,0:T(8,128)(2,1)S(1)} %pad_maximum_fusion.7), channel_id=1, source_target_pairs={{0,2},{2,0},{4,6},{6,4},{1,3},{3,1},{5,7},{7,5},{8,10},{10,8},{12,... | collective-permute-start | bytes 1277960 | tf_op jit(solution)/shard_map/ppermute | solution.py:318
  260.3 1.3 collective-permute-done.16.refs_4_
  262.2 1.6 assemble.1
  (84 shorter events, 3.9 us)
Async XLA Ops:
  1.0 13.0 %collective-permute-start.2 = (bf16[1,64,2560]{2,1,0:T(8,128)(2,1)S(1)}, bf16[1,64,2560]{2,1,0:T(8,128)(2,1)S(1)}, u32[]{:S(2)}, u32[]{:S(2)}) collective-permute-start(bf16[1,64,2560]{2,1,0:T(8,128)(2,1)S(1)} %constant_dynamic-slice_fusion), channel_id=1, source_target_pairs={{0,8},{8,0},{16,24},{24,16},{1,9},{9,1},{17,25},{25,17},{2,10},{10... | collective-permute-start | bytes 983048 | tf_op jit(solution)/shard_map/ppermute | solution.py:318
  1.1 16.6 %collective-permute-start.1 = (bf16[1,64,2560]{2,1,0:T(8,128)(2,1)S(1)}, bf16[1,64,2560]{2,1,0:T(8,128)(2,1)S(1)}, u32[]{:S(2)}, u32[]{:S(2)}) collective-permute-start(bf16[1,64,2560]{2,1,0:T(8,128)(2,1)S(1)} %constant_dynamic-slice_fusion), channel_id=1, source_target_pairs={{0,16},{8,24},{16,0},{24,8},{1,17},{9,25},{17,1},{25,9},{2,18},{10... | collective-permute-start | bytes 983048 | tf_op jit(solution)/shard_map/ppermute | solution.py:318
  3.5 28.1 %collective-permute-start = (bf16[1,64,2560]{2,1,0:T(8,128)(2,1)S(1)}, bf16[1,64,2560]{2,1,0:T(8,128)(2,1)S(1)}, u32[]{:S(2)}, u32[]{:S(2)}) collective-permute-start(bf16[1,64,2560]{2,1,0:T(8,128)(2,1)S(1)} %constant_dynamic-slice_fusion), channel_id=1, source_target_pairs={{0,24},{8,16},{16,8},{24,0},{1,25},{9,17},{17,9},{25,1},{2,26},{10... | collective-permute-start | bytes 983048 | tf_op jit(solution)/shard_map/ppermute | solution.py:318
  5.3 8.7 %copy-start.5 = (bf16[1,128,2560]{2,1,0:T(8,128)(2,1)S(1)}, bf16[1,128,2560]{2,1,0:T(8,128)(2,1)}, u32[]{:S(2)}) copy-start(bf16[1,128,2560]{2,1,0:T(8,128)(2,1)} %param.4) | copy-start | bytes 1966084
  10.2 21.8 %copy-start.1 = (bf16[16,5,160,256]{3,2,1,0:T(8,128)(2,1)}, bf16[16,5,160,256]{3,2,1,0:T(8,128)(2,1)S(1)}, u32[]{:S(2)}) copy-start(bf16[16,5,160,256]{3,2,1,0:T(8,128)(2,1)S(1)} %pack.1) | copy-start | bytes 19660804
  32.1 46.5 %collective-permute-start.3 = (bf16[1,4,64,2688]{3,2,1,0:T(8,128)(2,1)S(1)}, bf16[1,4,64,2688]{3,2,1,0:T(8,128)(2,1)S(1)}, u32[]{:S(2)}, u32[]{:S(2)}) collective-permute-start(bf16[1,4,64,2688]{3,2,1,0:T(8,128)(2,1)S(1)} %pad_maximum_fusion.4), channel_id=1, source_target_pairs={{0,4},{2,6},{4,0},{6,2},{1,5},{3,7},{5,1},{7,3},{8,12},{10,14},{12... | collective-permute-start | bytes 4128776 | tf_op jit(solution)/shard_map/ppermute | solution.py:318
  33.4 147.0 %all-to-all-start = ((bf16[16,800,256]{2,1,0:T(8,128)(2,1)}), bf16[16,800,256]{2,1,0:T(8,128)(2,1)}, u32[]{:S(2)}, u32[]{:S(2)}) async-start(bf16[16,800,256]{2,1,0:T(8,128)(2,1)} %bitcast.286), calls=%async_computation | async-start | bytes 13107200 | tf_op jit(solution)/shard_map/all_to_all | solution.py:275
  39.5 40.4 %collective-permute-start.5 = (bf16[1,4,64,2688]{3,2,1,0:T(8,128)(2,1)S(1)}, bf16[1,4,64,2688]{3,2,1,0:T(8,128)(2,1)}, u32[]{:S(2)}, u32[]{:S(2)}) collective-permute-start(bf16[1,4,64,2688]{3,2,1,0:T(8,128)(2,1)S(1)} %pad_maximum_fusion.4), channel_id=1, source_target_pairs={{0,1},{1,0},{2,3},{3,2},{4,5},{5,4},{6,7},{7,6},{8,9},{9,8},{10,11... | collective-permute-start | bytes 4128776 | tf_op jit(solution)/shard_map/ppermute | solution.py:318
  78.6 26.7 %collective-permute-start.4 = (bf16[1,4,64,2688]{3,2,1,0:T(8,128)(2,1)S(1)}, bf16[1,4,64,2688]{3,2,1,0:T(8,128)(2,1)}, u32[]{:S(2)}, u32[]{:S(2)}) collective-permute-start(bf16[1,4,64,2688]{3,2,1,0:T(8,128)(2,1)S(1)} %collective-permute-done.3), channel_id=1, source_target_pairs={{0,1},{1,0},{2,3},{3,2},{4,5},{5,4},{6,7},{7,6},{8,9},{9,8},{10,11... | collective-permute-start | bytes 4128776 | tf_op jit(solution)/shard_map/ppermute | solution.py:318
  107.6 3.3 %copy-start.4 = (bf16[2,4,64,2688]{3,2,1,0:T(8,128)(2,1)}, bf16[2,4,64,2688]{3,2,1,0:T(8,128)(2,1)S(1)}, u32[]{:S(2)}) copy-start(bf16[2,4,64,2688]{3,2,1,0:T(8,128)(2,1)S(1)} %get-tuple-element.47) | copy-start | bytes 8257540
  110.9 15.0 %collective-permute-start.6 = (bf16[4,4,64,2688]{3,2,1,0:T(8,128)(2,1)}, bf16[4,4,64,2688]{3,2,1,0:T(8,128)(2,1)}, u32[]{:S(2)}, u32[]{:S(2)}) collective-permute-start(bf16[4,4,64,2688]{3,2,1,0:T(8,128)(2,1)} %pad_maximum_fusion.1), channel_id=1, source_target_pairs={{0,2},{2,0},{4,6},{6,4},{1,3},{3,1},{5,7},{7,5},{8,10},{10,8},{12,... | collective-permute-start | bytes 16515080 | tf_op jit(solution)/shard_map/ppermute | solution.py:318
  130.3 2.4 copy-start.3
  133.9 5.8 %copy-start = (bf16[8,4,64,2688]{3,2,1,0:T(8,128)(2,1)}, bf16[8,4,64,2688]{3,2,1,0:T(8,128)(2,1)S(1)}, u32[]{:S(2)}) copy-start(bf16[8,4,64,2688]{3,2,1,0:T(8,128)(2,1)S(1)} %pad_maximum_fusion.states_ref) | copy-start | bytes 33030148
  139.8 3.9 %copy-start.2 = (bf16[4,2560,512]{2,1,0:T(8,128)(2,1)}, bf16[4,2560,512]{2,1,0:T(8,128)(2,1)S(1)}, u32[]{:S(2)}) copy-start(bf16[4,2560,512]{2,1,0:T(8,128)(2,1)S(1)} %get-tuple-element.24.hidden_ref) | copy-start | bytes 31457284
  180.3 27.7 %slice-start = ((s8[10485760]{0:T(1024)(128)(4,1)}), s8[4194304]{0:T(1024)(128)(4,1)S(1)}, s32[]{:S(2)}) async-start(s8[10485760]{0:T(1024)(128)(4,1)} %bitcast.287), calls=%async_computation.1 | async-start | bytes 8388608
  180.3 27.7 %slice-start.1 = ((s8[10485760]{0:T(1024)(128)(4,1)}), s8[4194304]{0:T(1024)(128)(4,1)S(1)}, s32[]{:S(2)}) async-start(s8[10485760]{0:T(1024)(128)(4,1)} %bitcast.287), calls=%async_computation.2 | async-start | bytes 8388608
  180.4 27.7 %slice-start.2 = ((s8[10485760]{0:T(1024)(128)(4,1)}), s8[2097152]{0:T(1024)(128)(4,1)S(1)}, s32[]{:S(2)}) async-start(s8[10485760]{0:T(1024)(128)(4,1)} %bitcast.287), calls=%async_computation.3 | async-start | bytes 4194304
  192.1 1.9 collective-permute-start.7
  194.0 4.1 %collective-permute-start.8 = (f32[4,4,512]{2,1,0:T(4,128)S(1)}, f32[4,4,512]{2,1,0:T(4,128)S(1)}, u32[]{:S(2)}, u32[]{:S(2)}) collective-permute-start(f32[4,4,512]{2,1,0:T(4,128)S(1)} %pad_maximum_fusion.9), channel_id=1, source_target_pairs={{0,4},{2,6},{4,0},{6,2},{1,5},{3,7},{5,1},{7,3},{8,12},{10,14},{12... | collective-permute-start | bytes 98312 | tf_op jit(solution)/shard_map/ppermute | solution.py:290
  198.2 2.8 %collective-permute-start.9 = (f32[4,4,512]{2,1,0:T(4,128)S(1)}, f32[4,4,512]{2,1,0:T(4,128)S(1)}, u32[]{:S(2)}, u32[]{:S(2)}) collective-permute-start(f32[4,4,512]{2,1,0:T(4,128)S(1)} %pad_maximum_fusion.10), channel_id=1, source_target_pairs={{0,8},{8,0},{16,24},{24,16},{1,9},{9,1},{17,25},{25,17},{2,10},{10... | collective-permute-start | bytes 98312 | tf_op jit(solution)/shard_map/ppermute | solution.py:290
  201.1 3.7 %collective-permute-start.10 = (f32[4,4,512]{2,1,0:T(4,128)S(1)}, f32[4,4,512]{2,1,0:T(4,128)S(1)}, u32[]{:S(2)}, u32[]{:S(2)}) collective-permute-start(f32[4,4,512]{2,1,0:T(4,128)S(1)} %pad_maximum_fusion.11), channel_id=1, source_target_pairs={{0,16},{8,24},{16,0},{24,8},{1,17},{9,25},{17,1},{25,9},{2,18},{10... | collective-permute-start | bytes 98312 | tf_op jit(solution)/shard_map/ppermute | solution.py:290
  204.9 2.9 %collective-permute-start.11 = (f32[4,4,512]{2,1,0:T(4,128)S(1)}, f32[4,4,512]{2,1,0:T(4,128)S(1)}, u32[]{:S(2)}, u32[]{:S(2)}) collective-permute-start(f32[4,4,512]{2,1,0:T(4,128)S(1)} %pad_maximum_fusion.12), channel_id=1, source_target_pairs={{0,1},{1,0},{2,3},{3,2},{4,5},{5,4},{6,7},{7,6},{8,9},{9,8},{10,11... | collective-permute-start | bytes 98312 | tf_op jit(solution)/shard_map/ppermute | solution.py:290
  218.7 25.5 %collective-permute-start.12 = (bf16[400,256]{1,0:T(8,128)(2,1)S(1)}, bf16[400,256]{1,0:T(8,128)(2,1)S(1)}, u32[]{:S(2)}, u32[]{:S(2)}) collective-permute-start(bf16[400,256]{1,0:T(8,128)(2,1)S(1)} %get-tuple-element.25), channel_id=1, source_target_pairs={{0,28},{2,30},{4,24},{6,26},{8,20},{10,22},{12,16},{14,18},{16,12}... | collective-permute-start | bytes 614408 | tf_op jit(solution)/shard_map/ppermute | solution.py:370
  220.2 28.9 %collective-permute-start.13 = (bf16[400,256]{1,0:T(8,128)(2,1)S(1)}, bf16[400,256]{1,0:T(8,128)(2,1)S(1)}, u32[]{:S(2)}, u32[]{:S(2)}) collective-permute-start(bf16[400,256]{1,0:T(8,128)(2,1)S(1)} %get-tuple-element.26), channel_id=1, source_target_pairs={{0,24},{2,26},{4,28},{6,30},{8,16},{10,18},{12,20},{14,22},{16,8},... | collective-permute-start | bytes 614408 | tf_op jit(solution)/shard_map/ppermute | solution.py:370
  221.6 28.3 %collective-permute-start.14 = (bf16[400,256]{1,0:T(8,128)(2,1)S(1)}, bf16[400,256]{1,0:T(8,128)(2,1)S(1)}, u32[]{:S(2)}, u32[]{:S(2)}) collective-permute-start(bf16[400,256]{1,0:T(8,128)(2,1)S(1)} %get-tuple-element.27), channel_id=1, source_target_pairs={{0,20},{2,22},{4,16},{6,18},{8,28},{10,30},{12,24},{14,26},{16,4},... | collective-permute-start | bytes 614408 | tf_op jit(solution)/shard_map/ppermute | solution.py:370
  224.4 29.7 %collective-permute-start.15 = (bf16[400,256]{1,0:T(8,128)(2,1)S(1)}, bf16[400,256]{1,0:T(8,128)(2,1)S(1)}, u32[]{:S(2)}, u32[]{:S(2)}) collective-permute-start(bf16[400,256]{1,0:T(8,128)(2,1)S(1)} %get-tuple-element.28), channel_id=1, source_target_pairs={{0,16},{2,18},{4,20},{6,22},{8,24},{10,26},{12,28},{14,30},{16,0},... | collective-permute-start | bytes 614408 | tf_op jit(solution)/shard_map/ppermute | solution.py:370
  224.8 29.4 %collective-permute-start.17 = (bf16[400,256]{1,0:T(8,128)(2,1)S(1)}, bf16[400,256]{1,0:T(8,128)(2,1)S(1)}, u32[]{:S(2)}, u32[]{:S(2)}) collective-permute-start(bf16[400,256]{1,0:T(8,128)(2,1)S(1)} %get-tuple-element.29), channel_id=1, source_target_pairs={{0,12},{2,14},{4,8},{6,10},{8,4},{10,6},{12,0},{14,2},{16,28},{18,... | collective-permute-start | bytes 614408 | tf_op jit(solution)/shard_map/ppermute | solution.py:370
  244.2 10.0 %collective-permute-start.18 = (bf16[400,256]{1,0:T(8,128)(2,1)S(1)}, bf16[400,256]{1,0:T(8,128)(2,1)S(1)}, u32[]{:S(2)}, u32[]{:S(2)}) collective-permute-start(bf16[400,256]{1,0:T(8,128)(2,1)S(1)} %get-tuple-element.30), channel_id=1, source_target_pairs={{0,8},{2,10},{4,12},{6,14},{8,0},{10,2},{12,4},{14,6},{16,24},{18,... | collective-permute-start | bytes 614408 | tf_op jit(solution)/shard_map/ppermute | solution.py:370
  249.2 5.0 %collective-permute-start.19 = (bf16[400,256]{1,0:T(8,128)(2,1)S(1)}, bf16[400,256]{1,0:T(8,128)(2,1)S(1)}, u32[]{:S(2)}, u32[]{:S(2)}) collective-permute-start(bf16[400,256]{1,0:T(8,128)(2,1)S(1)} %get-tuple-element.31), channel_id=1, source_target_pairs={{0,4},{2,6},{4,0},{6,2},{8,12},{10,14},{12,8},{14,10},{16,20},{18,... | collective-permute-start | bytes 614408 | tf_op jit(solution)/shard_map/ppermute | solution.py:370
  254.5 7.1 %collective-permute-start.16 = (bf16[4,208,256]{2,1,0:T(8,128)(2,1)S(1)}, bf16[4,208,256]{2,1,0:T(8,128)(2,1)S(1)}, u32[]{:S(2)}, u32[]{:S(2)}) collective-permute-start(bf16[4,208,256]{2,1,0:T(8,128)(2,1)S(1)} %pad_maximum_fusion.7), channel_id=1, source_target_pairs={{0,2},{2,0},{4,6},{6,4},{1,3},{3,1},{5,7},{7,5},{8,10},{10,8},{12,... | collective-permute-start | bytes 1277960 | tf_op jit(solution)/shard_map/ppermute | solution.py:318
  260.2 1.9 collective-permute-start.20
